TPU v7x, 32 devices: a whole 2x2x4 slice. The times are simulated.
32 devices in a mesh: gx: 4 (over x, core), gy: 4 (over z), gz: 2 (over y).
Axes of the slice: x: 2, y: 2, z: 4, core: 2. Of those that a mesh axis runs over, the one named last changes fastest.
Arguments:
- body_pos: float32 [3, 16384], P(None, ('gx', 'gy', 'gz')), may hold values from -1 to 1
- body_mass: float32 [16384], P(('gx', 'gy', 'gz')), may hold values from 0.003 to 0.03
- cell_mass: float32 [65536], P(('gx', 'gy', 'gz')), may hold values from 0.003 to 0.03
- cell_center: float32 [3, 65536], P(None, ('gx', 'gy', 'gz')), may hold values from -1 to 1
- cell_quad: float32 [6, 65536], P(None, ('gx', 'gy', 'gz')), may hold values from -0.001 to 0.001
- cell_lists: int32 [32, 5, 1024], P(('gx', 'gy', 'gz')), may hold values from 0 to 6143, as said below
- slot_masks: int32 [32, 5, 1024], P(('gx', 'gy', 'gz')), may hold values from 0 to 1, as said below
- face_lists: int32 [32, 2, 4], P(('gx', 'gy', 'gz')), may hold values from 0 to 3, as said below
- face_counts: int32 [32, 2], P(('gx', 'gy', 'gz')), may hold values from 1 to 4
Outputs:
- accel: float32 [3, 16384], P(None, ('gx', 'gy', 'gz'))
Inputs may be any that keep to these rules, and one draw needn't show every extreme that they name: `cell_lists`: at level l (from 0) every entry is below 2048 + l * 1024, and the 1024 entries of one level of one domain are distinct. `slot_masks`: each level of each domain has exactly 768 ones. `face_lists`: each side's list of a domain is a permutation of its 4 blocks.
All inputs are finite; a program needn't handle non-finite values.
Results may differ from a plain program's by a relative error of at most 0.00002.
Values sent between devices are 32-bit elements; how exact they have to be, the bound alone decides.
No kernel may reach another device: no remote copies, remote signals or barrier semaphores. Data moves between devices by JAX's collectives and lax.ppermute only.
A program may use at most 64 MiB of HBM per device.

v0:
```python
import math

import jax
import jax.numpy as jnp
from jax import lax
from jax.sharding import PartitionSpec as P

NBLK = 4
BLK = 128
LEVELS = 5


soften = 0.01


def padded(cells, sides, width):
    for axis, dim in sides:
        count = lax.axis_size(axis)
        ends = count - 1
        head = lax.slice_in_dim(cells, 0, width, axis=dim)
        tail = lax.slice_in_dim(cells, cells.shape[dim] - width, cells.shape[dim], axis=dim)
        cells = jnp.concatenate(
            [
                lax.ppermute(tail, axis, [(i, (i + 1) % count) for i in range(ends)]),
                cells,
                lax.ppermute(head, axis, [((i + 1) % count, i) for i in range(ends)]),
            ],
            axis=dim,
        )
    return cells


def swapped(value, axis, apart):
    mask = 2**apart
    pairs = [(source, source ^ mask) for source in range(lax.axis_size(axis))]
    return lax.ppermute(value, axis, pairs)


def tile_accel(targets, sources):
    offset = targets[:, :, None] - sources[1:4, None, :]
    distance = jnp.sum(offset * offset, axis=0) + soften
    inverse_one = lax.rsqrt(distance)
    inverse_two = inverse_one * inverse_one
    inverse_three = inverse_one * inverse_two
    radial = -sources[0][None, :] * inverse_three
    if sources.shape[0] == 10:
        quadrupole = sources[4:10]
        quad_x = (
            quadrupole[0][None, :] * offset[0]
            + quadrupole[3][None, :] * offset[1]
            + quadrupole[4][None, :] * offset[2]
        )
        quad_y = (
            quadrupole[3][None, :] * offset[0]
            + quadrupole[1][None, :] * offset[1]
            + quadrupole[5][None, :] * offset[2]
        )
        quad_z = (
            quadrupole[4][None, :] * offset[0]
            + quadrupole[5][None, :] * offset[1]
            + quadrupole[2][None, :] * offset[2]
        )
        inverse_five = inverse_three * inverse_two
        quad_form = offset[0] * quad_x + offset[1] * quad_y + offset[2] * quad_z
        radial = radial - 2.5 * quad_form * inverse_five * inverse_two
        return jnp.stack(
            [
                jnp.sum(radial * offset[0] + quad_x * inverse_five, axis=1),
                jnp.sum(radial * offset[1] + quad_y * inverse_five, axis=1),
                jnp.sum(radial * offset[2] + quad_z * inverse_five, axis=1),
            ]
        )
    return jnp.sum(radial[None] * offset, axis=2)


def tile_width_for(count):
    for width in (1024, 1152, 768, 512, 384, 256, 128):
        if count % width == 0:
            return width
    return math.gcd(count, 1024)


def cell_forces(targets, sources):
    source_count = sources.shape[1]
    source_width = tile_width_for(source_count)
    source_tiles = sources.reshape(
        sources.shape[0], source_count // source_width, source_width
    ).transpose(1, 0, 2)
    target_count = targets.shape[1]
    target_width = math.gcd(target_count, 512)
    target_tiles = targets.reshape(3, target_count // target_width, target_width).transpose(1, 0, 2)

    def one_target_tile(target_tile):

        def add_tile(summed, source_tile):
            return (summed + tile_accel(target_tile, source_tile), None)

        summed, unused = lax.scan(add_tile, jnp.zeros_like(target_tile), source_tiles)
        return summed

    results = lax.map(one_target_tile, target_tiles)
    return results.transpose(1, 0, 2).reshape(3, target_count)


def shards(
    body_pos,
    body_mass,
    cell_mass,
    cell_center,
    cell_quad,
    cell_lists,
    slot_masks,
    face_lists,
    face_counts,
):
    bit_count = lax.axis_size(("gx", "gy", "gz")).bit_length() - 1
    stacked = jnp.concatenate([body_mass[None], body_pos], 0)
    blocks_all = stacked.reshape(4, NBLK, BLK)
    chosen_blocks = jnp.take(blocks_all, face_lists[0].reshape(-1), axis=1)
    slot_numbers = jnp.arange(NBLK, dtype=jnp.int32)
    face_live = (slot_numbers[None, :] < face_counts[0][:, None]).reshape(-1)
    outgoing = chosen_blocks * face_live.astype(jnp.float32)[None, :, None]
    extended = padded(outgoing, (("gz", 1),), NBLK)
    near_bodies = jnp.concatenate(
        [stacked, extended[:, :NBLK].reshape(4, -1), extended[:, 3 * NBLK :].reshape(4, -1)], 1
    )
    held_cells = jnp.concatenate([cell_mass[None], cell_center, cell_quad], 0)
    forces = cell_forces(body_pos, near_bodies)
    forces = forces + cell_forces(body_pos, held_cells)
    for level_no in range(LEVELS):
        partner_bit = bit_count - 1 - level_no
        slot_index = cell_lists[0, level_no]
        slot_live = slot_masks[0, level_no]
        outbound = jnp.take(held_cells, slot_index, axis=1) * slot_live.astype(jnp.float32)[None]
        arrived = swapped(outbound, ("gx", "gy", "gz"), partner_bit)
        forces = forces + cell_forces(body_pos, arrived)
        held_cells = jnp.concatenate([held_cells, arrived], 1)
    return forces


def solution(mesh):
    in_specs = (
        P(None, ("gx", "gy", "gz")),
        P(("gx", "gy", "gz")),
        P(("gx", "gy", "gz")),
        P(None, ("gx", "gy", "gz")),
        P(None, ("gx", "gy", "gz")),
        P(("gx", "gy", "gz"), None, None),
        P(("gx", "gy", "gz"), None, None),
        P(("gx", "gy", "gz"), None, None),
        P(("gx", "gy", "gz"), None),
    )
    out_specs = P(None, ("gx", "gy", "gz"))
    return jax.shard_map(shards, mesh=mesh, in_specs=in_specs, out_specs=out_specs, check_vma=False)
```

profile of v0, /device:TPU:0, one launch (start us, length us, event | category | flops | bytes accessed | tf_op | source)
XLA Modules:
  0.0 155.1 jit_solution(14662439208825072677)
XLA Ops:
  4.5 4.9 %collective-permute-start = (f32[4,4,128]{2,0,1:T(4,128)S(1)}, f32[4,4,128]{2,0,1:T(4,128)S(1)}, u32[]{:S(2)}, u32[]{:S(2)}) collective-permute-start(f32[4,4,128]{2,0,1:T(4,128)S(1)} %get-tuple-element.348), channel_id=1, source_target_pairs={{0,1},{2,3},{4,5},{6,7},{8,9},{10,11},{12,13},{14,15},{16,17},{18,... | collective-permute-start | bytes 24584 | tf_op jit(solution)/shard_map/ppermute | solution.py:24
  9.4 1.3 collective-permute-start.1
  13.6 2.8 %gather_fusion.1 = f32[1024,10]{1,0:T(8,128)S(1)} fusion(f32[10,2048]{0,1:T(8,128)S(1)} %copy.45, s32[1024]{0:T(1024)S(1)} %get-tuple-element.351), kind=kCustom, calls=%fused_computation.1 | custom fusion | bytes 86016 | tf_op jit(solution)/shard_map/jit(_take)/gather | solution.py:134
  16.7 1.6 %collective-permute-start.2 = (f32[10,1024]{0,1:T(8,128)S(1)}, f32[10,1024]{0,1:T(8,128)S(1)}, u32[]{:S(2)}, u32[]{:S(2)}) collective-permute-start(f32[10,1024]{0,1:T(8,128)S(1)} %multiply_bitcast_fusion.4), channel_id=1, source_target_pairs={{0,16},{1,17},{2,18},{3,19},{4,20},{5,21},{6,22},{7,23},{8,24},{9,... | collective-permute-start | bytes 122888 | tf_op jit(solution)/shard_map/ppermute | solution.py:36
  19.5 8.7 %while.47 = (s32[]{:T(128)}, f32[3,512]{1,0:T(4,128)S(1)}, f32[2,10,1024]{2,1,0:T(8,128)S(1)}, f32[3,512]{1,0:T(4,128)S(1)}, s32[]{:T(128)}, /*index=5*/s32[]{:T...) while((s32[]{:T(128)}, f32[3,512]{1,0:T(4,128)S(1)}, f32[2,10,1024]{2,1,0:T(8,128)S(1)}, ...), condition=%wide.region_9.10_spmd.clone, body=%wide.region_4.9_spmd.clone.sunk | while | flops 25695752 | bytes 16931076 | solution.py:98
  20.3 3.5 %add_reduce_fusion.19 = (f32[512]{0:T(512)S(1)}, f32[512]{0:T(512)S(1)}, f32[512]{0:T(512)S(1)}) fusion(f32[3,512,1024]{2,1,0:T(8,128)S(1)} %get-tuple-element.414, f32[1024]{0:T(1024)S(1)} %bitcast.346, f32[1024]{0:T(1024)S(1)} %bitcast.347, f32[1024]{0:T(1024)S(1)} %bitcast.348, f32[512,1024]{1,0:T(8,128)S(1)} %get-tuple-element.418, ...), kind=kLoop, calls=%fused_computation.18.clone.1 | loop fusion | flops 21494272 | bytes 8423424 | tf_op jit(solution)/shard_map/while/body/eval_jaxpr/while/body/eval_jaxpr/reduce_sum | solution.py:68
  24.7 3.5 %add_reduce_fusion.19 = (f32[512]{0:T(512)S(1)}, f32[512]{0:T(512)S(1)}, f32[512]{0:T(512)S(1)}) fusion(f32[3,512,1024]{2,1,0:T(8,128)S(1)} %get-tuple-element.414, f32[1024]{0:T(1024)S(1)} %bitcast.346, f32[1024]{0:T(1024)S(1)} %bitcast.347, f32[1024]{0:T(1024)S(1)} %bitcast.348, f32[512,1024]{1,0:T(8,128)S(1)} %get-tuple-element.418, ...), kind=kLoop, calls=%fused_computation.18.clone.1 | loop fusion | flops 21494272 | bytes 8423424 | tf_op jit(solution)/shard_map/while/body/eval_jaxpr/while/body/eval_jaxpr/reduce_sum | solution.py:68
  28.3 3.1 %while.46 = (s32[]{:T(128)}, f32[3,512]{1,0:T(4,128)S(1)}, f32[2,4,768]{2,1,0:T(4,128)S(1)}, f32[3,512]{1,0:T(4,128)S(1)}, s32[]{:T(128)}, /*index=5*/s32[]{:T(128)}, s32[]{}) while((s32[]{:T(128)}, f32[3,512]{1,0:T(4,128)S(1)}, f32[2,4,768]{2,1,0:T(4,128)S(1)}, f32[3,512]{1,0:T(4,128)S(1)}, s32[]{:T(128)}, /*index=5*/s32[]{:T(128)}, ...), condition=%wide.region_3.4_spmd.clone, body=%wide.region_0.3_spmd.clone.sunk | while | flops 8259844 | bytes 6374519 | solution.py:98
  31.6 4.0 %gather_fusion.2 = f32[1024,10]{1,0:T(8,128)} fusion(f32[10,3072]{0,1:T(8,128)S(1)} %pad_maximum_fusion.2, s32[1024]{0:T(1024)S(1)} %broadcast_clamp_fusion.3), kind=kCustom, calls=%fused_computation.2 | custom fusion | bytes 86016 | tf_op jit(solution)/shard_map/jit(_take)/gather | solution.py:134
  35.6 1.4 multiply_bitcast_fusion.3
  37.0 1.9 %fusion.20 = (f32[1024]{0:T(1024)S(1)}, f32[1024]{0:T(1024)S(1)}, f32[1024]{0:T(1024)S(1)}, f32[1024]{0:T(1024)S(1)}, f32[1024]{0:T(1024)S(1)}, /*index=5*/f32[1024]{0:T(1024)S(1)}, f32[1024]{0:T(1024)S(1)}) fusion(f32[10,1024]{0,1:T(8,128)S(1)} %collective-permute-done.2), kind=kLoop, calls=%fused_computation.175 | loop fusion | flops 1024 | bytes 57344 | tf_op jit(solution)/shard_map/while/body/eval_jaxpr/while/body/eval_jaxpr/neg | solution.py:45
  40.1 1.5 pad_maximum_fusion.1
  41.6 4.4 %gather_fusion.3 = f32[1024,10]{1,0:T(8,128)S(1)} fusion(f32[10,4096]{0,1:T(8,128)} %pad_maximum_fusion.1, s32[1024]{0:T(1024)S(1)} %broadcast_clamp_fusion.2), kind=kCustom, calls=%fused_computation.3 | custom fusion | bytes 86016 | tf_op jit(solution)/shard_map/jit(_take)/gather | solution.py:134
  46.1 1.1 multiply_bitcast_fusion.2
  47.2 2.6 %collective-permute-start.4 = (f32[10,1024]{0,1:T(8,128)}, f32[10,1024]{0,1:T(8,128)S(1)}, u32[]{:S(2)}, u32[]{:S(2)}) collective-permute-start(f32[10,1024]{0,1:T(8,128)} %multiply_bitcast_fusion.2), channel_id=1, source_target_pairs={{0,4},{1,5},{2,6},{3,7},{4,0},{5,1},{6,2},{7,3},{8,12},{9,13},{10,... | collective-permute-start | bytes 122888 | tf_op jit(solution)/shard_map/ppermute | solution.py:36
  49.8 1.8 %fusion.19 = (f32[1024]{0:T(1024)S(1)}, f32[1024]{0:T(1024)S(1)}, f32[1024]{0:T(1024)S(1)}, f32[1024]{0:T(1024)S(1)}, f32[1024]{0:T(1024)S(1)}, /*index=5*/f32[1024]{0:T(1024)S(1)}, f32[1024]{0:T(1024)S(1)}) fusion(f32[10,1024]{0,1:T(8,128)S(1)} %collective-permute-done.3), kind=kLoop, calls=%fused_computation.167 | loop fusion | flops 1024 | bytes 57344 | tf_op jit(solution)/shard_map/while/body/eval_jaxpr/while/body/eval_jaxpr/neg | solution.py:45
  52.9 21.0 %collective-permute-done.4 = f32[10,1024]{0,1:T(8,128)S(1)} collective-permute-done((f32[10,1024]{0,1:T(8,128)}, f32[10,1024]{0,1:T(8,128)S(1)}, u32[]{:S(2)}, u32[]{:S(2)}) %collective-permute-start.4) | collective-permute-done | bytes 40992 | tf_op jit(solution)/shard_map/ppermute | solution.py:36
  73.8 1.7 %pad_maximum_fusion = f32[10,5120]{0,1:T(8,128)} fusion(f32[10,1024]{0,1:T(8,128)S(1)} %collective-permute-done.4, f32[10,1024]{0,1:T(8,128)S(1)} %collective-permute-done.3, f32[10,1024]{0,1:T(8,128)S(1)} %collective-permute-done.2, f32[10,2048]{0,1:T(8,128)S(1)} %copy.45), kind=kLoop, calls=%fused_computation.73 | loop fusion | flops 153600 | bytes 409600 | tf_op jit(solution)/shard_map/concatenate | solution.py:137
  75.6 4.7 %gather_fusion.4 = f32[1024,10]{1,0:T(8,128)S(1)} fusion(f32[10,5120]{0,1:T(8,128)} %pad_maximum_fusion, s32[1024]{0:T(1024)S(1)} %broadcast_clamp_fusion.1), kind=kCustom, calls=%fused_computation.4 | custom fusion | bytes 86016 | tf_op jit(solution)/shard_map/jit(_take)/gather | solution.py:134
  81.5 1.8 %fusion.18 = (f32[1024]{0:T(1024)S(1)}, f32[1024]{0:T(1024)S(1)}, f32[1024]{0:T(1024)S(1)}, f32[1024]{0:T(1024)S(1)}, f32[1024]{0:T(1024)S(1)}, /*index=5*/f32[1024]{0:T(1024)S(1)}, f32[1024]{0:T(1024)S(1)}) fusion(f32[10,1024]{0,1:T(8,128)S(1)} %collective-permute-done.4), kind=kLoop, calls=%fused_computation.159 | loop fusion | flops 1024 | bytes 57344 | tf_op jit(solution)/shard_map/while/body/eval_jaxpr/while/body/eval_jaxpr/neg | solution.py:45
  84.5 9.7 %collective-permute-done.5 = f32[10,1024]{0,1:T(8,128)S(1)} collective-permute-done((f32[10,1024]{0,1:T(8,128)S(1)}, f32[10,1024]{0,1:T(8,128)S(1)}, u32[]{:S(2)}, u32[]{:S(2)}) %collective-permute-start.5) | collective-permute-done | bytes 40992 | tf_op jit(solution)/shard_map/ppermute | solution.py:36
  95.1 4.7 %gather_fusion.5 = f32[1024,10]{1,0:T(8,128)S(1)} fusion(f32[10,6144]{0,1:T(8,128)} %constant_dynamic-update-slice_fusion, s32[1024]{0:T(1024)S(1)} %broadcast_clamp_fusion), kind=kCustom, calls=%fused_computation.5 | custom fusion | bytes 86016 | tf_op jit(solution)/shard_map/jit(_take)/gather | solution.py:134
  100.1 2.7 %collective-permute-start.6 = (f32[10,1024]{0,1:T(8,128)S(1)}, f32[10,1024]{0,1:T(8,128)S(1)}, u32[]{:S(2)}, u32[]{:S(2)}) collective-permute-start(f32[10,1024]{0,1:T(8,128)S(1)} %multiply_bitcast_fusion), channel_id=1, source_target_pairs={{0,1},{1,0},{2,3},{3,2},{4,5},{5,4},{6,7},{7,6},{8,9},{9,8},{10,11... | collective-permute-start | bytes 122888 | tf_op jit(solution)/shard_map/ppermute | solution.py:36
  102.8 1.8 %fusion.17 = (f32[1024]{0:T(1024)S(1)}, f32[1024]{0:T(1024)S(1)}, f32[1024]{0:T(1024)S(1)}, f32[1024]{0:T(1024)S(1)}, f32[1024]{0:T(1024)S(1)}, /*index=5*/f32[1024]{0:T(1024)S(1)}, f32[1024]{0:T(1024)S(1)}) fusion(f32[10,1024]{0,1:T(8,128)S(1)} %collective-permute-done.5), kind=kLoop, calls=%fused_computation.151 | loop fusion | flops 1024 | bytes 57344 | tf_op jit(solution)/shard_map/while/body/eval_jaxpr/while/body/eval_jaxpr/neg | solution.py:45
  105.1 8.7 %collective-permute-done.6 = f32[10,1024]{0,1:T(8,128)S(1)} collective-permute-done((f32[10,1024]{0,1:T(8,128)S(1)}, f32[10,1024]{0,1:T(8,128)S(1)}, u32[]{:S(2)}, u32[]{:S(2)}) %collective-permute-start.6) | collective-permute-done | bytes 40992 | tf_op jit(solution)/shard_map/ppermute | solution.py:36
  114.1 16.0 %multiply_reduce_fusion.1 = (f32[512,1024]{1,0:T(8,128)S(1)}, f32[512,1024]{1,0:T(8,128)S(1)}, f32[512,1024]{1,0:T(8,128)S(1)}, f32[512,1024]{1,0:T(8,128)}, f32...) fusion(f32[3,1024]{1,0:T(4,128)S(1)} %copy.54, ...), kind=kLoop, calls=%fused_computation.43 | loop fusion | flops 20971520 | bytes 42010624 | tf_op jit(solution)/shard_map/while/body/eval_jaxpr/while/body/eval_jaxpr/reduce_sum | solution.py:41
  130.1 5.8 %add_reduce_fusion.17 = (f32[512]{0:T(512)S(1)}, f32[512]{0:T(512)S(1)}, f32[512]{0:T(512)S(1)}) fusion(f32[3,512,1024]{2,1,0:T(8,128)} %get-tuple-element.332, f32[1024]{0:T(1024)S(1)} %get-tuple-element.295, f32[1024]{0:T(1024)S(1)} %get-tuple-element.296, f32[1024]{0:T(1024)S(1)} %get-tuple-element.297, f32[512,1024]{1,0:T(8,128)} %get-tuple-element.302, ...), kind=kLoop, calls=%fused_computation.129 | loop fusion | flops 21494272 | bytes 8423424 | tf_op jit(solution)/shard_map/while/body/eval_jaxpr/while/body/eval_jaxpr/reduce_sum | solution.py:68
  136.0 5.0 %add_reduce_fusion.14 = (f32[512]{0:T(512)S(1)}, f32[512]{0:T(512)S(1)}, f32[512]{0:T(512)S(1)}) fusion(f32[3,512,1024]{2,1,0:T(8,128)S(1)} %copy-done, f32[1024]{0:T(1024)S(1)} %get-tuple-element.288, f32[1024]{0:T(1024)S(1)} %get-tuple-element.289, f32[1024]{0:T(1024)S(1)} %get-tuple-element.290, f32[512,1024]{1,0:T(8,128)} %get-tuple-element.301, ...), kind=kLoop, calls=%fused_computation.121 | loop fusion | flops 21494272 | bytes 8423424 | tf_op jit(solution)/shard_map/while/body/eval_jaxpr/while/body/eval_jaxpr/reduce_sum | solution.py:68
  141.0 4.0 %add_reduce_fusion.11 = (f32[512]{0:T(512)S(1)}, f32[512]{0:T(512)S(1)}, f32[512]{0:T(512)S(1)}) fusion(f32[3,512,1024]{2,1,0:T(8,128)S(1)} %bitcast.340, f32[1024]{0:T(1024)S(1)} %get-tuple-element.281, f32[1024]{0:T(1024)S(1)} %get-tuple-element.282, f32[1024]{0:T(1024)S(1)} %get-tuple-element.283, f32[512,1024]{1,0:T(8,128)S(1)} %get-tuple-element.300, ...), kind=kLoop, calls=%fused_computation.113 | loop fusion | flops 21494272 | bytes 8423424 | tf_op jit(solution)/shard_map/while/body/eval_jaxpr/while/body/eval_jaxpr/reduce_sum | solution.py:68
  145.0 1.8 %fusion.16 = (f32[1024]{0:T(1024)S(1)}, f32[1024]{0:T(1024)S(1)}, f32[1024]{0:T(1024)S(1)}, f32[1024]{0:T(1024)S(1)}, f32[1024]{0:T(1024)S(1)}, /*index=5*/f32[1024]{0:T(1024)S(1)}, f32[1024]{0:T(1024)S(1)}) fusion(f32[10,1024]{0,1:T(8,128)S(1)} %collective-permute-done.6), kind=kLoop, calls=%fused_computation.143 | loop fusion | flops 1024 | bytes 57344 | tf_op jit(solution)/shard_map/while/body/eval_jaxpr/while/body/eval_jaxpr/neg | solution.py:45
  146.9 3.8 %add_reduce_fusion.5 = (f32[512]{0:T(512)S(1)}, f32[512]{0:T(512)S(1)}, f32[512]{0:T(512)S(1)}) fusion(f32[3,512,1024]{2,1,0:T(8,128)S(1)} %bitcast.338, f32[1024]{0:T(1024)S(1)} %get-tuple-element.267, f32[1024]{0:T(1024)S(1)} %get-tuple-element.268, f32[1024]{0:T(1024)S(1)} %get-tuple-element.269, f32[512,1024]{1,0:T(8,128)S(1)} %get-tuple-element.298, ...), kind=kLoop, calls=%fused_computation.97 | loop fusion | flops 21494272 | bytes 8423424 | tf_op jit(solution)/shard_map/while/body/eval_jaxpr/while/body/eval_jaxpr/reduce_sum | solution.py:68
  150.7 3.8 %add_reduce_fusion.8 = (f32[512]{0:T(512)S(1)}, f32[512]{0:T(512)S(1)}, f32[512]{0:T(512)S(1)}) fusion(f32[3,512,1024]{2,1,0:T(8,128)S(1)} %bitcast.336, f32[1024]{0:T(1024)S(1)} %get-tuple-element.274, f32[1024]{0:T(1024)S(1)} %get-tuple-element.275, f32[1024]{0:T(1024)S(1)} %get-tuple-element.276, f32[512,1024]{1,0:T(8,128)S(1)} %get-tuple-element.299, ...), kind=kLoop, calls=%fused_computation.105 | loop fusion | flops 21494272 | bytes 8423424 | tf_op jit(solution)/shard_map/while/body/eval_jaxpr/while/body/eval_jaxpr/reduce_sum | solution.py:68
  (102 shorter events, 21.2 us)
Async XLA Ops:
  4.5 23.7 %collective-permute-start = (f32[4,4,128]{2,0,1:T(4,128)S(1)}, f32[4,4,128]{2,0,1:T(4,128)S(1)}, u32[]{:S(2)}, u32[]{:S(2)}) collective-permute-start(f32[4,4,128]{2,0,1:T(4,128)S(1)} %get-tuple-element.348), channel_id=1, source_target_pairs={{0,1},{2,3},{4,5},{6,7},{8,9},{10,11},{12,13},{14,15},{16,17},{18,... | collective-permute-start | bytes 24584 | tf_op jit(solution)/shard_map/ppermute | solution.py:24
  9.4 18.9 %collective-permute-start.1 = (f32[4,4,128]{2,0,1:T(4,128)S(1)}, f32[4,4,128]{2,0,1:T(4,128)S(1)}, u32[]{:S(2)}, u32[]{:S(2)}) collective-permute-start(f32[4,4,128]{2,0,1:T(4,128)S(1)} %get-tuple-element.349), channel_id=1, source_target_pairs={{1,0},{3,2},{5,4},{7,6},{9,8},{11,10},{13,12},{15,14},{17,16},{19,... | collective-permute-start | bytes 24584 | tf_op jit(solution)/shard_map/ppermute | solution.py:26
  13.5 5.9 %copy-start.2 = (f32[6,2048]{1,0:T(8,128)S(1)}, f32[6,2048]{1,0:T(8,128)}, u32[]{:S(2)}) copy-start(f32[6,2048]{1,0:T(8,128)} %param.17) | copy-start | bytes 147460
  13.5 5.9 %copy-start.3 = (f32[3,2048]{1,0:T(4,128)S(1)}, f32[3,2048]{1,0:T(4,128)}, u32[]{:S(2)}) copy-start(f32[3,2048]{1,0:T(4,128)} %param.16) | copy-start | bytes 73732
  13.5 5.9 %copy-start.4 = (f32[2048]{0:T(1024)S(1)}, f32[2048]{0:T(1024)}, u32[]{:S(2)}) copy-start(f32[2048]{0:T(1024)} %param.15) | copy-start | bytes 24580
  13.5 5.9 %copy-start.1 = (f32[3,512]{1,0:T(4,128)S(1)}, f32[3,512]{1,0:T(4,128)}, u32[]{:S(2)}) copy-start(f32[3,512]{1,0:T(4,128)} %param.13) | copy-start | bytes 18436
  16.7 14.7 %collective-permute-start.2 = (f32[10,1024]{0,1:T(8,128)S(1)}, f32[10,1024]{0,1:T(8,128)S(1)}, u32[]{:S(2)}, u32[]{:S(2)}) collective-permute-start(f32[10,1024]{0,1:T(8,128)S(1)} %multiply_bitcast_fusion.4), channel_id=1, source_target_pairs={{0,16},{1,17},{2,18},{3,19},{4,20},{5,21},{6,22},{7,23},{8,24},{9,... | collective-permute-start | bytes 122888 | tf_op jit(solution)/shard_map/ppermute | solution.py:36
  19.5 8.8 %copy-start.5 = (f32[512]{0:T(512)S(1)}, f32[512]{0:T(512)}, u32[]{:S(2)}) copy-start(f32[512]{0:T(512)} %param.14) | copy-start | bytes 6148
  36.9 3.2 %collective-permute-start.3 = (f32[10,1024]{0,1:T(8,128)S(1)}, f32[10,1024]{0,1:T(8,128)S(1)}, u32[]{:S(2)}, u32[]{:S(2)}) collective-permute-start(f32[10,1024]{0,1:T(8,128)S(1)} %multiply_bitcast_fusion.3), channel_id=1, source_target_pairs={{0,8},{1,9},{2,10},{3,11},{4,12},{5,13},{6,14},{7,15},{8,0},{9,1},... | collective-permute-start | bytes 122888 | tf_op jit(solution)/shard_map/ppermute | solution.py:36
  47.2 26.7 %collective-permute-start.4 = (f32[10,1024]{0,1:T(8,128)}, f32[10,1024]{0,1:T(8,128)S(1)}, u32[]{:S(2)}, u32[]{:S(2)}) collective-permute-start(f32[10,1024]{0,1:T(8,128)} %multiply_bitcast_fusion.2), channel_id=1, source_target_pairs={{0,4},{1,5},{2,6},{3,7},{4,0},{5,1},{6,2},{7,3},{8,12},{9,13},{10,... | collective-permute-start | bytes 122888 | tf_op jit(solution)/shard_map/ppermute | solution.py:36
  80.6 13.6 %collective-permute-start.5 = (f32[10,1024]{0,1:T(8,128)S(1)}, f32[10,1024]{0,1:T(8,128)S(1)}, u32[]{:S(2)}, u32[]{:S(2)}) collective-permute-start(f32[10,1024]{0,1:T(8,128)S(1)} %multiply_bitcast_fusion.1), channel_id=1, source_target_pairs={{0,2},{1,3},{2,0},{3,1},{4,6},{5,7},{6,4},{7,5},{8,10},{9,11},{10,... | collective-permute-start | bytes 122888 | tf_op jit(solution)/shard_map/ppermute | solution.py:36
  100.1 13.6 %collective-permute-start.6 = (f32[10,1024]{0,1:T(8,128)S(1)}, f32[10,1024]{0,1:T(8,128)S(1)}, u32[]{:S(2)}, u32[]{:S(2)}) collective-permute-start(f32[10,1024]{0,1:T(8,128)S(1)} %multiply_bitcast_fusion), channel_id=1, source_target_pairs={{0,1},{1,0},{2,3},{3,2},{4,5},{5,4},{6,7},{7,6},{8,9},{9,8},{10,11... | collective-permute-start | bytes 122888 | tf_op jit(solution)/shard_map/ppermute | solution.py:36
  130.1 5.8 %copy-start = (f32[3,512,1024]{2,1,0:T(8,128)S(1)}, f32[3,512,1024]{2,1,0:T(8,128)}, u32[]{:S(2)}) copy-start(f32[3,512,1024]{2,1,0:T(8,128)} %get-tuple-element.329) | copy-start | bytes 18874372
  130.1 10.8 %slice-start.4 = ((s8[6291456]{0:T(1024)(128)(4,1)}), s8[4194304]{0:T(1024)(128)(4,1)S(1)}, s32[]{:S(2)}) async-start(s8[6291456]{0:T(1024)(128)(4,1)} %bitcast.339), calls=%async_computation.4 | async-start | bytes 8388608
  135.9 5.1 %slice-start.5 = ((s8[6291456]{0:T(1024)(128)(4,1)}), s8[2097152]{0:T(1024)(128)(4,1)S(1)}, s32[]{:S(2)}) async-start(s8[6291456]{0:T(1024)(128)(4,1)} %bitcast.339), calls=%async_computation.5 | async-start | bytes 4194304
  141.0 5.9 %slice-start.2 = ((s8[6291456]{0:T(1024)(128)(4,1)}), s8[4194304]{0:T(1024)(128)(4,1)S(1)}, s32[]{:S(2)}) async-start(s8[6291456]{0:T(1024)(128)(4,1)} %bitcast.337), calls=%async_computation.2 | async-start | bytes 8388608
  141.0 5.9 %slice-start.3 = ((s8[6291456]{0:T(1024)(128)(4,1)}), s8[2097152]{0:T(1024)(128)(4,1)S(1)}, s32[]{:S(2)}) async-start(s8[6291456]{0:T(1024)(128)(4,1)} %bitcast.337), calls=%async_computation.3 | async-start | bytes 4194304
  145.0 5.7 %slice-start = ((s8[6291456]{0:T(1024)(128)(4,1)}), s8[2097152]{0:T(1024)(128)(4,1)S(1)}, s32[]{:S(2)}) async-start(s8[6291456]{0:T(1024)(128)(4,1)} %bitcast.335), calls=%async_computation | async-start | bytes 4194304
  146.9 3.8 %slice-start.1 = ((s8[6291456]{0:T(1024)(128)(4,1)}), s8[4194304]{0:T(1024)(128)(4,1)S(1)}, s32[]{:S(2)}) async-start(s8[6291456]{0:T(1024)(128)(4,1)} %bitcast.335), calls=%async_computation.1 | async-start | bytes 8388608
where the time goes:
time: 156 us; the launch traced here: 155 us
  other arithmetic  70.7 us (45%)
  waiting for transfers between devices  39.4 us (25%)
  local copies, waits for them, and re-layouts  30.4 us (19%)
  starting transfers between devices  13.9 us (9%)
    ppermute x5, waiting for transfers between devices, swapped(): return lax.ppermute(value, axis, pairs)  39.4 us
    reduce_sum x7, other arithmetic, tile_accel(): jnp.sum(radial * offset[0] + quad_x * inverse_five, axis=1)  29.3 us
    gather x5, local copies, waits for them, and re-layouts, shards(): jnp.take(held_cells, slot_index, axis=1)  20.6 us
    reduce_sum x3, other arithmetic, tile_accel(): distance = jnp.sum(offset * offset, axis=0) + soften  17 us
    neg x9, other arithmetic, tile_accel(): radial = -sources[0][None, :] * inverse_three  9.37 us
    ppermute x5, starting transfers between devices, swapped(): return lax.ppermute(value, axis, pairs)  7.75 us
    ppermute x1, starting transfers between devices, padded(): lax.ppermute(tail, axis, [(i, (i + 1) % count) for i in range(ends)])  4.87 us
    unnamed x28, local copies, waits for them, and re-layouts  3.65 us
  transfers between devices with their start and end apart: 7, of which 3 were waited for; matrix products, arithmetic and copies ran while one was open for 19% of the time, Pallas kernels for 0%

commit v1 on v0

v1 whole, which is shorter than its diff:
```python
import functools
import math

import jax
import jax.numpy as jnp
from jax import lax
from jax.experimental import pallas as pl
from jax.experimental.pallas import tpu as pltpu
from jax.sharding import PartitionSpec as P

AXES = ("gx", "gy", "gz")
LANES = 128
SUBS = 8
NBLK = 4
SOFT = 0.01
QROWS = 64
SROWS = 32
FROWS = 48
UNIT = 256
A_PART = (0, 0, 1, 1, 0, 2)
B_PART = (0, 1, 0, 1, 2, 0)

f32 = jnp.float32
bf16 = jnp.bfloat16
dot = functools.partial(jnp.dot, preferred_element_type=f32)


def split3(value):
    one = value.astype(bf16).astype(f32)
    rest = value - one
    two = rest.astype(bf16).astype(f32)
    three = (rest - two).astype(bf16).astype(f32)
    return one, two, three


def halves(value):
    high = value.astype(bf16)
    return high, (value - high.astype(f32)).astype(bf16)


def paired(values, parts):
    pieces = [split3(v) for v in values]
    return [p[k] for k in parts for p in pieces]


def quad_rows(mass, center, quad):
    cx, cy, cz = center
    qxx, qyy, qzz, qxy, qxz, qyz = quad
    vx = qxx * cx + qxy * cy + qxz * cz
    vy = qxy * cx + qyy * cy + qyz * cz
    vz = qxz * cx + qyz * cy + qzz * cz
    h = 2.5 / jnp.maximum(mass, 1e-3)
    linear = [-2.0 * h * vx, -2.0 * h * vy, -2.0 * h * vz]
    square = [h * qxx, h * qyy, h * qzz, 2.0 * h * qxy, 2.0 * h * qxz, 2.0 * h * qyz]
    rows = list(split3(h * (cx * vx + cy * vy + cz * vz)))
    rows += paired(linear + square, B_PART)
    rows += [jnp.zeros_like(mass)] * (QROWS - len(rows))
    return rows, (vx, vy, vz)


def dist_rows(mass, center):
    cx, cy, cz = center
    rows = list(split3(cx * cx + cy * cy + cz * cz + SOFT))
    rows += paired([-2.0 * cx, -2.0 * cy, -2.0 * cz], B_PART)
    rows += [jnp.ones_like(mass)] * 3
    rows += [jnp.zeros_like(mass)] * (SROWS - len(rows))
    return rows


def mass_rows(mass, center):
    cx, cy, cz = center
    rows = paired([mass, mass * cx, mass * cy, mass * cz], (0, 1, 2))
    return rows + [jnp.zeros_like(mass)] * (16 - len(rows))


def moment_rows(quad, v):
    rows = paired(list(quad) + list(v), (0, 1, 2))
    return rows + [jnp.zeros_like(v[0])] * (32 - len(rows))


def target_rows(x, y, z):
    one = jnp.ones_like(x)
    zero = jnp.zeros_like(x)
    q = [one] * 3 + paired([x, y, z, x * x, y * y, z * z, x * y, x * z, y * z], A_PART)
    q += [zero] * (QROWS - len(q))
    s = [one] * 3 + paired([x, y, z], A_PART) + list(split3(x * x + y * y + z * z))
    s += [zero] * (SROWS - len(s))
    return q, s


def stage_rows(feat, rows, sub):
    for k, value in enumerate(rows):
        feat[k * sub : (k + 1) * sub, :] = value


def cell_features(read, sub, feat, lhs, fw, fu, base):
    mass, center, quad = read
    q, v = quad_rows(mass, center, quad)
    rows = q + dist_rows(mass, center) + mass_rows(mass, center) + moment_rows(quad, v)
    stage_rows(feat, rows, sub)
    wide = QROWS + SROWS
    for r in range(sub):
        at = slice(base + r * LANES, base + (r + 1) * LANES)
        left = feat[pl.ds(r, wide, stride=sub), :]
        lhs[at, 0:wide] = left.T.astype(bf16)
        right = feat[pl.ds(wide * sub + r, FROWS, stride=sub), :]
        fw[:, at] = right[0:16].astype(bf16)
        fu[:, at] = right[16:FROWS].astype(bf16)


def body_features(mass, center, sub, feat, lhs, fw, base):
    rows = dist_rows(mass, center) + mass_rows(mass, center)
    stage_rows(feat, rows, sub)
    for r in range(sub):
        at = slice(base + r * LANES, base + (r + 1) * LANES)
        left = feat[pl.ds(r, SROWS, stride=sub), :]
        lhs[at, 0:SROWS] = left.T.astype(bf16)
        right = feat[pl.ds(SROWS * sub + r, 16, stride=sub), :]
        fw[:, at] = right.astype(bf16)


def twice(left, high, low):
    return dot(jnp.concatenate([left, left], 1), jnp.concatenate([high, low], 0))


def pair_sums(cells, bodies, at_q, at_s, lhs, fw, fu, blhs, bfw, aw, au):
    targets = at_q.shape[1]
    wide = math.gcd(targets, UNIT)
    units = []
    for count, is_cell in ((cells, True), (bodies, False)):
        deep = math.gcd(count, UNIT) if count else 1
        for b in range(count // deep):
            for t in range(targets // wide):
                units.append((slice(b * deep, (b + 1) * deep), slice(t * wide, (t + 1) * wide), is_cell))
    aw[...] = jnp.zeros_like(aw)
    au[...] = jnp.zeros_like(au)

    def first(src, tgt, is_cell):
        if not is_cell:
            return dot(blhs[src, 0:SROWS], at_s[QROWS : QROWS + SROWS, tgt]), None
        s = dot(lhs[src, 0 : QROWS + SROWS], at_s[:, tgt])
        return s, dot(lhs[src, 0:QROWS], at_q[:, tgt])

    def second(src, tgt, is_cell, s, q):
        y = lax.rsqrt(s)
        y2 = y * y
        y3 = y * y2
        if not is_cell:
            aw[:, tgt] += twice(bfw[:, src], *halves(y3))
            return
        y5 = y3 * y2
        w = y3 + (q * y2) * y5
        aw[:, tgt] += twice(fw[:, src], *halves(w))
        au[:, tgt] += twice(fu[:, src], *halves(y5))

    ready = first(*units[0])
    for k, unit in enumerate(units):
        coming = first(*units[k + 1]) if k + 1 < len(units) else None
        second(*unit, *ready)
        ready = coming


def from_sums(x, y, z, aw, au):
    w = aw[0:4, :] + aw[4:8, :] + aw[8:12, :]
    u = au[0:9, :] + au[9:18, :] + au[18:27, :]

    def g(k):
        return u[k : k + 1, :]

    return (
        g(0) * x + g(3) * y + g(4) * z - g(6) - (w[0:1] * x - w[1:2]),
        g(3) * x + g(1) * y + g(5) * z - g(7) - (w[0:1] * y - w[2:3]),
        g(4) * x + g(5) * y + g(2) * z - g(8) - (w[0:1] * z - w[3:4]),
    )


def open_kernel(mass, center, quad, lists, masks, own, place, pick, vm, vc, vq, vl, vk, tab, sems):
    moves = [
        pltpu.make_async_copy(src, dst, sems.at[k])
        for k, (src, dst) in enumerate(((lists, vl), (masks, vk), (mass, vm), (center, vc), (quad, vq)))
    ]
    for move in moves:
        move.start()
    levels = lists.shape[0]
    moves[0].wait()
    moves[1].wait()
    slots = lists.shape[1] // LANES
    for level in range(levels):
        for r in range(slots):
            at = slice(r * LANES, (r + 1) * LANES)
            index = vl[level : level + 1, at]
            live = vk[level : level + 1, at]
            place[2 * level * slots + r : 2 * level * slots + r + 1, :] = jnp.where(live > 0, index >> 7, -1)
            place[(2 * level + 1) * slots + r : (2 * level + 1) * slots + r + 1, :] = index & (LANES - 1)
    moves[2].wait()
    moves[3].wait()
    moves[4].wait()
    rows = center.shape[1] // LANES
    for k in range(rows):
        at = slice(k * LANES, (k + 1) * LANES)
        tab[k * 16 : k * 16 + 1, :] = vm[k : k + 1, :]
        tab[k * 16 + 1 : k * 16 + 4, :] = vc[:, at]
        tab[k * 16 + 4 : k * 16 + 10, :] = vq[:, at]
    for f in range(10):
        own[f * rows : (f + 1) * rows, :] = tab[pl.ds(f, rows, stride=16), :]
    picked(0, [own], place, pick)


def picked(level, tables, place, pick):
    slots = pick.shape[0] // 10 if pick.shape[0] % 10 == 0 else SUBS
    row = place[2 * level * slots : (2 * level + 1) * slots, :]
    lane = place[(2 * level + 1) * slots : (2 * level + 2) * slots, :]
    out = [jnp.zeros((slots, LANES), f32)] * 10
    base = 0
    for table in tables:
        rows = table.shape[0] // 10
        for k in range(rows):
            hit = row == base + k
            for f in range(10):
                line = jnp.broadcast_to(table[f * rows + k : f * rows + k + 1, :], (slots, LANES))
                got = jnp.take_along_axis(line, lane, axis=1, mode="promise_in_bounds")
                out[f] = jnp.where(hit, got, out[f])
        base += rows
    for f in range(10):
        pick[f * slots : (f + 1) * slots, :] = out[f]


def pick_kernel(level, *refs):
    place, *tables = refs[:-1]
    picked(level, tables, place, refs[-1])


def read_cells(table, first, count, mid):
    rows = table.shape[0] // 10

    def row(f):
        return table[f * rows + first : f * rows + first + count, :]

    center = [row(1 + k) - mid[k : k + 1, :] for k in range(3)]
    return row(0), center, [row(4 + k) for k in range(6)]


def start_kernel(pos, mass, lists, counts, at_q, at_s, shifted, mid, face, bod, out, feat, blhs, bfw, aw, au):
    count = pos.shape[1]
    blocks = count // LANES
    low = jnp.min(pos[...], axis=1, keepdims=True)
    high = jnp.max(pos[...], axis=1, keepdims=True)
    middle = jnp.broadcast_to(0.5 * (low + high), (3, LANES))
    mid[0:3, :] = middle
    moved = pos[...] - middle[:, 0:1]
    shifted[0:3, :] = moved
    x, y, z = moved[0:1], moved[1:2], moved[2:3]
    q, s = target_rows(x, y, z)
    at_q[...] = jnp.concatenate(q, axis=0).astype(bf16)
    at_s[...] = jnp.concatenate([jnp.zeros_like(x)] * QROWS + s, axis=0).astype(bf16)
    bod[0:blocks, :] = mass[...]
    for f in range(3):
        for k in range(blocks):
            at = slice(k * LANES, (k + 1) * LANES)
            bod[(f + 1) * blocks + k : (f + 1) * blocks + k + 1, :] = pos[f : f + 1, at]
    for side in range(2):
        for j in range(blocks):
            block = lists[side, j]
            live = (j < counts[0, side]).astype(f32)
            for f in range(4):
                to = side * 4 * blocks + f * blocks + j
                face[to : to + 1, :] = bod[pl.ds(f * blocks + block, 1), :] * live
    center = [bod[(1 + k) * blocks : (2 + k) * blocks, :] - mid[k : k + 1, :] for k in range(3)]
    body_features(bod[0:blocks, :], center, blocks, feat, blhs, bfw, 0)
    pair_sums(0, count, at_q, at_s, None, None, None, blhs, bfw, aw, au)
    ax, ay, az = from_sums(x, y, z, aw, au)
    out[0:1, :] = ax
    out[1:2, :] = ay
    out[2:3, :] = az


def cell_kernel(first, count, at_q, at_s, shifted, mid, table, out, feat, lhs, fw, fu, aw, au):
    for g in range(count // SUBS):
        read = read_cells(table, first + g * SUBS, SUBS, mid)
        cell_features(read, SUBS, feat, lhs, fw, fu, g * SUBS * LANES)
    pair_sums(count * LANES, 0, at_q, at_s, lhs, fw, fu, None, None, aw, au)
    ax, ay, az = from_sums(shifted[0:1], shifted[1:2], shifted[2:3], aw, au)
    out[0:1, :] = ax
    out[1:2, :] = ay
    out[2:3, :] = az


def last_kernel(faces, parts, *refs):
    at_q, at_s, shifted, mid, table = refs[:5]
    sides = refs[5 : 5 + faces]
    sums = refs[5 + faces : 5 + faces + parts]
    out, feat, lhs, fw, fu, blhs, bfw, aw, au = refs[5 + faces + parts :]
    rows = table.shape[0] // 10
    for g in range(rows // SUBS):
        read = read_cells(table, g * SUBS, SUBS, mid)
        cell_features(read, SUBS, feat, lhs, fw, fu, g * SUBS * LANES)
    base = 0
    for side in sides:
        blocks = side.shape[0] // 4
        center = [side[(1 + k) * blocks : (2 + k) * blocks, :] - mid[k : k + 1, :] for k in range(3)]
        body_features(side[0:blocks, :], center, blocks, feat, blhs, bfw, base)
        base += blocks * LANES
    pair_sums(rows * LANES, base, at_q, at_s, lhs, fw, fu, blhs, bfw, aw, au)
    total = list(from_sums(shifted[0:1], shifted[1:2], shifted[2:3], aw, au))
    for part in sums:
        total = [t + part[k : k + 1, :] for k, t in enumerate(total)]
    for k in range(3):
        out[k : k + 1, :] = total[k]


def call(kernel, out_shape, args, scratch=(), in_specs=None, flops=0):
    specs = in_specs or [pl.BlockSpec(memory_space=pltpu.VMEM)] * len(args)
    many = isinstance(out_shape, (list, tuple))
    vmem = pl.BlockSpec(memory_space=pltpu.VMEM)
    return pl.pallas_call(
        kernel,
        out_shape=out_shape,
        in_specs=specs,
        out_specs=[vmem] * len(out_shape) if many else vmem,
        scratch_shapes=list(scratch),
        compiler_params=pltpu.CompilerParams(vmem_limit_bytes=32 * 2**20),
        cost_estimate=pl.CostEstimate(flops=flops, bytes_accessed=2**18, transcendentals=0),
    )(*args)


def shaped(*shape, dtype=f32):
    return jax.ShapeDtypeStruct(shape, dtype)


def sum_scratch(targets, cells, bodies):
    got = [pltpu.VMEM(((QROWS + SROWS + FROWS) * SUBS, LANES), f32)]
    if cells:
        got += [pltpu.VMEM((cells, LANES), bf16), pltpu.VMEM((16, cells), bf16), pltpu.VMEM((32, cells), bf16)]
    if bodies:
        got += [pltpu.VMEM((bodies, LANES), bf16), pltpu.VMEM((16, bodies), bf16)]
    return got + [pltpu.VMEM((16, targets), f32), pltpu.VMEM((32, targets), f32)]


def swapped(value, apart):
    mask = 2**apart
    return lax.ppermute(value, AXES, [(k, k ^ mask) for k in range(lax.axis_size(AXES))])


def shards(body_pos, body_mass, cell_mass, cell_center, cell_quad, cell_lists, slot_masks, face_lists, face_counts):
    bits = lax.axis_size(AXES).bit_length() - 1
    levels, slots = cell_lists.shape[1:]
    cells = cell_mass.shape[0]
    targets = body_mass.shape[0]
    blocks = targets // LANES
    rows = cells // LANES
    pick_rows = 10 * slots // LANES
    anywhere = pl.BlockSpec(memory_space=pl.ANY)
    vmem = pl.BlockSpec(memory_space=pltpu.VMEM)
    smem = pl.BlockSpec(memory_space=pltpu.SMEM)
    own, place, pick = call(
        open_kernel,
        [shaped(10 * rows, LANES), shaped(2 * levels * slots // LANES, LANES, dtype=jnp.int32), shaped(pick_rows, LANES)],
        [cell_mass.reshape(rows, LANES), cell_center, cell_quad, cell_lists[0], slot_masks[0]],
        [
            pltpu.VMEM((rows, LANES), f32),
            pltpu.VMEM(cell_center.shape, f32),
            pltpu.VMEM(cell_quad.shape, f32),
            pltpu.VMEM((levels, slots), jnp.int32),
            pltpu.VMEM((levels, slots), jnp.int32),
            pltpu.VMEM((rows * 16, LANES), f32),
            pltpu.SemaphoreType.DMA((5,)),
        ],
        [anywhere] * 5,
    )
    arrived = swapped(pick, bits - 1)
    at_q, at_s, shifted, mid, face, unused, near = call(
        start_kernel,
        [
            shaped(QROWS, targets, dtype=bf16),
            shaped(QROWS + SROWS, targets, dtype=bf16),
            shaped(SUBS, targets),
            shaped(SUBS, LANES),
            shaped(2 * 4 * blocks, LANES),
            shaped(4 * blocks, LANES),
            shaped(3, targets),
        ],
        [body_pos, body_mass.reshape(blocks, LANES), face_lists[0], face_counts],
        sum_scratch(targets, 0, targets),
        [vmem, vmem, smem, smem],
        flops=targets * targets * 20,
    )
    common = [at_q, at_s, shifted, mid]

    def cell_sums(table, first, count):
        kernel = functools.partial(cell_kernel, first, count)
        flops = targets * count * LANES * 50
        return call(kernel, shaped(3, targets), common + [table], sum_scratch(targets, count * LANES, 0), flops=flops)

    lower, upper = face[: 4 * blocks], face[4 * blocks :]
    count = lax.axis_size("gz")
    if count == 2:
        side = jnp.where(lax.axis_index("gz") == 0, upper, lower)
        sides = [lax.ppermute(side, "gz", [(0, 1), (1, 0)])]
    else:
        sides = [
            lax.ppermute(upper, "gz", [(k, k + 1) for k in range(count - 1)]),
            lax.ppermute(lower, "gz", [(k + 1, k) for k in range(count - 1)]),
        ]
    sums = [near]
    half = rows // 2
    sums.append(cell_sums(own, 0, half))
    sums.append(cell_sums(own, half, rows - half))
    tables = [own, arrived]
    for level in range(1, levels):
        pick = call(functools.partial(pick_kernel, level), shaped(pick_rows, LANES), [place] + tables)
        arrived = swapped(pick, bits - 1 - level)
        sums.append(cell_sums(tables[-1], 0, slots // LANES))
        tables.append(arrived)
    return call(
        functools.partial(last_kernel, len(sides), len(sums)),
        shaped(3, targets),
        common + [arrived] + sides + sums,
        sum_scratch(targets, slots, targets * len(sides)),
        flops=targets * slots * 50,
    )


def solution(mesh):
    in_specs = (
        P(None, AXES),
        P(AXES),
        P(AXES),
        P(None, AXES),
        P(None, AXES),
        P(AXES, None, None),
        P(AXES, None, None),
        P(AXES, None, None),
        P(AXES, None),
    )
    out_specs = P(None, AXES)
    return jax.shard_map(shards, mesh=mesh, in_specs=in_specs, out_specs=out_specs, check_vma=False)
```

time: 156 us -> 33.8 us (0.22)
  other arithmetic: 70.7 us -> 0.01 us
  waiting for transfers between devices: 39.4 us -> 5.18 us
  local copies, waits for them, and re-layouts: 30.4 us -> 1.53 us
  Pallas kernels: 0 us -> 16.2 us
  starting transfers between devices: 13.9 us -> 10.6 us
    reduce_sum x12 -> x0, other arithmetic: 47.7 us -> none  [the longest x7 29.3 us: tile_accel(): jnp.sum(radial * offset[0] + quad_x * inverse_five, axis=1)]
    ppermute x7 -> x6, waiting for transfers between devices: 39.4 us -> 5.18 us  [the longest x5 5.17 us: swapped(): lax.ppermute(value, AXES, [(k, k ^ mask) for k in range(lax.axis_size(AXE...]
    gather x6 -> x0, local copies, waits for them, and re-layouts: 21.2 us -> none  [the longest x5 20.6 us: shards(): jnp.take(held_cells, slot_index, axis=1)]
    pallas_call x0 -> x13, Pallas kernels: none -> 16.2 us  [call(): pl.pallas_call(kernel, out_shape=out_shape, in_specs=specs, out_specs=[vm...]
    neg x9 -> x0, other arithmetic: 9.37 us -> none  [tile_accel(): radial = -sources[0][None, :] * inverse_three]
    concatenate x6 -> x0, other arithmetic: 4.95 us -> none  [the longest x3 3.33 us: shards(): held_cells = jnp.concatenate([held_cells, arrived], 1)]
    mul x8 -> x0, other arithmetic: 4.11 us -> none  [the longest x5 3.51 us: shards(): jnp.take(held_cells, slot_index, axis=1)]
    ppermute x7 -> x6, starting transfers between devices: 13.9 us -> 10.6 us  [the longest x5 10.5 us: swapped(): lax.ppermute(value, AXES, [(k, k ^ mask) for k in range(lax.axis_size(AXE...]
  transfers between devices with their start and end apart: 7 -> 6, of which waited for: 3 -> 3; matrix products, arithmetic and copies ran while one was open for 19% -> 0% of each run, Pallas kernels for 0% -> 33%
where the time goes in v1:
time: 33.8 us; the launch traced here: 33.7 us
  Pallas kernels  16.2 us (48%)
  starting transfers between devices  10.6 us (31%)
  waiting for transfers between devices  5.18 us (15%)
  local copies, waits for them, and re-layouts  1.53 us (5%)
    pallas_call x13, Pallas kernels, call(): pl.pallas_call(kernel, out_shape=out_shape, in_specs=specs, out_specs=[vm...  16.2 us
    ppermute x5, starting transfers between devices, swapped(): lax.ppermute(value, AXES, [(k, k ^ mask) for k in range(lax.axis_size(AXE...  10.5 us
    ppermute x5, waiting for transfers between devices, swapped(): lax.ppermute(value, AXES, [(k, k ^ mask) for k in range(lax.axis_size(AXE...  5.17 us
    unnamed x15, local copies, waits for them, and re-layouts  1.53 us
  transfers between devices with their start and end apart: 6, of which 3 were waited for; matrix products, arithmetic and copies ran while one was open for 0% of the time, Pallas kernels for 33%

profile of v1, /device:TPU:0, one launch (start us, length us, event | category | flops | bytes accessed | tf_op | source)
XLA Modules:
  0.0 33.7 jit_solution(13263207941886972686)
XLA Ops:
  0.0 0.8 %copy_bitcast_fusion = (s32[5,1024]{1,0:T(8,128)S(1)}, s32[5,1024]{1,0:T(8,128)S(1)}) fusion(s32[1,5,1024]{2,0,1:T(1,128)} %param.15, s32[1,5,1024]{2,0,1:T(1,128)} %param.14), kind=kLoop, calls=%fused_computation | loop fusion | bytes 81920
  0.8 0.0 copy-done
  0.8 0.0 copy-done.1
  0.8 0.6 %shard_map.92 = (f32[160,128]{1,0:T(8,128)S(1)}, s32[80,128]{1,0:T(8,128)S(1)}, f32[80,128]{1,0:T(8,128)S(1)}) custom-call(f32[16,128]{1,0:T(8,128)S(1)} %bitcast.7, f32[3,2048]{1,0:T(4,128)S(1)} %copy-done.1, f32[6,2048]{1,0:T(8,128)S(1)} %copy-done, s32[5,1024]{1,0:T(8,128)S(1)} %get-tuple-element.24.lists, s32[5,1024]{1,0:T(8,128)S(1)} %get-tuple-element.23.masks), custom_call_target="tpu_custom_call" | custom-call | bytes 262144 | tf_op jit(solution)/shard_map/pallas_call | solution.py:315
  1.4 3.0 %collective-permute-start = (f32[80,128]{1,0:T(8,128)S(1)}, f32[80,128]{1,0:T(8,128)S(1)}, u32[]{:S(2)}, u32[]{:S(2)}) collective-permute-start(f32[80,128]{1,0:T(8,128)S(1)} %get-tuple-element.20), channel_id=1, source_target_pairs={{0,16},{1,17},{2,18},{3,19},{4,20},{5,21},{6,22},{7,23},{8,24},{9,... | collective-permute-start | bytes 122888 | tf_op jit(solution)/shard_map/ppermute | solution.py:341
  4.4 2.0 %collective-permute-done.refs_2_.table = f32[80,128]{1,0:T(8,128)S(1)} collective-permute-done((f32[80,128]{1,0:T(8,128)S(1)}, f32[80,128]{1,0:T(8,128)S(1)}, u32[]{:S(2)}, u32[]{:S(2)}) %collective-permute-start) | collective-permute-done | bytes 40992 | tf_op jit(solution)/shard_map/ppermute | solution.py:341
  6.4 0.3 shard_map.93
  6.7 0.1 collective-permute-start.1
  6.8 1.2 %collective-permute-done.1.refs_3_.table = f32[80,128]{1,0:T(8,128)S(1)} collective-permute-done((f32[80,128]{1,0:T(8,128)S(1)}, f32[80,128]{1,0:T(8,128)S(1)}, u32[]{:S(2)}, u32[]{:S(2)}) %collective-permute-start.1) | collective-permute-done | bytes 40992 | tf_op jit(solution)/shard_map/ppermute | solution.py:341
  8.0 0.4 %shard_map.94 = f32[80,128]{1,0:T(8,128)S(1)} custom-call(s32[80,128]{1,0:T(8,128)S(1)} %get-tuple-element.18.refs_0_, f32[160,128]{1,0:T(8,128)S(1)} %get-tuple-element.19.refs_1_.table, f32[80,128]{1,0:T(8,128)S(1)} %collective-permute-done.refs_2_.table, f32[80,128]{1,0:T(8,128)S(1)} %collective-permute-done.1.refs_3_.table), custom_call_target="tpu_custom_call" | custom-call | bytes 262144 | tf_op jit(solution)/shard_map/pallas_call | solution.py:315
  8.4 3.2 %collective-permute-start.2 = (f32[80,128]{1,0:T(8,128)S(1)}, f32[80,128]{1,0:T(8,128)S(1)}, u32[]{:S(2)}, u32[]{:S(2)}) collective-permute-start(f32[80,128]{1,0:T(8,128)S(1)} %shard_map.94), channel_id=1, source_target_pairs={{0,4},{1,5},{2,6},{3,7},{4,0},{5,1},{6,2},{7,3},{8,12},{9,13},{10,... | collective-permute-start | bytes 122888 | tf_op jit(solution)/shard_map/ppermute | solution.py:341
  11.6 2.0 %collective-permute-done.2.refs_4_.table = f32[80,128]{1,0:T(8,128)S(1)} collective-permute-done((f32[80,128]{1,0:T(8,128)S(1)}, f32[80,128]{1,0:T(8,128)S(1)}, u32[]{:S(2)}, u32[]{:S(2)}) %collective-permute-start.2) | collective-permute-done | bytes 40992 | tf_op jit(solution)/shard_map/ppermute | solution.py:341
  13.6 0.5 %shard_map.95 = f32[80,128]{1,0:T(8,128)S(1)} custom-call(s32[80,128]{1,0:T(8,128)S(1)} %get-tuple-element.18.refs_0_, f32[160,128]{1,0:T(8,128)S(1)} %get-tuple-element.19.refs_1_.table, f32[80,128]{1,0:T(8,128)S(1)} %collective-permute-done.refs_2_.table, f32[80,128]{1,0:T(8,128)S(1)} %collective-permute-done.1.refs_3_.table, ...), custom_call_target="tpu_custom_call" | custom-call | bytes 262144 | tf_op jit(solution)/shard_map/pallas_call | solution.py:315
  14.1 0.0 copy-start.3
  14.1 2.0 %collective-permute-start.3 = (f32[80,128]{1,0:T(8,128)S(1)}, f32[80,128]{1,0:T(8,128)S(1)}, u32[]{:S(2)}, u32[]{:S(2)}) collective-permute-start(f32[80,128]{1,0:T(8,128)S(1)} %shard_map.95), channel_id=1, source_target_pairs={{0,2},{1,3},{2,0},{3,1},{4,6},{5,7},{6,4},{7,5},{8,10},{9,11},{10,... | collective-permute-start | bytes 122888 | tf_op jit(solution)/shard_map/ppermute | solution.py:341
  16.1 0.0 copy-done.3
  16.1 0.7 %copy-done.4 = f32[512]{0:T(512)S(1)} copy-done((f32[512]{0:T(512)S(1)}, f32[512]{0:T(512)}, u32[]{:S(2)}) %copy-start.4) | copy-done | bytes 2072
  16.8 0.0 copy-done.5
  16.8 1.5 %shard_map.91 = (bf16[64,512]{1,0:T(8,128)(2,1)S(1)}, bf16[96,512]{1,0:T(8,128)(2,1)S(1)}, f32[8,512]{1,0:T(8,128)S(1)}, f32[8,128]{1,0:T(8,128)S(1)}, f32[32,12...) custom-call(f32[3,512]{1,0:T(4,128)S(1)} %copy-done.3, f32[4,128]{1,0:T(4,128)S(1)} %bitcast.8, ...), custom_call_target="tpu_custom_call" | custom-call | flops 5242880 | bytes 262144 | tf_op jit(solution)/shard_map/pallas_call | solution.py:315
  18.3 0.0 collective-permute-done.3.refs_5_.table
  18.3 0.6 %shard_map.96 = f32[80,128]{1,0:T(8,128)S(1)} custom-call(s32[80,128]{1,0:T(8,128)S(1)} %get-tuple-element.18.refs_0_, f32[160,128]{1,0:T(8,128)S(1)} %get-tuple-element.19.refs_1_.table, f32[80,128]{1,0:T(8,128)S(1)} %collective-permute-done.refs_2_.table, f32[80,128]{1,0:T(8,128)S(1)} %collective-permute-done.1.refs_3_.table, ...), custom_call_target="tpu_custom_call" | custom-call | bytes 262144 | tf_op jit(solution)/shard_map/pallas_call | solution.py:315
  18.9 2.3 %collective-permute-start.4 = (f32[80,128]{1,0:T(8,128)S(1)}, f32[80,128]{1,0:T(8,128)S(1)}, u32[]{:S(2)}, u32[]{:S(2)}) collective-permute-start(f32[80,128]{1,0:T(8,128)S(1)} %shard_map.96), channel_id=1, source_target_pairs={{0,1},{1,0},{2,3},{3,2},{4,5},{5,4},{6,7},{7,6},{8,9},{9,8},{10,11... | collective-permute-start | bytes 122888 | tf_op jit(solution)/shard_map/ppermute | solution.py:341
  21.1 0.1 collective-permute-start.5
  21.2 1.6 %shard_map.98.refs_8_ = f32[3,512]{1,0:T(4,128)S(1)} custom-call(bf16[64,512]{1,0:T(8,128)(2,1)S(1)} %get-tuple-element.14.at_q.refs_0_, bf16[96,512]{1,0:T(8,128)(2,1)S(1)} %get-tuple-element.15.at_s.refs_1_, f32[8,512]{1,0:T(8,128)S(1)} %get-tuple-element.16.shifted.refs_2_, f32[8,128]{1,0:T(8,128)S(1)} %get-tuple-element.17.mid.refs_3_, ...), custom_call_target="tpu_custom_call" | custom-call | flops 26214400 | bytes 262144 | tf_op jit(solution)/shard_map/pallas_call | solution.py:315
  22.9 1.6 %shard_map.97.refs_7_ = f32[3,512]{1,0:T(4,128)S(1)} custom-call(bf16[64,512]{1,0:T(8,128)(2,1)S(1)} %get-tuple-element.14.at_q.refs_0_, bf16[96,512]{1,0:T(8,128)(2,1)S(1)} %get-tuple-element.15.at_s.refs_1_, f32[8,512]{1,0:T(8,128)S(1)} %get-tuple-element.16.shifted.refs_2_, f32[8,128]{1,0:T(8,128)S(1)} %get-tuple-element.17.mid.refs_3_, ...), custom_call_target="tpu_custom_call" | custom-call | flops 26214400 | bytes 262144 | tf_op jit(solution)/shard_map/pallas_call | solution.py:315
  24.5 1.6 %shard_map.99.refs_9_ = f32[3,512]{1,0:T(4,128)S(1)} custom-call(bf16[64,512]{1,0:T(8,128)(2,1)S(1)} %get-tuple-element.14.at_q.refs_0_, bf16[96,512]{1,0:T(8,128)(2,1)S(1)} %get-tuple-element.15.at_s.refs_1_, f32[8,512]{1,0:T(8,128)S(1)} %get-tuple-element.16.shifted.refs_2_, f32[8,128]{1,0:T(8,128)S(1)} %get-tuple-element.17.mid.refs_3_, ...), custom_call_target="tpu_custom_call" | custom-call | flops 26214400 | bytes 262144 | tf_op jit(solution)/shard_map/pallas_call | solution.py:315
  26.1 1.6 %shard_map.100.refs_10_ = f32[3,512]{1,0:T(4,128)S(1)} custom-call(bf16[64,512]{1,0:T(8,128)(2,1)S(1)} %get-tuple-element.14.at_q.refs_0_, bf16[96,512]{1,0:T(8,128)(2,1)S(1)} %get-tuple-element.15.at_s.refs_1_, f32[8,512]{1,0:T(8,128)S(1)} %get-tuple-element.16.shifted.refs_2_, f32[8,128]{1,0:T(8,128)S(1)} %get-tuple-element.17.mid.refs_3_, ...), custom_call_target="tpu_custom_call" | custom-call | flops 26214400 | bytes 262144 | tf_op jit(solution)/shard_map/pallas_call | solution.py:315
  27.8 1.6 %shard_map.101.refs_11_ = f32[3,512]{1,0:T(4,128)S(1)} custom-call(bf16[64,512]{1,0:T(8,128)(2,1)S(1)} %get-tuple-element.14.at_q.refs_0_, bf16[96,512]{1,0:T(8,128)(2,1)S(1)} %get-tuple-element.15.at_s.refs_1_, f32[8,512]{1,0:T(8,128)S(1)} %get-tuple-element.16.shifted.refs_2_, f32[8,128]{1,0:T(8,128)S(1)} %get-tuple-element.17.mid.refs_3_, ...), custom_call_target="tpu_custom_call" | custom-call | flops 26214400 | bytes 262144 | tf_op jit(solution)/shard_map/pallas_call | solution.py:315
  29.4 1.6 %shard_map.102.refs_12_ = f32[3,512]{1,0:T(4,128)S(1)} custom-call(bf16[64,512]{1,0:T(8,128)(2,1)S(1)} %get-tuple-element.14.at_q.refs_0_, bf16[96,512]{1,0:T(8,128)(2,1)S(1)} %get-tuple-element.15.at_s.refs_1_, f32[8,512]{1,0:T(8,128)S(1)} %get-tuple-element.16.shifted.refs_2_, f32[8,128]{1,0:T(8,128)S(1)} %get-tuple-element.17.mid.refs_3_, ...), custom_call_target="tpu_custom_call" | custom-call | flops 26214400 | bytes 262144 | tf_op jit(solution)/shard_map/pallas_call | solution.py:315
  31.0 0.0 collective-permute-done.5.refs_5_
  31.0 0.0 collective-permute-done.4.refs_4_
  31.1 2.6 %shard_map.103 = f32[3,512]{1,0:T(4,128)} custom-call(bf16[64,512]{1,0:T(8,128)(2,1)S(1)} %get-tuple-element.14.at_q.refs_0_, bf16[96,512]{1,0:T(8,128)(2,1)S(1)} %get-tuple-element.15.at_s.refs_1_, f32[8,512]{1,0:T(8,128)S(1)} %get-tuple-element.16.shifted.refs_2_, f32[8,128]{1,0:T(8,128)S(1)} %get-tuple-element.17.mid.refs_3_, ...), custom_call_target="tpu_custom_call" | custom-call | flops 26214400 | bytes 262144 | tf_op jit(solution)/shard_map/pallas_call | solution.py:315
  (9 shorter events, 0.0 us)
Async XLA Ops:
  0.0 0.8 %copy-start = (f32[6,2048]{1,0:T(8,128)S(1)}, f32[6,2048]{1,0:T(8,128)}, u32[]{:S(2)}) copy-start(f32[6,2048]{1,0:T(8,128)} %quad.1) | copy-start | bytes 147460
  0.0 0.8 %copy-start.1 = (f32[3,2048]{1,0:T(4,128)S(1)}, f32[3,2048]{1,0:T(4,128)}, u32[]{:S(2)}) copy-start(f32[3,2048]{1,0:T(4,128)} %center.1) | copy-start | bytes 73732
  0.0 0.8 %copy-start.2 = (f32[2048]{0:T(1024)S(1)}, f32[2048]{0:T(1024)}, u32[]{:S(2)}) copy-start(f32[2048]{0:T(1024)} %param.11) | copy-start | bytes 24580
  1.4 5.0 %collective-permute-start = (f32[80,128]{1,0:T(8,128)S(1)}, f32[80,128]{1,0:T(8,128)S(1)}, u32[]{:S(2)}, u32[]{:S(2)}) collective-permute-start(f32[80,128]{1,0:T(8,128)S(1)} %get-tuple-element.20), channel_id=1, source_target_pairs={{0,16},{1,17},{2,18},{3,19},{4,20},{5,21},{6,22},{7,23},{8,24},{9,... | collective-permute-start | bytes 122888 | tf_op jit(solution)/shard_map/ppermute | solution.py:341
  6.7 1.3 %collective-permute-start.1 = (f32[80,128]{1,0:T(8,128)S(1)}, f32[80,128]{1,0:T(8,128)S(1)}, u32[]{:S(2)}, u32[]{:S(2)}) collective-permute-start(f32[80,128]{1,0:T(8,128)S(1)} %shard_map.93), channel_id=1, source_target_pairs={{0,8},{1,9},{2,10},{3,11},{4,12},{5,13},{6,14},{7,15},{8,0},{9,1},... | collective-permute-start | bytes 122888 | tf_op jit(solution)/shard_map/ppermute | solution.py:341
  8.4 5.2 %collective-permute-start.2 = (f32[80,128]{1,0:T(8,128)S(1)}, f32[80,128]{1,0:T(8,128)S(1)}, u32[]{:S(2)}, u32[]{:S(2)}) collective-permute-start(f32[80,128]{1,0:T(8,128)S(1)} %shard_map.94), channel_id=1, source_target_pairs={{0,4},{1,5},{2,6},{3,7},{4,0},{5,1},{6,2},{7,3},{8,12},{9,13},{10,... | collective-permute-start | bytes 122888 | tf_op jit(solution)/shard_map/ppermute | solution.py:341
  13.6 2.5 %copy-start.6 = (s32[1,2]{1,0:T(1,128)S(1)}, s32[1,2]{1,0:T(1,128)}, u32[]{:S(2)}) copy-start(s32[1,2]{1,0:T(1,128)} %counts.1) | copy-start | bytes 28
  14.1 2.0 %copy-start.3 = (f32[3,512]{1,0:T(4,128)S(1)}, f32[3,512]{1,0:T(4,128)}, u32[]{:S(2)}) copy-start(f32[3,512]{1,0:T(4,128)} %pos.1) | copy-start | bytes 18436
  14.1 4.1 %collective-permute-start.3 = (f32[80,128]{1,0:T(8,128)S(1)}, f32[80,128]{1,0:T(8,128)S(1)}, u32[]{:S(2)}, u32[]{:S(2)}) collective-permute-start(f32[80,128]{1,0:T(8,128)S(1)} %shard_map.95), channel_id=1, source_target_pairs={{0,2},{1,3},{2,0},{3,1},{4,6},{5,7},{6,4},{7,5},{8,10},{9,11},{10,... | collective-permute-start | bytes 122888 | tf_op jit(solution)/shard_map/ppermute | solution.py:341
  16.1 0.7 %copy-start.4 = (f32[512]{0:T(512)S(1)}, f32[512]{0:T(512)}, u32[]{:S(2)}) copy-start(f32[512]{0:T(512)} %param.10) | copy-start | bytes 6148
  16.1 0.7 %copy-start.5 = (s32[1,2,4]{2,1,0:T(2,128)S(1)}, s32[1,2,4]{2,1,0:T(2,128)}, u32[]{:S(2)}) copy-start(s32[1,2,4]{2,1,0:T(2,128)} %param.16) | copy-start | bytes 100
  18.9 12.2 %collective-permute-start.4 = (f32[80,128]{1,0:T(8,128)S(1)}, f32[80,128]{1,0:T(8,128)S(1)}, u32[]{:S(2)}, u32[]{:S(2)}) collective-permute-start(f32[80,128]{1,0:T(8,128)S(1)} %shard_map.96), channel_id=1, source_target_pairs={{0,1},{1,0},{2,3},{3,2},{4,5},{5,4},{6,7},{7,6},{8,9},{9,8},{10,11... | collective-permute-start | bytes 122888 | tf_op jit(solution)/shard_map/ppermute | solution.py:341
  21.1 9.9 %collective-permute-start.5 = (f32[16,128]{1,0:T(8,128)S(1)}, f32[16,128]{1,0:T(8,128)S(1)}, u32[]{:S(2)}, u32[]{:S(2)}) collective-permute-start(f32[16,128]{1,0:T(8,128)S(1)} %slice_select_fusion), channel_id=1, source_target_pairs={{0,1},{1,0},{2,3},{3,2},{4,5},{5,4},{6,7},{7,6},{8,9},{9,8},{10,11... | collective-permute-start | bytes 24584 | tf_op jit(solution)/shard_map/ppermute | solution.py:398

commit v2 on v1

--- a/solution.py
+++ b/solution.py
@@ -207,7 +207,7 @@
 
 
 def picked(level, tables, place, pick):
-    slots = pick.shape[0] // 10 if pick.shape[0] % 10 == 0 else SUBS
+    slots = SUBS
     row = place[2 * level * slots : (2 * level + 1) * slots, :]
     lane = place[(2 * level + 1) * slots : (2 * level + 2) * slots, :]
     out = [jnp.zeros((slots, LANES), f32)] * 10
@@ -225,13 +225,16 @@
         pick[f * slots : (f + 1) * slots, :] = out[f]
 
 
-def pick_kernel(level, *refs):
-    place, *tables = refs[:-1]
-    picked(level, tables, place, refs[-1])
+def pick_kernel(level, faces, *refs):
+    place, *tables = refs[: len(refs) - 1 - faces]
+    pick = refs[-1]
+    for face in refs[len(refs) - 1 - faces : -1]:
+        pick[pick.shape[0] - face.shape[0] :, :] = face[...]
+    picked(level, tables, place, pick)
 
 
 def read_cells(table, first, count, mid):
-    rows = table.shape[0] // 10
+    rows = table.shape[0] // 10 // SUBS * SUBS
 
     def row(f):
         return table[f * rows + first : f * rows + first + count, :]
@@ -240,7 +243,7 @@
     return row(0), center, [row(4 + k) for k in range(6)]
 
 
-def start_kernel(pos, mass, lists, counts, at_q, at_s, shifted, mid, face, bod, out, feat, blhs, bfw, aw, au):
+def start_kernel(one_side, pos, mass, lists, counts, at_q, at_s, shifted, mid, face, out, bod, feat, blhs, bfw, aw, au):
     count = pos.shape[1]
     blocks = count // LANES
     low = jnp.min(pos[...], axis=1, keepdims=True)
@@ -258,12 +261,13 @@
         for k in range(blocks):
             at = slice(k * LANES, (k + 1) * LANES)
             bod[(f + 1) * blocks + k : (f + 1) * blocks + k + 1, :] = pos[f : f + 1, at]
-    for side in range(2):
+    sides = [1 - lax.axis_index("gz")] if one_side else [0, 1]
+    for k, side in enumerate(sides):
         for j in range(blocks):
             block = lists[side, j]
             live = (j < counts[0, side]).astype(f32)
             for f in range(4):
-                to = side * 4 * blocks + f * blocks + j
+                to = k * 4 * blocks + f * blocks + j
                 face[to : to + 1, :] = bod[pl.ds(f * blocks + block, 1), :] * live
     center = [bod[(1 + k) * blocks : (2 + k) * blocks, :] - mid[k : k + 1, :] for k in range(3)]
     body_features(bod[0:blocks, :], center, blocks, feat, blhs, bfw, 0)
@@ -274,33 +278,38 @@
     out[2:3, :] = az
 
 
-def cell_kernel(first, count, at_q, at_s, shifted, mid, table, out, feat, lhs, fw, fu, aw, au):
-    for g in range(count // SUBS):
-        read = read_cells(table, first + g * SUBS, SUBS, mid)
-        cell_features(read, SUBS, feat, lhs, fw, fu, g * SUBS * LANES)
-    pair_sums(count * LANES, 0, at_q, at_s, lhs, fw, fu, None, None, aw, au)
+def cell_kernel(spans, at_q, at_s, shifted, mid, *refs):
+    tables = refs[: len(spans)]
+    out, feat, lhs, fw, fu, aw, au = refs[len(spans) :]
+    base = 0
+    for table, (first, count) in zip(tables, spans):
+        for g in range(count // SUBS):
+            read = read_cells(table, first + g * SUBS, SUBS, mid)
+            cell_features(read, SUBS, feat, lhs, fw, fu, base)
+            base += SUBS * LANES
+    pair_sums(base, 0, at_q, at_s, lhs, fw, fu, None, None, aw, au)
     ax, ay, az = from_sums(shifted[0:1], shifted[1:2], shifted[2:3], aw, au)
     out[0:1, :] = ax
     out[1:2, :] = ay
     out[2:3, :] = az
 
 
-def last_kernel(faces, parts, *refs):
+def last_kernel(merged, faces, parts, *refs):
     at_q, at_s, shifted, mid, table = refs[:5]
-    sides = refs[5 : 5 + faces]
+    sides = list(refs[5 : 5 + faces])
     sums = refs[5 + faces : 5 + faces + parts]
     out, feat, lhs, fw, fu, blhs, bfw, aw, au = refs[5 + faces + parts :]
-    rows = table.shape[0] // 10
-    for g in range(rows // SUBS):
-        read = read_cells(table, g * SUBS, SUBS, mid)
-        cell_features(read, SUBS, feat, lhs, fw, fu, g * SUBS * LANES)
+    if merged:
+        sides.append(table.at[10 * SUBS :])
+    read = read_cells(table, 0, SUBS, mid)
+    cell_features(read, SUBS, feat, lhs, fw, fu, 0)
     base = 0
     for side in sides:
         blocks = side.shape[0] // 4
         center = [side[(1 + k) * blocks : (2 + k) * blocks, :] - mid[k : k + 1, :] for k in range(3)]
         body_features(side[0:blocks, :], center, blocks, feat, blhs, bfw, base)
         base += blocks * LANES
-    pair_sums(rows * LANES, base, at_q, at_s, lhs, fw, fu, blhs, bfw, aw, au)
+    pair_sums(SUBS * LANES, base, at_q, at_s, lhs, fw, fu, blhs, bfw, aw, au)
     total = list(from_sums(shifted[0:1], shifted[1:2], shifted[2:3], aw, au))
     for part in sums:
         total = [t + part[k : k + 1, :] for k, t in enumerate(total)]
@@ -368,54 +377,69 @@
         [anywhere] * 5,
     )
     arrived = swapped(pick, bits - 1)
-    at_q, at_s, shifted, mid, face, unused, near = call(
-        start_kernel,
+    near_by = lax.axis_size("gz")
+    merged = near_by == 2 and bits == levels
+    at_q, at_s, shifted, mid, face, near = call(
+        functools.partial(start_kernel, merged),
         [
             shaped(QROWS, targets, dtype=bf16),
             shaped(QROWS + SROWS, targets, dtype=bf16),
             shaped(SUBS, targets),
             shaped(SUBS, LANES),
-            shaped(2 * 4 * blocks, LANES),
-            shaped(4 * blocks, LANES),
+            shaped((1 if merged else 2) * 4 * blocks, LANES),
             shaped(3, targets),
         ],
         [body_pos, body_mass.reshape(blocks, LANES), face_lists[0], face_counts],
-        sum_scratch(targets, 0, targets),
+        [pltpu.VMEM((4 * blocks, LANES), f32)] + sum_scratch(targets, 0, targets),
         [vmem, vmem, smem, smem],
         flops=targets * targets * 20,
     )
     common = [at_q, at_s, shifted, mid]
 
-    def cell_sums(table, first, count):
-        kernel = functools.partial(cell_kernel, first, count)
-        flops = targets * count * LANES * 50
-        return call(kernel, shaped(3, targets), common + [table], sum_scratch(targets, count * LANES, 0), flops=flops)
-
-    lower, upper = face[: 4 * blocks], face[4 * blocks :]
-    count = lax.axis_size("gz")
-    if count == 2:
-        side = jnp.where(lax.axis_index("gz") == 0, upper, lower)
-        sides = [lax.ppermute(side, "gz", [(0, 1), (1, 0)])]
-    else:
+    def cell_sums(*spans):
+        kernel = functools.partial(cell_kernel, [span[1:] for span in spans])
+        count = sum(span[2] for span in spans) * LANES
+        args = common + [span[0] for span in spans]
+        return call(kernel, shaped(3, targets), args, sum_scratch(targets, count, 0), flops=targets * count * 50)
+
+    sides = []
+    if not merged:
+        lower, upper = face[: 4 * blocks], face[4 * blocks :]
         sides = [
-            lax.ppermute(upper, "gz", [(k, k + 1) for k in range(count - 1)]),
-            lax.ppermute(lower, "gz", [(k + 1, k) for k in range(count - 1)]),
+            lax.ppermute(upper, "gz", [(k, k + 1) for k in range(near_by - 1)]),
+            lax.ppermute(lower, "gz", [(k + 1, k) for k in range(near_by - 1)]),
         ]
-    sums = [near]
     half = rows // 2
-    sums.append(cell_sums(own, 0, half))
-    sums.append(cell_sums(own, half, rows - half))
+    wide = slots // LANES
+    sums = []
     tables = [own, arrived]
+    window = [cell_sums((own, 0, half)), near]
     for level in range(1, levels):
-        pick = call(functools.partial(pick_kernel, level), shaped(pick_rows, LANES), [place] + tables)
+        tied = lax.optimization_barrier((tables[-1], *window))
+        tables[-1] = tied[0]
+        sums += tied[1:]
+        last = level == levels - 1
+        extra = [face] if merged and last else []
+        pick = call(
+            functools.partial(pick_kernel, level, len(extra)),
+            shaped(pick_rows + len(extra) * 4 * blocks, LANES),
+            [place] + tables + extra,
+        )
         arrived = swapped(pick, bits - 1 - level)
-        sums.append(cell_sums(tables[-1], 0, slots // LANES))
+        if level == 1:
+            window = [cell_sums((own, half, rows - half))]
+        elif last:
+            window = [cell_sums((tables[-2], 0, wide), (tables[-1], 0, wide))]
+        else:
+            window = [cell_sums((tables[level - 1], 0, wide))]
         tables.append(arrived)
+    sums += window
+    count = targets * (len(sides) + merged)
     return call(
-        functools.partial(last_kernel, len(sides), len(sums)),
+        functools.partial(last_kernel, merged, len(sides), len(sums)),
         shaped(3, targets),
         common + [arrived] + sides + sums,
-        sum_scratch(targets, slots, targets * len(sides)),
+        sum_scratch(targets, slots, count),
         flops=targets * slots * 50,
     )
 

time: 33.8 us -> 28.1 us (0.83)
  waiting for transfers between devices: 5.18 us -> 1.5 us
  starting transfers between devices: 10.6 us -> 8.96 us
  Pallas kernels: 16.2 us -> 15.8 us
    ppermute x5, waiting for transfers between devices: 5.17 us -> 1.5 us  [swapped(): lax.ppermute(value, AXES, [(k, k ^ mask) for k in range(lax.axis_size(AXE...]
    ppermute x5, starting transfers between devices: 10.5 us -> 8.96 us  [swapped(): lax.ppermute(value, AXES, [(k, k ^ mask) for k in range(lax.axis_size(AXE...]
    pallas_call x13 -> x12, Pallas kernels: 16.2 us -> 15.8 us  [call(): pl.pallas_call(kernel, out_shape=out_shape, in_specs=specs, out_specs=[vm...]
  transfers between devices with their start and end apart: 6 -> 5, of which waited for: 3 -> 2; matrix products, arithmetic and copies ran while one was open for 0% -> 0% of each run, Pallas kernels for 33% -> 39%
where the time goes in v2:
time: 28.1 us; the launch traced here: 27.9 us
  Pallas kernels  15.8 us (56%)
  starting transfers between devices  8.96 us (32%)
  local copies, waits for them, and re-layouts  1.52 us (5%)
  waiting for transfers between devices  1.5 us (5%)
    pallas_call x12, Pallas kernels, call(): pl.pallas_call(kernel, out_shape=out_shape, in_specs=specs, out_specs=[vm...  15.8 us
    ppermute x5, starting transfers between devices, swapped(): lax.ppermute(value, AXES, [(k, k ^ mask) for k in range(lax.axis_size(AXE...  8.96 us
    unnamed x15, local copies, waits for them, and re-layouts  1.52 us
    ppermute x5, waiting for transfers between devices, swapped(): lax.ppermute(value, AXES, [(k, k ^ mask) for k in range(lax.axis_size(AXE...  1.5 us
  transfers between devices with their start and end apart: 5, of which 2 were waited for; matrix products, arithmetic and copies ran while one was open for 0% of the time, Pallas kernels for 39%

profile of v2, /device:TPU:0, one launch (start us, length us, event | category | flops | bytes accessed | tf_op | source)
XLA Modules:
  0.0 27.9 jit_solution(12408953787181947771)
XLA Ops:
  0.0 0.0 copy-start
  0.0 0.8 %copy_bitcast_fusion = (s32[5,1024]{1,0:T(8,128)S(1)}, s32[5,1024]{1,0:T(8,128)S(1)}) fusion(s32[1,5,1024]{2,0,1:T(1,128)} %param.15, s32[1,5,1024]{2,0,1:T(1,128)} %param.14), kind=kLoop, calls=%fused_computation | loop fusion | bytes 81920
  0.8 0.0 copy-done
  0.8 0.0 copy-done.1
  0.8 0.0 copy-done.2
  0.8 0.6 %shard_map.92 = (f32[160,128]{1,0:T(8,128)S(1)}, s32[80,128]{1,0:T(8,128)S(1)}, f32[80,128]{1,0:T(8,128)S(1)}) custom-call(f32[16,128]{1,0:T(8,128)S(1)} %bitcast.7, f32[3,2048]{1,0:T(4,128)S(1)} %copy-done.1, f32[6,2048]{1,0:T(8,128)S(1)} %copy-done, s32[5,1024]{1,0:T(8,128)S(1)} %get-tuple-element.42.lists, s32[5,1024]{1,0:T(8,128)S(1)} %get-tuple-element.41.masks), custom_call_target="tpu_custom_call" | custom-call | bytes 262144 | tf_op jit(solution)/shard_map/pallas_call | solution.py:324
  1.4 0.0 copy-start.4
  1.4 3.0 %collective-permute-start = (f32[80,128]{1,0:T(8,128)S(1)}, f32[80,128]{1,0:T(8,128)S(1)}, u32[]{:S(2)}, u32[]{:S(2)}) collective-permute-start(f32[80,128]{1,0:T(8,128)S(1)} %get-tuple-element.29), channel_id=1, source_target_pairs={{0,16},{1,17},{2,18},{3,19},{4,20},{5,21},{6,22},{7,23},{8,24},{9,... | collective-permute-start | bytes 122888 | tf_op jit(solution)/shard_map/ppermute | solution.py:350
  4.5 0.0 copy-done.3
  4.5 0.0 copy-done.4
  4.5 0.7 %copy-done.5 = s32[1,2,4]{2,1,0:T(2,128)S(1)} copy-done((s32[1,2,4]{2,1,0:T(2,128)S(1)}, s32[1,2,4]{2,1,0:T(2,128)}, u32[]{:S(2)}) %copy-start.5) | copy-done | bytes 56
  5.1 0.0 copy-done.6
  5.1 1.4 %shard_map.91 = (bf16[64,512]{1,0:T(8,128)(2,1)S(1)}, bf16[96,512]{1,0:T(8,128)(2,1)S(1)}, f32[8,512]{1,0:T(8,128)S(1)}, f32[8,128]{1,0:T(8,128)S(1)}, f32[16,128]{1,0:T(8,128)S(1)}, /*index=5*/f32[3,512]{1,0:T(4,128)S(1)}) custom-call(f32[3,512]{1,0:T(4,128)S(1)} %copy-done.3, f32[4,128]{1,0:T(4,128)S(1)} %bitcast.8, s32[2,4]{1,0:T(2,128)S(1)} %bitcast.9, ...), custom_call_target="tpu_custom_call" | custom-call | flops 5242880 | bytes 262144 | tf_op jit(solution)/shard_map/pallas_call | solution.py:324
  6.6 1.6 %shard_map.93.refs_5_ = f32[3,512]{1,0:T(4,128)S(1)} custom-call(bf16[64,512]{1,0:T(8,128)(2,1)S(1)} %get-tuple-element.23.at_q.refs_0_, bf16[96,512]{1,0:T(8,128)(2,1)S(1)} %get-tuple-element.24.at_s.refs_1_, f32[8,512]{1,0:T(8,128)S(1)} %get-tuple-element.25.shifted.refs_2_, f32[8,128]{1,0:T(8,128)S(1)} %get-tuple-element.26.mid.refs_3_, ...), custom_call_target="tpu_custom_call" | custom-call | flops 26214400 | bytes 262144 | tf_op jit(solution)/shard_map/pallas_call | solution.py:324
  8.2 0.0 collective-permute-done.refs_2_.refs_0_
  8.2 0.3 %shard_map.94 = f32[80,128]{1,0:T(8,128)S(1)} custom-call(s32[80,128]{1,0:T(8,128)S(1)} %get-tuple-element.27.refs_0_, f32[160,128]{1,0:T(8,128)S(1)} %get-tuple-element.28.refs_0_.refs_1_, f32[80,128]{1,0:T(8,128)S(1)} %collective-permute-done.refs_2_.refs_0_), custom_call_target="tpu_custom_call" | custom-call | bytes 262144 | tf_op jit(solution)/shard_map/pallas_call | solution.py:324
  8.5 0.1 collective-permute-start.1
  8.6 1.6 %shard_map.95.refs_7_ = f32[3,512]{1,0:T(4,128)S(1)} custom-call(bf16[64,512]{1,0:T(8,128)(2,1)S(1)} %get-tuple-element.23.at_q.refs_0_, bf16[96,512]{1,0:T(8,128)(2,1)S(1)} %get-tuple-element.24.at_s.refs_1_, f32[8,512]{1,0:T(8,128)S(1)} %get-tuple-element.25.shifted.refs_2_, f32[8,128]{1,0:T(8,128)S(1)} %get-tuple-element.26.mid.refs_3_, ...), custom_call_target="tpu_custom_call" | custom-call | flops 26214400 | bytes 262144 | tf_op jit(solution)/shard_map/pallas_call | solution.py:324
  10.2 0.0 collective-permute-done.1.refs_3_.refs_0_
  10.3 0.4 %shard_map.96 = f32[80,128]{1,0:T(8,128)S(1)} custom-call(s32[80,128]{1,0:T(8,128)S(1)} %get-tuple-element.27.refs_0_, f32[160,128]{1,0:T(8,128)S(1)} %get-tuple-element.28.refs_0_.refs_1_, f32[80,128]{1,0:T(8,128)S(1)} %collective-permute-done.refs_2_.refs_0_, f32[80,128]{1,0:T(8,128)S(1)} %collective-permute-done.1.refs_3_.refs_0_), custom_call_target="tpu_custom_call" | custom-call | bytes 262144 | tf_op jit(solution)/shard_map/pallas_call | solution.py:324
  10.7 2.6 %collective-permute-start.2 = (f32[80,128]{1,0:T(8,128)S(1)}, f32[80,128]{1,0:T(8,128)S(1)}, u32[]{:S(2)}, u32[]{:S(2)}) collective-permute-start(f32[80,128]{1,0:T(8,128)S(1)} %shard_map.96), channel_id=1, source_target_pairs={{0,4},{1,5},{2,6},{3,7},{4,0},{5,1},{6,2},{7,3},{8,12},{9,13},{10,... | collective-permute-start | bytes 122888 | tf_op jit(solution)/shard_map/ppermute | solution.py:350
  13.3 1.6 %shard_map.97.refs_8_ = f32[3,512]{1,0:T(4,128)S(1)} custom-call(bf16[64,512]{1,0:T(8,128)(2,1)S(1)} %get-tuple-element.23.at_q.refs_0_, bf16[96,512]{1,0:T(8,128)(2,1)S(1)} %get-tuple-element.24.at_s.refs_1_, f32[8,512]{1,0:T(8,128)S(1)} %get-tuple-element.25.shifted.refs_2_, f32[8,128]{1,0:T(8,128)S(1)} %get-tuple-element.26.mid.refs_3_, ...), custom_call_target="tpu_custom_call" | custom-call | flops 26214400 | bytes 262144 | tf_op jit(solution)/shard_map/pallas_call | solution.py:324
  14.9 0.7 %collective-permute-done.2.refs_4_.refs_0_ = f32[80,128]{1,0:T(8,128)S(1)} collective-permute-done((f32[80,128]{1,0:T(8,128)S(1)}, f32[80,128]{1,0:T(8,128)S(1)}, u32[]{:S(2)}, u32[]{:S(2)}) %collective-permute-start.2) | collective-permute-done | bytes 40992 | tf_op jit(solution)/shard_map/ppermute | solution.py:350
  15.6 0.5 %shard_map.98 = f32[80,128]{1,0:T(8,128)S(1)} custom-call(s32[80,128]{1,0:T(8,128)S(1)} %get-tuple-element.27.refs_0_, f32[160,128]{1,0:T(8,128)S(1)} %get-tuple-element.28.refs_0_.refs_1_, f32[80,128]{1,0:T(8,128)S(1)} %collective-permute-done.refs_2_.refs_0_, f32[80,128]{1,0:T(8,128)S(1)} %collective-permute-done.1.refs_3_.refs_0_, ...), custom_call_target="tpu_custom_call" | custom-call | bytes 262144 | tf_op jit(solution)/shard_map/pallas_call | solution.py:324
  16.1 1.6 %collective-permute-start.3 = (f32[80,128]{1,0:T(8,128)S(1)}, f32[80,128]{1,0:T(8,128)S(1)}, u32[]{:S(2)}, u32[]{:S(2)}) collective-permute-start(f32[80,128]{1,0:T(8,128)S(1)} %shard_map.98), channel_id=1, source_target_pairs={{0,2},{1,3},{2,0},{3,1},{4,6},{5,7},{6,4},{7,5},{8,10},{9,11},{10,... | collective-permute-start | bytes 122888 | tf_op jit(solution)/shard_map/ppermute | solution.py:350
  17.8 1.6 %shard_map.99.refs_9_ = f32[3,512]{1,0:T(4,128)S(1)} custom-call(bf16[64,512]{1,0:T(8,128)(2,1)S(1)} %get-tuple-element.23.at_q.refs_0_, bf16[96,512]{1,0:T(8,128)(2,1)S(1)} %get-tuple-element.24.at_s.refs_1_, f32[8,512]{1,0:T(8,128)S(1)} %get-tuple-element.25.shifted.refs_2_, f32[8,128]{1,0:T(8,128)S(1)} %get-tuple-element.26.mid.refs_3_, ...), custom_call_target="tpu_custom_call" | custom-call | flops 26214400 | bytes 262144 | tf_op jit(solution)/shard_map/pallas_call | solution.py:324
  19.4 0.8 %collective-permute-done.3.refs_5_.refs_1_ = f32[80,128]{1,0:T(8,128)S(1)} collective-permute-done((f32[80,128]{1,0:T(8,128)S(1)}, f32[80,128]{1,0:T(8,128)S(1)}, u32[]{:S(2)}, u32[]{:S(2)}) %collective-permute-start.3) | collective-permute-done | bytes 40992 | tf_op jit(solution)/shard_map/ppermute | solution.py:350
  20.2 0.6 %shard_map.100 = f32[96,128]{1,0:T(8,128)S(1)} custom-call(s32[80,128]{1,0:T(8,128)S(1)} %get-tuple-element.27.refs_0_, f32[160,128]{1,0:T(8,128)S(1)} %get-tuple-element.28.refs_0_.refs_1_, f32[80,128]{1,0:T(8,128)S(1)} %collective-permute-done.refs_2_.refs_0_, f32[80,128]{1,0:T(8,128)S(1)} %collective-permute-done.1.refs_3_.refs_0_, ...), custom_call_target="tpu_custom_call" | custom-call | bytes 262144 | tf_op jit(solution)/shard_map/pallas_call | solution.py:324
  20.8 1.6 %collective-permute-start.4 = (f32[96,128]{1,0:T(8,128)S(1)}, f32[96,128]{1,0:T(8,128)S(1)}, u32[]{:S(2)}, u32[]{:S(2)}) collective-permute-start(f32[96,128]{1,0:T(8,128)S(1)} %shard_map.100), channel_id=1, source_target_pairs={{0,1},{1,0},{2,3},{3,2},{4,5},{5,4},{6,7},{7,6},{8,9},{9,8},{10,11... | collective-permute-start | bytes 147464 | tf_op jit(solution)/shard_map/ppermute | solution.py:350
  22.4 2.9 %shard_map.101.refs_10_ = f32[3,512]{1,0:T(4,128)S(1)} custom-call(bf16[64,512]{1,0:T(8,128)(2,1)S(1)} %get-tuple-element.23.at_q.refs_0_, bf16[96,512]{1,0:T(8,128)(2,1)S(1)} %get-tuple-element.24.at_s.refs_1_, f32[8,512]{1,0:T(8,128)S(1)} %get-tuple-element.25.shifted.refs_2_, f32[8,128]{1,0:T(8,128)S(1)} %get-tuple-element.26.mid.refs_3_, ...), custom_call_target="tpu_custom_call" | custom-call | flops 52428800 | bytes 262144 | tf_op jit(solution)/shard_map/pallas_call | solution.py:324
  25.3 0.0 collective-permute-done.4.refs_4_
  25.3 2.6 %shard_map.102 = f32[3,512]{1,0:T(4,128)} custom-call(bf16[64,512]{1,0:T(8,128)(2,1)S(1)} %get-tuple-element.23.at_q.refs_0_, bf16[96,512]{1,0:T(8,128)(2,1)S(1)} %get-tuple-element.24.at_s.refs_1_, f32[8,512]{1,0:T(8,128)S(1)} %get-tuple-element.25.shifted.refs_2_, f32[8,128]{1,0:T(8,128)S(1)} %get-tuple-element.26.mid.refs_3_, ...), custom_call_target="tpu_custom_call" | custom-call | flops 26214400 | bytes 262144 | tf_op jit(solution)/shard_map/pallas_call | solution.py:324
  (5 shorter events, 0.0 us)
Async XLA Ops:
  0.0 0.8 %copy-start = (f32[6,2048]{1,0:T(8,128)S(1)}, f32[6,2048]{1,0:T(8,128)}, u32[]{:S(2)}) copy-start(f32[6,2048]{1,0:T(8,128)} %quad.1) | copy-start | bytes 147460
  0.0 0.8 %copy-start.1 = (f32[3,2048]{1,0:T(4,128)S(1)}, f32[3,2048]{1,0:T(4,128)}, u32[]{:S(2)}) copy-start(f32[3,2048]{1,0:T(4,128)} %center.1) | copy-start | bytes 73732
  0.0 0.8 %copy-start.2 = (f32[2048]{0:T(1024)S(1)}, f32[2048]{0:T(1024)}, u32[]{:S(2)}) copy-start(f32[2048]{0:T(1024)} %param.11) | copy-start | bytes 24580
  0.8 3.6 %copy-start.3 = (f32[3,512]{1,0:T(4,128)S(1)}, f32[3,512]{1,0:T(4,128)}, u32[]{:S(2)}) copy-start(f32[3,512]{1,0:T(4,128)} %pos.1) | copy-start | bytes 18436
  1.4 3.0 %copy-start.4 = (f32[512]{0:T(512)S(1)}, f32[512]{0:T(512)}, u32[]{:S(2)}) copy-start(f32[512]{0:T(512)} %param.10) | copy-start | bytes 6148
  1.4 6.8 %collective-permute-start = (f32[80,128]{1,0:T(8,128)S(1)}, f32[80,128]{1,0:T(8,128)S(1)}, u32[]{:S(2)}, u32[]{:S(2)}) collective-permute-start(f32[80,128]{1,0:T(8,128)S(1)} %get-tuple-element.29), channel_id=1, source_target_pairs={{0,16},{1,17},{2,18},{3,19},{4,20},{5,21},{6,22},{7,23},{8,24},{9,... | collective-permute-start | bytes 122888 | tf_op jit(solution)/shard_map/ppermute | solution.py:350
  4.5 0.7 %copy-start.5 = (s32[1,2,4]{2,1,0:T(2,128)S(1)}, s32[1,2,4]{2,1,0:T(2,128)}, u32[]{:S(2)}) copy-start(s32[1,2,4]{2,1,0:T(2,128)} %param.16) | copy-start | bytes 100
  4.5 0.7 %copy-start.6 = (s32[1,2]{1,0:T(1,128)S(1)}, s32[1,2]{1,0:T(1,128)}, u32[]{:S(2)}) copy-start(s32[1,2]{1,0:T(1,128)} %counts.1) | copy-start | bytes 28
  8.5 1.7 %collective-permute-start.1 = (f32[80,128]{1,0:T(8,128)S(1)}, f32[80,128]{1,0:T(8,128)S(1)}, u32[]{:S(2)}, u32[]{:S(2)}) collective-permute-start(f32[80,128]{1,0:T(8,128)S(1)} %shard_map.94), channel_id=1, source_target_pairs={{0,8},{1,9},{2,10},{3,11},{4,12},{5,13},{6,14},{7,15},{8,0},{9,1},... | collective-permute-start | bytes 122888 | tf_op jit(solution)/shard_map/ppermute | solution.py:350
  10.7 5.0 %collective-permute-start.2 = (f32[80,128]{1,0:T(8,128)S(1)}, f32[80,128]{1,0:T(8,128)S(1)}, u32[]{:S(2)}, u32[]{:S(2)}) collective-permute-start(f32[80,128]{1,0:T(8,128)S(1)} %shard_map.96), channel_id=1, source_target_pairs={{0,4},{1,5},{2,6},{3,7},{4,0},{5,1},{6,2},{7,3},{8,12},{9,13},{10,... | collective-permute-start | bytes 122888 | tf_op jit(solution)/shard_map/ppermute | solution.py:350
  16.1 4.1 %collective-permute-start.3 = (f32[80,128]{1,0:T(8,128)S(1)}, f32[80,128]{1,0:T(8,128)S(1)}, u32[]{:S(2)}, u32[]{:S(2)}) collective-permute-start(f32[80,128]{1,0:T(8,128)S(1)} %shard_map.98), channel_id=1, source_target_pairs={{0,2},{1,3},{2,0},{3,1},{4,6},{5,7},{6,4},{7,5},{8,10},{9,11},{10,... | collective-permute-start | bytes 122888 | tf_op jit(solution)/shard_map/ppermute | solution.py:350
  20.8 4.5 %collective-permute-start.4 = (f32[96,128]{1,0:T(8,128)S(1)}, f32[96,128]{1,0:T(8,128)S(1)}, u32[]{:S(2)}, u32[]{:S(2)}) collective-permute-start(f32[96,128]{1,0:T(8,128)S(1)} %shard_map.100), channel_id=1, source_target_pairs={{0,1},{1,0},{2,3},{3,2},{4,5},{5,4},{6,7},{7,6},{8,9},{9,8},{10,11... | collective-permute-start | bytes 147464 | tf_op jit(solution)/shard_map/ppermute | solution.py:350

commit v3 on v2

v3 whole, which is shorter than its diff:
```python
import functools
import math

import jax
import jax.numpy as jnp
from jax import lax
from jax.experimental import pallas as pl
from jax.experimental.pallas import tpu as pltpu
from jax.sharding import PartitionSpec as P

AXES = ("gx", "gy", "gz")
LANES = 128
SUBS = 8
LIVE = 768
SOFT = 0.01
QROWS = 64
SROWS = 32
FROWS = 48
UNIT = 256
A_PART = (0, 0, 1, 1, 0, 2)
B_PART = (0, 1, 0, 1, 2, 0)

f32 = jnp.float32
bf16 = jnp.bfloat16
dot = functools.partial(jnp.dot, preferred_element_type=f32)


def split3(value):
    one = value.astype(bf16).astype(f32)
    rest = value - one
    two = rest.astype(bf16).astype(f32)
    three = (rest - two).astype(bf16).astype(f32)
    return one, two, three


def halves(value):
    high = value.astype(bf16)
    return high, (value - high.astype(f32)).astype(bf16)


def paired(values, parts):
    pieces = [split3(v) for v in values]
    return [p[k] for k in parts for p in pieces]


def quad_rows(mass, center, quad):
    cx, cy, cz = center
    qxx, qyy, qzz, qxy, qxz, qyz = quad
    vx = qxx * cx + qxy * cy + qxz * cz
    vy = qxy * cx + qyy * cy + qyz * cz
    vz = qxz * cx + qyz * cy + qzz * cz
    h = 2.5 / jnp.maximum(mass, 1e-3)
    linear = [-2.0 * h * vx, -2.0 * h * vy, -2.0 * h * vz]
    square = [h * qxx, h * qyy, h * qzz, 2.0 * h * qxy, 2.0 * h * qxz, 2.0 * h * qyz]
    rows = list(split3(h * (cx * vx + cy * vy + cz * vz)))
    rows += paired(linear + square, B_PART)
    rows += [jnp.zeros_like(mass)] * (QROWS - len(rows))
    return rows, (vx, vy, vz)


def dist_rows(mass, center):
    cx, cy, cz = center
    rows = list(split3(cx * cx + cy * cy + cz * cz + SOFT))
    rows += paired([-2.0 * cx, -2.0 * cy, -2.0 * cz], B_PART)
    rows += [jnp.ones_like(mass)] * 3
    rows += [jnp.zeros_like(mass)] * (SROWS - len(rows))
    return rows


def mass_rows(mass, center):
    cx, cy, cz = center
    rows = paired([mass, mass * cx, mass * cy, mass * cz], (0, 1, 2))
    return rows + [jnp.zeros_like(mass)] * (16 - len(rows))


def moment_rows(quad, v):
    rows = paired(list(quad) + list(v), (0, 1, 2))
    return rows + [jnp.zeros_like(v[0])] * (32 - len(rows))


def target_rows(x, y, z):
    one = jnp.ones_like(x)
    zero = jnp.zeros_like(x)
    q = [one] * 3 + paired([x, y, z, x * x, y * y, z * z, x * y, x * z, y * z], A_PART)
    q += [zero] * (QROWS - len(q))
    s = [one] * 3 + paired([x, y, z], A_PART) + list(split3(x * x + y * y + z * z))
    s += [zero] * (SROWS - len(s))
    return q, s


def stage_rows(feat, rows, sub):
    for k, value in enumerate(rows):
        feat[k * sub : (k + 1) * sub, :] = value


def cell_features(read, sub, feat, lhs, fw, fu, base):
    mass, center, quad = read
    q, v = quad_rows(mass, center, quad)
    rows = q + dist_rows(mass, center) + mass_rows(mass, center) + moment_rows(quad, v)
    stage_rows(feat, rows, sub)
    wide = QROWS + SROWS
    for r in range(sub):
        at = slice(base + r * LANES, base + (r + 1) * LANES)
        left = feat[pl.ds(r, wide, stride=sub), :]
        lhs[at, 0:wide] = left.T.astype(bf16)
        right = feat[pl.ds(wide * sub + r, FROWS, stride=sub), :]
        fw[:, at] = right[0:16].astype(bf16)
        fu[:, at] = right[16:FROWS].astype(bf16)


def body_features(mass, center, sub, feat, lhs, fw, base):
    rows = dist_rows(mass, center) + mass_rows(mass, center)
    stage_rows(feat, rows, sub)
    for r in range(sub):
        at = slice(base + r * LANES, base + (r + 1) * LANES)
        left = feat[pl.ds(r, SROWS, stride=sub), :]
        lhs[at, 0:SROWS] = left.T.astype(bf16)
        right = feat[pl.ds(SROWS * sub + r, 16, stride=sub), :]
        fw[:, at] = right.astype(bf16)


def twice(left, high, low):
    return dot(jnp.concatenate([left, left], 1), jnp.concatenate([high, low], 0))


def pair_sums(cells, bodies, at_q, at_s, lhs, fw, fu, blhs, bfw, aw, au):
    targets = at_q.shape[1]
    wide = math.gcd(targets, UNIT)
    units = []
    for count, is_cell in ((cells, True), (bodies, False)):
        deep = math.gcd(count, UNIT) if count else 1
        for b in range(count // deep):
            for t in range(targets // wide):
                units.append((slice(b * deep, (b + 1) * deep), slice(t * wide, (t + 1) * wide), is_cell))
    aw[...] = jnp.zeros_like(aw)
    au[...] = jnp.zeros_like(au)

    def first(src, tgt, is_cell):
        if not is_cell:
            return dot(blhs[src, 0:SROWS], at_s[QROWS : QROWS + SROWS, tgt]), None
        s = dot(lhs[src, 0 : QROWS + SROWS], at_s[:, tgt])
        return s, dot(lhs[src, 0:QROWS], at_q[:, tgt])

    def second(src, tgt, is_cell, s, q):
        y = lax.rsqrt(s)
        y2 = y * y
        y3 = y * y2
        if not is_cell:
            aw[:, tgt] += twice(bfw[:, src], *halves(y3))
            return
        y5 = y3 * y2
        w = y3 + (q * y2) * y5
        aw[:, tgt] += twice(fw[:, src], *halves(w))
        au[:, tgt] += twice(fu[:, src], *halves(y5))

    ready = first(*units[0])
    for k, unit in enumerate(units):
        coming = first(*units[k + 1]) if k + 1 < len(units) else None
        second(*unit, *ready)
        ready = coming


def from_sums(x, y, z, aw, au):
    w = aw[0:4, :] + aw[4:8, :] + aw[8:12, :]
    u = au[0:9, :] + au[9:18, :] + au[18:27, :]

    def g(k):
        return u[k : k + 1, :]

    return (
        g(0) * x + g(3) * y + g(4) * z - g(6) - (w[0:1] * x - w[1:2]),
        g(3) * x + g(1) * y + g(5) * z - g(7) - (w[0:1] * y - w[2:3]),
        g(4) * x + g(5) * y + g(2) * z - g(8) - (w[0:1] * z - w[3:4]),
    )


def slot_place(lists, masks, level):
    slots = lists.shape[2] // LANES
    rows, lanes = [], []
    for r in range(slots):
        at = slice(r * LANES, (r + 1) * LANES)
        index = lists[0, level : level + 1, at]
        rows.append(jnp.where(masks[0, level : level + 1, at] > 0, index >> 7, -1))
        lanes.append(index & (LANES - 1))
    return jnp.concatenate(rows, 0), jnp.concatenate(lanes, 0)


def picked(row, lane, lines, base, count, out):
    out = list(out)
    for k in range(count):
        hit = row == base + k
        for f in range(10):
            line = jnp.broadcast_to(lines(f, k), row.shape)
            got = jnp.take_along_axis(line, lane, axis=1, mode="promise_in_bounds")
            out[f] = jnp.where(hit, got, out[f])
    return out


def table_lines(table):
    rows = table.shape[0] // 10

    def line(f, k):
        return table[f * rows + k : f * rows + k + 1, :]

    return rows, line


def picked_tables(row, lane, tables):
    out = [jnp.zeros(row.shape, f32)] * 10
    base = 0
    for table in tables:
        rows, line = table_lines(table)
        out = picked(row, lane, line, base, rows, out)
        base += rows
    return out


def store_rows(to, values, count):
    for f, value in enumerate(values):
        to[f * count : (f + 1) * count, :] = value[0:count, :]


def open_kernel(mass, center, quad, lists, masks, pos, weight, faces, counts, pick):
    row, lane = slot_place(lists, masks, 0)

    def line(f, k):
        at = slice(k * LANES, (k + 1) * LANES)
        if f == 0:
            return mass[k : k + 1, :]
        return center[f - 1 : f, at] if f < 4 else quad[f - 4 : f - 3, at]

    zeros = [jnp.zeros(row.shape, f32)] * 10
    store_rows(pick, picked(row, lane, line, 0, mass.shape[0], zeros), row.shape[0])


def packed(row, lane):
    subs = row.shape[0]
    live = row >= 0
    at_row = lax.broadcasted_iota(jnp.int32, row.shape, 0)
    at_lane = lax.broadcasted_iota(jnp.int32, row.shape, 1)
    upper = lax.broadcasted_iota(jnp.int32, (LANES, LANES), 0) < lax.broadcasted_iota(jnp.int32, (LANES, LANES), 1)
    dead = jnp.where(live, 0.0, 1.0).astype(bf16)
    before = dot(dead, jnp.where(upper, 1.0, 0.0).astype(bf16))
    whole = dot(dead, jnp.ones((LANES, LANES), bf16))
    run = whole
    step = 1
    while step < subs:
        run = run + jnp.where(at_row >= step, pltpu.roll(run, step, axis=0), 0.0)
        step *= 2
    move = (before + run - whole).astype(jnp.int32)
    word = jnp.where(live, (((move + subs * LANES) << 6) + row << 7) + lane, 0)
    step = 1
    shift = 13
    while step < subs * LANES:
        if step < LANES:
            turned = pltpu.roll(word, LANES - step, axis=1)
            come = jnp.where(at_lane < LANES - step, turned, pltpu.roll(turned, subs - 1, axis=0))
        else:
            come = pltpu.roll(word, subs - step // LANES, axis=0)
        stay = jnp.where((word >> shift) & 1 == 0, word, 0)
        word = jnp.where((come >> shift) & 1 == 1, come, stay)
        step *= 2
        shift += 1
    return jnp.where(word > 0, (word >> 7) & 63, -1), word & (LANES - 1)


def read_cells(table, first, count, mid):
    rows, unused = table_lines(table)

    def row(f):
        return table[f * rows + first : f * rows + first + count, :]

    center = [row(1 + k) - mid[k : k + 1, :] for k in range(3)]
    return row(0), center, [row(4 + k) for k in range(6)]


def read_bodies(table, mid):
    blocks = table.shape[0] // 4
    center = [table[(1 + k) * blocks : (2 + k) * blocks, :] - mid[k : k + 1, :] for k in range(3)]
    return table[0:blocks, :], center, blocks


def span_features(spans, mid, feat, lhs, fw, fu):
    base = 0
    for table, first, count in spans:
        done = 0
        while done < count:
            sub = min(SUBS, count - done)
            cell_features(read_cells(table, first + done, sub, mid), sub, feat, lhs, fw, fu, base)
            base += sub * LANES
            done += sub
    return base


def store_sums(out, shifted, aw, au, parts=()):
    total = list(from_sums(shifted[0:1], shifted[1:2], shifted[2:3], aw, au))
    for part in parts:
        total = [t + part[k : k + 1, :] for k, t in enumerate(total)]
    for k in range(3):
        out[k : k + 1, :] = total[k]


def start_kernel(
    one_side, some, mass, center, quad, lists, masks, pos, weight, faces, counts,
    own, place, part, at_q, at_s, shifted, mid, face, out,
    tab, bod, feat, lhs, fw, fu, blhs, bfw, aw, au,
):
    levels = lists.shape[1]
    slots = lists.shape[2] // LANES
    for level in range(levels):
        row, lane = slot_place(lists, masks, level)
        if level == levels - 1:
            row, lane = packed(row, lane)
        place[2 * level * slots : (2 * level + 1) * slots, :] = row
        place[(2 * level + 1) * slots : (2 * level + 2) * slots, :] = lane
    rows = mass.shape[0]
    for k in range(rows):
        at = slice(k * LANES, (k + 1) * LANES)
        tab[k * 16 : k * 16 + 1, :] = mass[k : k + 1, :]
        tab[k * 16 + 1 : k * 16 + 4, :] = center[:, at]
        tab[k * 16 + 4 : k * 16 + 10, :] = quad[:, at]
    for f in range(10):
        own[f * rows : (f + 1) * rows, :] = tab[pl.ds(f, rows, stride=16), :]

    targets = pos.shape[1]
    blocks = targets // LANES
    low = jnp.min(pos[...], axis=1, keepdims=True)
    high = jnp.max(pos[...], axis=1, keepdims=True)
    middle = jnp.broadcast_to(0.5 * (low + high), (3, LANES))
    mid[0:3, :] = middle
    bod[0:blocks, :] = weight[...]
    for k in range(blocks):
        at = slice(k * LANES, (k + 1) * LANES)
        here = pos[:, at]
        bod[pl.ds(blocks + k, 3, stride=blocks), :] = here
        shifted[0:3, at] = here - middle
    own_mass, own_center, unused = read_bodies(bod, mid)
    q, s = target_rows(*own_center)
    stage_rows(feat, q + s, blocks)
    for k in range(blocks):
        at = slice(k * LANES, (k + 1) * LANES)
        rows_here = feat[pl.ds(k, QROWS + SROWS, stride=blocks), :]
        at_q[:, at] = rows_here[0:QROWS].astype(bf16)
        at_s[0:QROWS, at] = jnp.zeros((QROWS, LANES), bf16)
        at_s[QROWS : QROWS + SROWS, at] = rows_here[QROWS : QROWS + SROWS].astype(bf16)
    body_features(own_mass, own_center, blocks, feat, blhs, bfw, 0)
    span_features([(own, 0, some)], mid, feat, lhs, fw, fu)

    lower = lax.axis_index("gz") > 0
    for k in range(1 if one_side else 2):
        order = jnp.where(lower, faces[0:1, :], faces[1:2, :]) if one_side else faces[k : k + 1, :]
        many = jnp.where(lower, counts[:, 0:1], counts[:, 1:2]) if one_side else counts[:, k : k + 1]
        for j in range(blocks):
            take = jnp.where(j < many, order[:, j : j + 1], -1)
            got = jnp.zeros((4, LANES), f32)
            for b in range(blocks):
                got = jnp.where(take == b, bod[pl.ds(b, 4, stride=blocks), :], got)
            face[pl.ds(k * 4 * blocks + j, 4, stride=blocks), :] = got
    row, lane = place[2 * slots : 3 * slots, :], place[3 * slots : 4 * slots, :]
    store_rows(part, picked_tables(row, lane, [own]), slots)
    pair_sums(some * LANES, targets, at_q, at_s, lhs, fw, fu, blhs, bfw, aw, au)
    store_sums(out, shifted, aw, au)


def window_kernel(spans, ahead, count, at_q, at_s, shifted, mid, place, *refs):
    tables = refs[:count]
    if ahead:
        out, part, feat, lhs, fw, fu, aw, au = refs[count:]
        level, ids = ahead
        row = place[2 * level * SUBS : (2 * level + 1) * SUBS, :]
        lane = place[(2 * level + 1) * SUBS : (2 * level + 2) * SUBS, :]
        store_rows(part, picked_tables(row, lane, [tables[k] for k in ids]), SUBS)
    else:
        out, feat, lhs, fw, fu, aw, au = refs[count:]
    base = span_features([(tables[k], first, many) for k, first, many in spans], mid, feat, lhs, fw, fu)
    pair_sums(base, 0, at_q, at_s, lhs, fw, fu, None, None, aw, au)
    store_sums(out, shifted, aw, au)


def pick_kernel(level, base, live, faces, place, part, table, *refs):
    pick = refs[-1]
    row = place[2 * level * SUBS : (2 * level + 1) * SUBS, :]
    lane = place[(2 * level + 1) * SUBS : (2 * level + 2) * SUBS, :]
    rows, line = table_lines(table)
    out = [part[f * SUBS : (f + 1) * SUBS, :] for f in range(10)]
    store_rows(pick, picked(row, lane, line, base, rows, out), live)
    if faces:
        pick[10 * live :, :] = refs[0][...]


def last_kernel(merged, faces, parts, live, *refs):
    at_q, at_s, shifted, mid, table = refs[:5]
    sides = list(refs[5 : 5 + faces])
    sums = refs[5 + faces : 5 + faces + parts]
    out, feat, lhs, fw, fu, blhs, bfw, aw, au = refs[5 + faces + parts :]
    if merged:
        sides.append(table.at[10 * live :])
        table = table.at[: 10 * live]
    base = 0
    for side in sides:
        mass, center, blocks = read_bodies(side, mid)
        body_features(mass, center, blocks, feat, blhs, bfw, base)
        base += blocks * LANES
    count = span_features([(table, 0, live)], mid, feat, lhs, fw, fu)
    pair_sums(count, base, at_q, at_s, lhs, fw, fu, blhs, bfw, aw, au)
    store_sums(out, shifted, aw, au, sums)


def call(kernel, out_shape, args, scratch=(), in_specs=None, flops=0):
    specs = in_specs or [pl.BlockSpec(memory_space=pltpu.VMEM)] * len(args)
    many = isinstance(out_shape, (list, tuple))
    vmem = pl.BlockSpec(memory_space=pltpu.VMEM)
    return pl.pallas_call(
        kernel,
        out_shape=out_shape,
        in_specs=specs,
        out_specs=[vmem] * len(out_shape) if many else vmem,
        scratch_shapes=list(scratch),
        compiler_params=pltpu.CompilerParams(vmem_limit_bytes=32 * 2**20),
        cost_estimate=pl.CostEstimate(flops=flops, bytes_accessed=2**18, transcendentals=0),
    )(*args)


def shaped(*shape, dtype=f32):
    return jax.ShapeDtypeStruct(shape, dtype)


def sum_scratch(targets, cells, bodies):
    got = [pltpu.VMEM(((QROWS + SROWS + FROWS) * SUBS, LANES), f32)]
    if cells:
        got += [pltpu.VMEM((cells, LANES), bf16), pltpu.VMEM((16, cells), bf16), pltpu.VMEM((32, cells), bf16)]
    if bodies:
        got += [pltpu.VMEM((bodies, LANES), bf16), pltpu.VMEM((16, bodies), bf16)]
    return got + [pltpu.VMEM((16, targets), f32), pltpu.VMEM((32, targets), f32)]


def swapped(value, apart):
    mask = 2**apart
    return lax.ppermute(value, AXES, [(k, k ^ mask) for k in range(lax.axis_size(AXES))])


def shards(body_pos, body_mass, cell_mass, cell_center, cell_quad, cell_lists, slot_masks, face_lists, face_counts):
    bits = lax.axis_size(AXES).bit_length() - 1
    levels, slots = cell_lists.shape[1:]
    targets = body_mass.shape[0]
    blocks = targets // LANES
    rows = cell_mass.shape[0] // LANES
    wide = slots // LANES
    live = LIVE // LANES
    near_by = lax.axis_size("gz")
    merged = near_by == 2 and bits == levels
    given = [cell_mass.reshape(rows, LANES), cell_center, cell_quad, cell_lists, slot_masks]
    given += [body_pos, body_mass.reshape(blocks, LANES), face_lists[0], face_counts]
    pick = call(open_kernel, shaped(10 * wide, LANES), given)
    arrived = swapped(pick, bits - 1)

    some = rows // 4
    own, place, part, at_q, at_s, shifted, mid, face, near = call(
        functools.partial(start_kernel, merged, some),
        [
            shaped(10 * rows, LANES),
            shaped(2 * levels * wide, LANES, dtype=jnp.int32),
            shaped(10 * wide, LANES),
            shaped(QROWS, targets, dtype=bf16),
            shaped(QROWS + SROWS, targets, dtype=bf16),
            shaped(SUBS, targets),
            shaped(SUBS, LANES),
            shaped((1 if merged else 2) * 4 * blocks, LANES),
            shaped(3, targets),
        ],
        given,
        [pltpu.VMEM((16 * rows, LANES), f32), pltpu.VMEM((4 * blocks, LANES), f32)]
        + sum_scratch(targets, some * LANES, targets),
        flops=targets * (some * LANES * 50 + targets * 20),
    )
    common = [at_q, at_s, shifted, mid]

    def window(spans, ahead):
        tables = []
        for table, first, many in spans:
            if not any(table is known for known in tables):
                tables.append(table)
        if ahead:
            tables += [t for t in ahead[1] if not any(t is known for known in tables)]

        def place_of(table):
            return [table is known for known in tables].index(True)

        count = sum(many for table, first, many in spans) * LANES
        kernel = functools.partial(
            window_kernel,
            [(place_of(table), first, many) for table, first, many in spans],
            (ahead[0], [place_of(t) for t in ahead[1]]) if ahead else None,
            len(tables),
        )
        outs = [shaped(3, targets)] + ([shaped(10 * wide, LANES)] if ahead else [])
        scratch = sum_scratch(targets, count, 0)
        got = call(kernel, outs, common + [place] + tables, scratch, flops=targets * count * 50)
        return got

    sides = []
    if not merged:
        lower, upper = face[: 4 * blocks], face[4 * blocks :]
        sides = [
            lax.ppermute(upper, "gz", [(k, k + 1) for k in range(near_by - 1)]),
            lax.ppermute(lower, "gz", [(k + 1, k) for k in range(near_by - 1)]),
        ]
    tables = [own]
    sums = []
    tied = [near, part]
    for level in range(1, levels):
        arrived, total, part = lax.optimization_barrier((arrived, *tied))
        sums.append(total)
        last = level == levels - 1
        extra = [face] if merged and last else []
        many = live if last else wide
        base = rows + (level - 1) * wide
        pick = call(
            functools.partial(pick_kernel, level, base, many, len(extra)),
            shaped(10 * many + len(extra) * 4 * blocks, LANES),
            [place, part, arrived] + extra,
        )
        tables.append(arrived)
        arrived = swapped(pick, bits - 1 - level)
        if level == 1:
            spans = [(own, some, some)]
        elif level == 2:
            spans = [(own, 2 * some, rows - 2 * some)]
        elif level == 3:
            spans = [(tables[1], 0, wide), (tables[2], 0, wide)]
        else:
            spans = [(t, 0, wide) for t in tables[3:]]
        tied = window(spans, None if last else (level + 1, list(tables)))
    sums += tied
    return call(
        functools.partial(last_kernel, merged, len(sides), len(sums), live),
        shaped(3, targets),
        common + [arrived] + sides + sums,
        sum_scratch(targets, live * LANES, targets * (len(sides) + merged)),
        flops=targets * LIVE * 50,
    )


def solution(mesh):
    in_specs = (
        P(None, AXES),
        P(AXES),
        P(AXES),
        P(None, AXES),
        P(None, AXES),
        P(AXES, None, None),
        P(AXES, None, None),
        P(AXES, None, None),
        P(AXES, None),
    )
    out_specs = P(None, AXES)
    return jax.shard_map(shards, mesh=mesh, in_specs=in_specs, out_specs=out_specs, check_vma=False)
```

time: 28.1 us -> 27.3 us (0.972)
  Pallas kernels: 15.8 us -> 13.4 us
  local copies, waits for them, and re-layouts: 1.52 us -> 2.87 us
  starting transfers between devices: 8.96 us -> 9.73 us
  waiting for transfers between devices: 1.5 us -> 0.93 us
    pallas_call x12 -> x11, Pallas kernels: 15.8 us -> 13.4 us  [call(): pl.pallas_call(kernel, out_shape=out_shape, in_specs=specs, out_specs=[vm...]
    unnamed x15 -> x16, local copies, waits for them, and re-layouts: 1.52 us -> 2.87 us
    ppermute x5, starting transfers between devices: 8.96 us -> 9.73 us  [swapped(): lax.ppermute(value, AXES, [(k, k ^ mask) for k in range(lax.axis_size(AXE...]
    ppermute x5, waiting for transfers between devices: 1.5 us -> 0.93 us  [swapped(): lax.ppermute(value, AXES, [(k, k ^ mask) for k in range(lax.axis_size(AXE...]
  transfers between devices with their start and end apart: 5 -> 5, of which waited for: 2 -> 3; matrix products, arithmetic and copies ran while one was open for 0% -> 0% of each run, Pallas kernels for 39% -> 38%
where the time goes in v3:
time: 27.3 us; the launch traced here: 27.1 us
  Pallas kernels  13.4 us (49%)
  starting transfers between devices  9.73 us (36%)
  local copies, waits for them, and re-layouts  2.87 us (11%)
  waiting for transfers between devices  0.93 us (3%)
    pallas_call x11, Pallas kernels, call(): pl.pallas_call(kernel, out_shape=out_shape, in_specs=specs, out_specs=[vm...  13.4 us
    ppermute x5, starting transfers between devices, swapped(): lax.ppermute(value, AXES, [(k, k ^ mask) for k in range(lax.axis_size(AXE...  9.73 us
    unnamed x16, local copies, waits for them, and re-layouts  2.87 us
    ppermute x5, waiting for transfers between devices, swapped(): lax.ppermute(value, AXES, [(k, k ^ mask) for k in range(lax.axis_size(AXE...  0.93 us
  transfers between devices with their start and end apart: 5, of which 3 were waited for; matrix products, arithmetic and copies ran while one was open for 0% of the time, Pallas kernels for 38%

profile of v3, /device:TPU:0, one launch (start us, length us, event | category | flops | bytes accessed | tf_op | source)
XLA Modules:
  0.0 27.1 jit_solution(306070511483506952)
XLA Ops:
  0.0 0.8 %copy.10.lists = s32[1,5,1024]{2,1,0:T(8,128)S(1)} copy(s32[1,5,1024]{2,0,1:T(1,128)} %param.14) | data formatting | bytes 40960 | tf_op args[5]
  0.8 0.0 copy-start.2
  0.8 0.7 %copy.11.masks = s32[1,5,1024]{2,1,0:T(8,128)S(1)} copy(s32[1,5,1024]{2,0,1:T(1,128)} %param.15) | data formatting | bytes 40960 | tf_op args[6]
  1.5 0.0 copy-start.5
  1.6 0.0 copy-start.6
  1.6 0.0 copy-done
  1.6 0.0 copy-done.1
  1.6 0.0 copy-done.2
  1.6 0.6 %copy-done.4 = f32[512]{0:T(512)S(1)} copy-done((f32[512]{0:T(512)S(1)}, f32[512]{0:T(512)}, u32[]{:S(2)}) %copy-start.4) | copy-done | bytes 2072
  2.2 0.0 copy-done.5
  2.2 0.7 %copy-done.3 = f32[3,512]{1,0:T(4,128)S(1)} copy-done((f32[3,512]{1,0:T(4,128)S(1)}, f32[3,512]{1,0:T(4,128)}, u32[]{:S(2)}) %copy-start.3) | copy-done | bytes 6168
  2.9 0.2 shard_map.92
  3.2 3.0 %collective-permute-start = (f32[80,128]{1,0:T(8,128)S(1)}, f32[80,128]{1,0:T(8,128)S(1)}, u32[]{:S(2)}, u32[]{:S(2)}) collective-permute-start(f32[80,128]{1,0:T(8,128)S(1)} %shard_map.92), channel_id=1, source_target_pairs={{0,16},{1,17},{2,18},{3,19},{4,20},{5,21},{6,22},{7,23},{8,24},{9,... | collective-permute-start | bytes 122888 | tf_op jit(solution)/shard_map/ppermute | solution.py:439
  6.2 1.6 %shard_map.91 = (f32[160,128]{1,0:T(8,128)S(1)}, s32[80,128]{1,0:T(8,128)S(1)}, f32[80,128]{1,0:T(8,128)S(1)}, bf16[64,512]{1,0:T(8,128)(2,1)S(1)}, bf16[96,512]...) custom-call(f32[16,128]{1,0:T(8,128)S(1)} %bitcast.4, ...), custom_call_target="tpu_custom_call" | custom-call | flops 18350080 | bytes 262144 | tf_op jit(solution)/shard_map/pallas_call | solution.py:413
  7.8 0.4 %collective-permute-done.table.refs_1_.refs_0_ = f32[80,128]{1,0:T(8,128)S(1)} collective-permute-done((f32[80,128]{1,0:T(8,128)S(1)}, f32[80,128]{1,0:T(8,128)S(1)}, u32[]{:S(2)}, u32[]{:S(2)}) %collective-permute-start) | collective-permute-done | bytes 40992 | tf_op jit(solution)/shard_map/ppermute | solution.py:439
  8.2 0.1 shard_map.93
  8.3 0.1 collective-permute-start.1
  8.4 1.1 %shard_map.94 = (f32[3,512]{1,0:T(4,128)S(1)}, f32[80,128]{1,0:T(8,128)S(1)}) custom-call(bf16[64,512]{1,0:T(8,128)(2,1)S(1)} %get-tuple-element.32.at_q.refs_0_, bf16[96,512]{1,0:T(8,128)(2,1)S(1)} %get-tuple-element.33.at_s.refs_1_, f32[8,512]{1,0:T(8,128)S(1)} %get-tuple-element.34.shifted.refs_2_, f32[8,128]{1,0:T(8,128)S(1)} %get-tuple-element.35.mid.refs_3_, ...), custom_call_target="tpu_custom_call" | custom-call | flops 13107200 | bytes 262144 | tf_op jit(solution)/shard_map/pallas_call | solution.py:413
  9.5 0.1 collective-permute-done.1.table.refs_2_.refs_1_
  9.6 0.1 shard_map.95
  9.8 3.2 %collective-permute-start.2 = (f32[80,128]{1,0:T(8,128)S(1)}, f32[80,128]{1,0:T(8,128)S(1)}, u32[]{:S(2)}, u32[]{:S(2)}) collective-permute-start(f32[80,128]{1,0:T(8,128)S(1)} %shard_map.95), channel_id=1, source_target_pairs={{0,4},{1,5},{2,6},{3,7},{4,0},{5,1},{6,2},{7,3},{8,12},{9,13},{10,... | collective-permute-start | bytes 122888 | tf_op jit(solution)/shard_map/ppermute | solution.py:439
  13.0 1.7 %shard_map.96 = (f32[3,512]{1,0:T(4,128)S(1)}, f32[80,128]{1,0:T(8,128)S(1)}) custom-call(bf16[64,512]{1,0:T(8,128)(2,1)S(1)} %get-tuple-element.32.at_q.refs_0_, bf16[96,512]{1,0:T(8,128)(2,1)S(1)} %get-tuple-element.33.at_s.refs_1_, f32[8,512]{1,0:T(8,128)S(1)} %get-tuple-element.34.shifted.refs_2_, f32[8,128]{1,0:T(8,128)S(1)} %get-tuple-element.35.mid.refs_3_, ...), custom_call_target="tpu_custom_call" | custom-call | flops 26214400 | bytes 262144 | tf_op jit(solution)/shard_map/pallas_call | solution.py:413
  14.7 0.4 %collective-permute-done.2.table.refs_3_.refs_0_ = f32[80,128]{1,0:T(8,128)S(1)} collective-permute-done((f32[80,128]{1,0:T(8,128)S(1)}, f32[80,128]{1,0:T(8,128)S(1)}, u32[]{:S(2)}, u32[]{:S(2)}) %collective-permute-start.2) | collective-permute-done | bytes 40992 | tf_op jit(solution)/shard_map/ppermute | solution.py:439
  15.0 0.1 shard_map.97
  15.2 1.9 %collective-permute-start.3 = (f32[80,128]{1,0:T(8,128)S(1)}, f32[80,128]{1,0:T(8,128)S(1)}, u32[]{:S(2)}, u32[]{:S(2)}) collective-permute-start(f32[80,128]{1,0:T(8,128)S(1)} %shard_map.97), channel_id=1, source_target_pairs={{0,2},{1,3},{2,0},{3,1},{4,6},{5,7},{6,4},{7,5},{8,10},{9,11},{10,... | collective-permute-start | bytes 122888 | tf_op jit(solution)/shard_map/ppermute | solution.py:439
  17.1 3.0 %shard_map.98 = (f32[3,512]{1,0:T(4,128)S(1)}, f32[80,128]{1,0:T(8,128)S(1)}) custom-call(bf16[64,512]{1,0:T(8,128)(2,1)S(1)} %get-tuple-element.32.at_q.refs_0_, bf16[96,512]{1,0:T(8,128)(2,1)S(1)} %get-tuple-element.33.at_s.refs_1_, f32[8,512]{1,0:T(8,128)S(1)} %get-tuple-element.34.shifted.refs_2_, f32[8,128]{1,0:T(8,128)S(1)} %get-tuple-element.35.mid.refs_3_, ...), custom_call_target="tpu_custom_call" | custom-call | flops 52428800 | bytes 262144 | tf_op jit(solution)/shard_map/pallas_call | solution.py:413
  20.1 0.0 collective-permute-done.3.table.refs_1_
  20.1 0.1 shard_map.99
  20.2 1.6 %collective-permute-start.4 = (f32[76,128]{1,0:T(8,128)S(1)}, f32[76,128]{1,0:T(8,128)S(1)}, u32[]{:S(2)}, u32[]{:S(2)}) collective-permute-start(f32[76,128]{1,0:T(8,128)S(1)} %shard_map.99), channel_id=1, source_target_pairs={{0,1},{1,0},{2,3},{3,2},{4,5},{5,4},{6,7},{7,6},{8,9},{9,8},{10,11... | collective-permute-start | bytes 116744 | tf_op jit(solution)/shard_map/ppermute | solution.py:439
  21.8 2.9 %shard_map.100.refs_9_ = f32[3,512]{1,0:T(4,128)S(1)} custom-call(bf16[64,512]{1,0:T(8,128)(2,1)S(1)} %get-tuple-element.32.at_q.refs_0_, bf16[96,512]{1,0:T(8,128)(2,1)S(1)} %get-tuple-element.33.at_s.refs_1_, f32[8,512]{1,0:T(8,128)S(1)} %get-tuple-element.34.shifted.refs_2_, f32[8,128]{1,0:T(8,128)S(1)} %get-tuple-element.35.mid.refs_3_, ...), custom_call_target="tpu_custom_call" | custom-call | flops 52428800 | bytes 262144 | tf_op jit(solution)/shard_map/pallas_call | solution.py:413
  24.7 0.0 collective-permute-done.4.refs_4_
  24.7 2.3 %shard_map.101 = f32[3,512]{1,0:T(4,128)} custom-call(bf16[64,512]{1,0:T(8,128)(2,1)S(1)} %get-tuple-element.32.at_q.refs_0_, bf16[96,512]{1,0:T(8,128)(2,1)S(1)} %get-tuple-element.33.at_s.refs_1_, f32[8,512]{1,0:T(8,128)S(1)} %get-tuple-element.34.shifted.refs_2_, f32[8,128]{1,0:T(8,128)S(1)} %get-tuple-element.35.mid.refs_3_, ...), custom_call_target="tpu_custom_call" | custom-call | flops 19660800 | bytes 262144 | tf_op jit(solution)/shard_map/pallas_call | solution.py:413
  (5 shorter events, 0.0 us)
Async XLA Ops:
  0.0 1.6 %copy-start = (f32[6,2048]{1,0:T(8,128)S(1)}, f32[6,2048]{1,0:T(8,128)}, u32[]{:S(2)}) copy-start(f32[6,2048]{1,0:T(8,128)} %quad.3) | copy-start | bytes 147460
  0.8 0.8 %copy-start.1 = (f32[3,2048]{1,0:T(4,128)S(1)}, f32[3,2048]{1,0:T(4,128)}, u32[]{:S(2)}) copy-start(f32[3,2048]{1,0:T(4,128)} %center.3) | copy-start | bytes 73732
  0.8 0.8 %copy-start.2 = (f32[2048]{0:T(1024)S(1)}, f32[2048]{0:T(1024)}, u32[]{:S(2)}) copy-start(f32[2048]{0:T(1024)} %param.11) | copy-start | bytes 24580
  1.5 0.7 %copy-start.4 = (f32[512]{0:T(512)S(1)}, f32[512]{0:T(512)}, u32[]{:S(2)}) copy-start(f32[512]{0:T(512)} %param.10) | copy-start | bytes 6148
  1.5 0.7 %copy-start.5 = (s32[1,2,4]{2,1,0:T(2,128)S(1)}, s32[1,2,4]{2,1,0:T(2,128)}, u32[]{:S(2)}) copy-start(s32[1,2,4]{2,1,0:T(2,128)} %param.16) | copy-start | bytes 100
  1.6 0.7 %copy-start.6 = (s32[1,2]{1,0:T(1,128)S(1)}, s32[1,2]{1,0:T(1,128)}, u32[]{:S(2)}) copy-start(s32[1,2]{1,0:T(1,128)} %counts.3) | copy-start | bytes 28
  2.2 0.7 %copy-start.3 = (f32[3,512]{1,0:T(4,128)S(1)}, f32[3,512]{1,0:T(4,128)}, u32[]{:S(2)}) copy-start(f32[3,512]{1,0:T(4,128)} %pos.3) | copy-start | bytes 18436
  3.2 5.0 %collective-permute-start = (f32[80,128]{1,0:T(8,128)S(1)}, f32[80,128]{1,0:T(8,128)S(1)}, u32[]{:S(2)}, u32[]{:S(2)}) collective-permute-start(f32[80,128]{1,0:T(8,128)S(1)} %shard_map.92), channel_id=1, source_target_pairs={{0,16},{1,17},{2,18},{3,19},{4,20},{5,21},{6,22},{7,23},{8,24},{9,... | collective-permute-start | bytes 122888 | tf_op jit(solution)/shard_map/ppermute | solution.py:439
  8.3 1.3 %collective-permute-start.1 = (f32[80,128]{1,0:T(8,128)S(1)}, f32[80,128]{1,0:T(8,128)S(1)}, u32[]{:S(2)}, u32[]{:S(2)}) collective-permute-start(f32[80,128]{1,0:T(8,128)S(1)} %shard_map.93), channel_id=1, source_target_pairs={{0,8},{1,9},{2,10},{3,11},{4,12},{5,13},{6,14},{7,15},{8,0},{9,1},... | collective-permute-start | bytes 122888 | tf_op jit(solution)/shard_map/ppermute | solution.py:439
  9.8 5.3 %collective-permute-start.2 = (f32[80,128]{1,0:T(8,128)S(1)}, f32[80,128]{1,0:T(8,128)S(1)}, u32[]{:S(2)}, u32[]{:S(2)}) collective-permute-start(f32[80,128]{1,0:T(8,128)S(1)} %shard_map.95), channel_id=1, source_target_pairs={{0,4},{1,5},{2,6},{3,7},{4,0},{5,1},{6,2},{7,3},{8,12},{9,13},{10,... | collective-permute-start | bytes 122888 | tf_op jit(solution)/shard_map/ppermute | solution.py:439
  15.2 4.9 %collective-permute-start.3 = (f32[80,128]{1,0:T(8,128)S(1)}, f32[80,128]{1,0:T(8,128)S(1)}, u32[]{:S(2)}, u32[]{:S(2)}) collective-permute-start(f32[80,128]{1,0:T(8,128)S(1)} %shard_map.97), channel_id=1, source_target_pairs={{0,2},{1,3},{2,0},{3,1},{4,6},{5,7},{6,4},{7,5},{8,10},{9,11},{10,... | collective-permute-start | bytes 122888 | tf_op jit(solution)/shard_map/ppermute | solution.py:439
  20.2 4.5 %collective-permute-start.4 = (f32[76,128]{1,0:T(8,128)S(1)}, f32[76,128]{1,0:T(8,128)S(1)}, u32[]{:S(2)}, u32[]{:S(2)}) collective-permute-start(f32[76,128]{1,0:T(8,128)S(1)} %shard_map.99), channel_id=1, source_target_pairs={{0,1},{1,0},{2,3},{3,2},{4,5},{5,4},{6,7},{7,6},{8,9},{9,8},{10,11... | collective-permute-start | bytes 116744 | tf_op jit(solution)/shard_map/ppermute | solution.py:439

commit v4 on v3

--- a/solution.py
+++ b/solution.py
@@ -175,12 +175,11 @@
 
 
 def slot_place(lists, masks, level):
-    slots = lists.shape[2] // LANES
     rows, lanes = [], []
-    for r in range(slots):
+    for r in range(lists.shape[1] // LANES):
         at = slice(r * LANES, (r + 1) * LANES)
-        index = lists[0, level : level + 1, at]
-        rows.append(jnp.where(masks[0, level : level + 1, at] > 0, index >> 7, -1))
+        index = lists[level : level + 1, at]
+        rows.append(jnp.where(masks[level : level + 1, at] > 0, index >> 7, -1))
         lanes.append(index & (LANES - 1))
     return jnp.concatenate(rows, 0), jnp.concatenate(lanes, 0)
 
@@ -220,7 +219,7 @@
         to[f * count : (f + 1) * count, :] = value[0:count, :]
 
 
-def open_kernel(mass, center, quad, lists, masks, pos, weight, faces, counts, pick):
+def open_kernel(mass, center, quad, lists, masks, pick):
     row, lane = slot_place(lists, masks, 0)
 
     def line(f, k):
@@ -305,8 +304,8 @@
     own, place, part, at_q, at_s, shifted, mid, face, out,
     tab, bod, feat, lhs, fw, fu, blhs, bfw, aw, au,
 ):
-    levels = lists.shape[1]
-    slots = lists.shape[2] // LANES
+    slots = SUBS
+    levels = lists.shape[0]
     for level in range(levels):
         row, lane = slot_place(lists, masks, level)
         if level == levels - 1:
@@ -449,9 +448,10 @@
     live = LIVE // LANES
     near_by = lax.axis_size("gz")
     merged = near_by == 2 and bits == levels
-    given = [cell_mass.reshape(rows, LANES), cell_center, cell_quad, cell_lists, slot_masks]
+    given = [cell_mass.reshape(rows, LANES), cell_center, cell_quad]
+    given += [cell_lists[0], slot_masks[0]]
     given += [body_pos, body_mass.reshape(blocks, LANES), face_lists[0], face_counts]
-    pick = call(open_kernel, shaped(10 * wide, LANES), given)
+    pick = call(open_kernel, shaped(10 * wide, LANES), given[:5])
     arrived = swapped(pick, bits - 1)
 
     some = rows // 4

time: 27.3 us -> 25.2 us (0.923)
  local copies, waits for them, and re-layouts: 2.87 us -> 1.52 us
  waiting for transfers between devices: 0.93 us -> 0.55 us
  starting transfers between devices: 9.73 us -> 9.42 us
    unnamed x16 -> x15, local copies, waits for them, and re-layouts: 2.87 us -> 1.52 us
    ppermute x5, waiting for transfers between devices: 0.93 us -> 0.55 us  [swapped(): lax.ppermute(value, AXES, [(k, k ^ mask) for k in range(lax.axis_size(AXE...]
    ppermute x5, starting transfers between devices: 9.73 us -> 9.42 us  [swapped(): lax.ppermute(value, AXES, [(k, k ^ mask) for k in range(lax.axis_size(AXE...]
  transfers between devices with their start and end apart: 5 -> 5, of which waited for: 3 -> 2; matrix products, arithmetic and copies ran while one was open for 0% -> 0% of each run, Pallas kernels for 38% -> 41%
where the time goes in v4:
time: 25.2 us; the launch traced here: 25 us
  Pallas kernels  13.4 us (53%)
  starting transfers between devices  9.42 us (37%)
  local copies, waits for them, and re-layouts  1.52 us (6%)
  waiting for transfers between devices  0.55 us (2%)
    pallas_call x11, Pallas kernels, call(): pl.pallas_call(kernel, out_shape=out_shape, in_specs=specs, out_specs=[vm...  13.4 us
    ppermute x5, starting transfers between devices, swapped(): lax.ppermute(value, AXES, [(k, k ^ mask) for k in range(lax.axis_size(AXE...  9.42 us
    unnamed x15, local copies, waits for them, and re-layouts  1.52 us
    ppermute x5, waiting for transfers between devices, swapped(): lax.ppermute(value, AXES, [(k, k ^ mask) for k in range(lax.axis_size(AXE...  0.55 us
  transfers between devices with their start and end apart: 5, of which 2 were waited for; matrix products, arithmetic and copies ran while one was open for 0% of the time, Pallas kernels for 41%

profile of v4, /device:TPU:0, one launch (start us, length us, event | category | flops | bytes accessed | tf_op | source)
XLA Modules:
  0.0 25.0 jit_solution(12823459543653744638)
XLA Ops:
  0.0 0.0 copy-start
  0.0 0.0 copy-start.1
  0.0 0.8 %copy_bitcast_fusion = (s32[5,1024]{1,0:T(8,128)S(1)}, s32[5,1024]{1,0:T(8,128)S(1)}) fusion(s32[1,5,1024]{2,0,1:T(1,128)} %param.15, s32[1,5,1024]{2,0,1:T(1,128)} %param.14), kind=kLoop, calls=%fused_computation | loop fusion | bytes 81920
  0.8 0.0 copy-done
  0.8 0.0 copy-done.1
  0.8 0.0 copy-done.2
  0.8 0.2 shard_map.92
  1.1 0.0 copy-start.4
  1.1 3.0 %collective-permute-start = (f32[80,128]{1,0:T(8,128)S(1)}, f32[80,128]{1,0:T(8,128)S(1)}, u32[]{:S(2)}, u32[]{:S(2)}) collective-permute-start(f32[80,128]{1,0:T(8,128)S(1)} %shard_map.92), channel_id=1, source_target_pairs={{0,16},{1,17},{2,18},{3,19},{4,20},{5,21},{6,22},{7,23},{8,24},{9,... | collective-permute-start | bytes 122888 | tf_op jit(solution)/shard_map/ppermute | solution.py:438
  4.1 0.0 copy-done.3
  4.1 0.0 copy-done.4
  4.1 0.7 %copy-done.5 = s32[1,2,4]{2,1,0:T(2,128)S(1)} copy-done((s32[1,2,4]{2,1,0:T(2,128)S(1)}, s32[1,2,4]{2,1,0:T(2,128)}, u32[]{:S(2)}) %copy-start.5) | copy-done | bytes 56
  4.8 0.0 copy-done.6
  4.8 1.6 %shard_map.91 = (f32[160,128]{1,0:T(8,128)S(1)}, s32[80,128]{1,0:T(8,128)S(1)}, f32[80,128]{1,0:T(8,128)S(1)}, bf16[64,512]{1,0:T(8,128)(2,1)S(1)}, bf16[96,512]...) custom-call(f32[16,128]{1,0:T(8,128)S(1)} %bitcast.8, ...), custom_call_target="tpu_custom_call" | custom-call | flops 18350080 | bytes 262144 | tf_op jit(solution)/shard_map/pallas_call | solution.py:412
  6.4 0.0 collective-permute-done.table.refs_1_.refs_0_
  6.4 0.1 shard_map.93
  6.6 0.1 collective-permute-start.1
  6.6 1.1 %shard_map.94 = (f32[3,512]{1,0:T(4,128)S(1)}, f32[80,128]{1,0:T(8,128)S(1)}) custom-call(bf16[64,512]{1,0:T(8,128)(2,1)S(1)} %get-tuple-element.32.at_q.refs_0_, bf16[96,512]{1,0:T(8,128)(2,1)S(1)} %get-tuple-element.33.at_s.refs_1_, f32[8,512]{1,0:T(8,128)S(1)} %get-tuple-element.34.shifted.refs_2_, f32[8,128]{1,0:T(8,128)S(1)} %get-tuple-element.35.mid.refs_3_, ...), custom_call_target="tpu_custom_call" | custom-call | flops 13107200 | bytes 262144 | tf_op jit(solution)/shard_map/pallas_call | solution.py:412
  7.7 0.1 collective-permute-done.1.table.refs_2_.refs_1_
  7.8 0.1 shard_map.95
  8.0 2.9 %collective-permute-start.2 = (f32[80,128]{1,0:T(8,128)S(1)}, f32[80,128]{1,0:T(8,128)S(1)}, u32[]{:S(2)}, u32[]{:S(2)}) collective-permute-start(f32[80,128]{1,0:T(8,128)S(1)} %shard_map.95), channel_id=1, source_target_pairs={{0,4},{1,5},{2,6},{3,7},{4,0},{5,1},{6,2},{7,3},{8,12},{9,13},{10,... | collective-permute-start | bytes 122888 | tf_op jit(solution)/shard_map/ppermute | solution.py:438
  10.9 1.7 %shard_map.96 = (f32[3,512]{1,0:T(4,128)S(1)}, f32[80,128]{1,0:T(8,128)S(1)}) custom-call(bf16[64,512]{1,0:T(8,128)(2,1)S(1)} %get-tuple-element.32.at_q.refs_0_, bf16[96,512]{1,0:T(8,128)(2,1)S(1)} %get-tuple-element.33.at_s.refs_1_, f32[8,512]{1,0:T(8,128)S(1)} %get-tuple-element.34.shifted.refs_2_, f32[8,128]{1,0:T(8,128)S(1)} %get-tuple-element.35.mid.refs_3_, ...), custom_call_target="tpu_custom_call" | custom-call | flops 26214400 | bytes 262144 | tf_op jit(solution)/shard_map/pallas_call | solution.py:412
  12.6 0.4 %collective-permute-done.2.table.refs_3_.refs_0_ = f32[80,128]{1,0:T(8,128)S(1)} collective-permute-done((f32[80,128]{1,0:T(8,128)S(1)}, f32[80,128]{1,0:T(8,128)S(1)}, u32[]{:S(2)}, u32[]{:S(2)}) %collective-permute-start.2) | collective-permute-done | bytes 40992 | tf_op jit(solution)/shard_map/ppermute | solution.py:438
  13.0 0.1 shard_map.97
  13.1 1.9 %collective-permute-start.3 = (f32[80,128]{1,0:T(8,128)S(1)}, f32[80,128]{1,0:T(8,128)S(1)}, u32[]{:S(2)}, u32[]{:S(2)}) collective-permute-start(f32[80,128]{1,0:T(8,128)S(1)} %shard_map.97), channel_id=1, source_target_pairs={{0,2},{1,3},{2,0},{3,1},{4,6},{5,7},{6,4},{7,5},{8,10},{9,11},{10,... | collective-permute-start | bytes 122888 | tf_op jit(solution)/shard_map/ppermute | solution.py:438
  15.0 3.0 %shard_map.98 = (f32[3,512]{1,0:T(4,128)S(1)}, f32[80,128]{1,0:T(8,128)S(1)}) custom-call(bf16[64,512]{1,0:T(8,128)(2,1)S(1)} %get-tuple-element.32.at_q.refs_0_, bf16[96,512]{1,0:T(8,128)(2,1)S(1)} %get-tuple-element.33.at_s.refs_1_, f32[8,512]{1,0:T(8,128)S(1)} %get-tuple-element.34.shifted.refs_2_, f32[8,128]{1,0:T(8,128)S(1)} %get-tuple-element.35.mid.refs_3_, ...), custom_call_target="tpu_custom_call" | custom-call | flops 52428800 | bytes 262144 | tf_op jit(solution)/shard_map/pallas_call | solution.py:412
  18.0 0.0 collective-permute-done.3.table.refs_1_
  18.0 0.1 shard_map.99
  18.2 1.6 %collective-permute-start.4 = (f32[76,128]{1,0:T(8,128)S(1)}, f32[76,128]{1,0:T(8,128)S(1)}, u32[]{:S(2)}, u32[]{:S(2)}) collective-permute-start(f32[76,128]{1,0:T(8,128)S(1)} %shard_map.99), channel_id=1, source_target_pairs={{0,1},{1,0},{2,3},{3,2},{4,5},{5,4},{6,7},{7,6},{8,9},{9,8},{10,11... | collective-permute-start | bytes 116744 | tf_op jit(solution)/shard_map/ppermute | solution.py:438
  19.8 2.9 %shard_map.100.refs_9_ = f32[3,512]{1,0:T(4,128)S(1)} custom-call(bf16[64,512]{1,0:T(8,128)(2,1)S(1)} %get-tuple-element.32.at_q.refs_0_, bf16[96,512]{1,0:T(8,128)(2,1)S(1)} %get-tuple-element.33.at_s.refs_1_, f32[8,512]{1,0:T(8,128)S(1)} %get-tuple-element.34.shifted.refs_2_, f32[8,128]{1,0:T(8,128)S(1)} %get-tuple-element.35.mid.refs_3_, ...), custom_call_target="tpu_custom_call" | custom-call | flops 52428800 | bytes 262144 | tf_op jit(solution)/shard_map/pallas_call | solution.py:412
  22.7 0.0 collective-permute-done.4.refs_4_
  22.7 2.3 %shard_map.101 = f32[3,512]{1,0:T(4,128)} custom-call(bf16[64,512]{1,0:T(8,128)(2,1)S(1)} %get-tuple-element.32.at_q.refs_0_, bf16[96,512]{1,0:T(8,128)(2,1)S(1)} %get-tuple-element.33.at_s.refs_1_, f32[8,512]{1,0:T(8,128)S(1)} %get-tuple-element.34.shifted.refs_2_, f32[8,128]{1,0:T(8,128)S(1)} %get-tuple-element.35.mid.refs_3_, ...), custom_call_target="tpu_custom_call" | custom-call | flops 19660800 | bytes 262144 | tf_op jit(solution)/shard_map/pallas_call | solution.py:412
  (4 shorter events, 0.0 us)
Async XLA Ops:
  0.0 0.8 %copy-start = (f32[6,2048]{1,0:T(8,128)S(1)}, f32[6,2048]{1,0:T(8,128)}, u32[]{:S(2)}) copy-start(f32[6,2048]{1,0:T(8,128)} %quad.3) | copy-start | bytes 147460
  0.0 0.8 %copy-start.1 = (f32[3,2048]{1,0:T(4,128)S(1)}, f32[3,2048]{1,0:T(4,128)}, u32[]{:S(2)}) copy-start(f32[3,2048]{1,0:T(4,128)} %center.3) | copy-start | bytes 73732
  0.0 0.8 %copy-start.2 = (f32[2048]{0:T(1024)S(1)}, f32[2048]{0:T(1024)}, u32[]{:S(2)}) copy-start(f32[2048]{0:T(1024)} %param.11) | copy-start | bytes 24580
  0.8 3.3 %copy-start.3 = (f32[3,512]{1,0:T(4,128)S(1)}, f32[3,512]{1,0:T(4,128)}, u32[]{:S(2)}) copy-start(f32[3,512]{1,0:T(4,128)} %pos.1) | copy-start | bytes 18436
  1.1 3.0 %copy-start.4 = (f32[512]{0:T(512)S(1)}, f32[512]{0:T(512)}, u32[]{:S(2)}) copy-start(f32[512]{0:T(512)} %param.10) | copy-start | bytes 6148
  1.1 5.3 %collective-permute-start = (f32[80,128]{1,0:T(8,128)S(1)}, f32[80,128]{1,0:T(8,128)S(1)}, u32[]{:S(2)}, u32[]{:S(2)}) collective-permute-start(f32[80,128]{1,0:T(8,128)S(1)} %shard_map.92), channel_id=1, source_target_pairs={{0,16},{1,17},{2,18},{3,19},{4,20},{5,21},{6,22},{7,23},{8,24},{9,... | collective-permute-start | bytes 122888 | tf_op jit(solution)/shard_map/ppermute | solution.py:438
  4.1 0.7 %copy-start.5 = (s32[1,2,4]{2,1,0:T(2,128)S(1)}, s32[1,2,4]{2,1,0:T(2,128)}, u32[]{:S(2)}) copy-start(s32[1,2,4]{2,1,0:T(2,128)} %param.16) | copy-start | bytes 100
  4.1 0.7 %copy-start.6 = (s32[1,2]{1,0:T(1,128)S(1)}, s32[1,2]{1,0:T(1,128)}, u32[]{:S(2)}) copy-start(s32[1,2]{1,0:T(1,128)} %counts.1) | copy-start | bytes 28
  6.6 1.3 %collective-permute-start.1 = (f32[80,128]{1,0:T(8,128)S(1)}, f32[80,128]{1,0:T(8,128)S(1)}, u32[]{:S(2)}, u32[]{:S(2)}) collective-permute-start(f32[80,128]{1,0:T(8,128)S(1)} %shard_map.93), channel_id=1, source_target_pairs={{0,8},{1,9},{2,10},{3,11},{4,12},{5,13},{6,14},{7,15},{8,0},{9,1},... | collective-permute-start | bytes 122888 | tf_op jit(solution)/shard_map/ppermute | solution.py:438
  8.0 5.0 %collective-permute-start.2 = (f32[80,128]{1,0:T(8,128)S(1)}, f32[80,128]{1,0:T(8,128)S(1)}, u32[]{:S(2)}, u32[]{:S(2)}) collective-permute-start(f32[80,128]{1,0:T(8,128)S(1)} %shard_map.95), channel_id=1, source_target_pairs={{0,4},{1,5},{2,6},{3,7},{4,0},{5,1},{6,2},{7,3},{8,12},{9,13},{10,... | collective-permute-start | bytes 122888 | tf_op jit(solution)/shard_map/ppermute | solution.py:438
  13.1 4.9 %collective-permute-start.3 = (f32[80,128]{1,0:T(8,128)S(1)}, f32[80,128]{1,0:T(8,128)S(1)}, u32[]{:S(2)}, u32[]{:S(2)}) collective-permute-start(f32[80,128]{1,0:T(8,128)S(1)} %shard_map.97), channel_id=1, source_target_pairs={{0,2},{1,3},{2,0},{3,1},{4,6},{5,7},{6,4},{7,5},{8,10},{9,11},{10,... | collective-permute-start | bytes 122888 | tf_op jit(solution)/shard_map/ppermute | solution.py:438
  18.2 4.5 %collective-permute-start.4 = (f32[76,128]{1,0:T(8,128)S(1)}, f32[76,128]{1,0:T(8,128)S(1)}, u32[]{:S(2)}, u32[]{:S(2)}) collective-permute-start(f32[76,128]{1,0:T(8,128)S(1)} %shard_map.99), channel_id=1, source_target_pairs={{0,1},{1,0},{2,3},{3,2},{4,5},{5,4},{6,7},{7,6},{8,9},{9,8},{10,11... | collective-permute-start | bytes 116744 | tf_op jit(solution)/shard_map/ppermute | solution.py:438

commit v5 on v4

--- a/solution.py
+++ b/solution.py
@@ -232,11 +232,10 @@
     store_rows(pick, picked(row, lane, line, 0, mass.shape[0], zeros), row.shape[0])
 
 
-def packed(row, lane):
-    subs = row.shape[0]
-    live = row >= 0
-    at_row = lax.broadcasted_iota(jnp.int32, row.shape, 0)
-    at_lane = lax.broadcasted_iota(jnp.int32, row.shape, 1)
+def packed(live, value, bits):
+    subs = live.shape[0]
+    at_row = lax.broadcasted_iota(jnp.int32, live.shape, 0)
+    at_lane = lax.broadcasted_iota(jnp.int32, live.shape, 1)
     upper = lax.broadcasted_iota(jnp.int32, (LANES, LANES), 0) < lax.broadcasted_iota(jnp.int32, (LANES, LANES), 1)
     dead = jnp.where(live, 0.0, 1.0).astype(bf16)
     before = dot(dead, jnp.where(upper, 1.0, 0.0).astype(bf16))
@@ -247,9 +246,9 @@
         run = run + jnp.where(at_row >= step, pltpu.roll(run, step, axis=0), 0.0)
         step *= 2
     move = (before + run - whole).astype(jnp.int32)
-    word = jnp.where(live, (((move + subs * LANES) << 6) + row << 7) + lane, 0)
+    word = jnp.where(live, ((move + subs * LANES) << bits) + value, 0)
     step = 1
-    shift = 13
+    shift = bits
     while step < subs * LANES:
         if step < LANES:
             turned = pltpu.roll(word, LANES - step, axis=1)
@@ -260,7 +259,20 @@
         word = jnp.where((come >> shift) & 1 == 1, come, stay)
         step *= 2
         shift += 1
-    return jnp.where(word > 0, (word >> 7) & 63, -1), word & (LANES - 1)
+    return word > 0, word & ((1 << bits) - 1)
+
+
+def packed_place(row, lane, live):
+    found, value = packed(live, row * LANES + lane, 13)
+    return jnp.where(found, value >> 7, -1), value & (LANES - 1)
+
+
+def packed_table(table, to, count):
+    shape = (SUBS, LANES)
+    index = lax.broadcasted_iota(jnp.int32, shape, 0) * LANES + lax.broadcasted_iota(jnp.int32, shape, 1)
+    found, value = packed(table[0:SUBS, :] > 0.0, index, 10)
+    row = jnp.where(found, value >> 7, -1)
+    store_rows(to, picked_tables(row, value & (LANES - 1), [table]), count)
 
 
 def read_cells(table, first, count, mid):
@@ -309,7 +321,7 @@
     for level in range(levels):
         row, lane = slot_place(lists, masks, level)
         if level == levels - 1:
-            row, lane = packed(row, lane)
+            row, lane = packed_place(row, lane, row >= 0)
         place[2 * level * slots : (2 * level + 1) * slots, :] = row
         place[(2 * level + 1) * slots : (2 * level + 2) * slots, :] = lane
     rows = mass.shape[0]
@@ -361,30 +373,45 @@
     store_sums(out, shifted, aw, au)
 
 
-def window_kernel(spans, ahead, count, at_q, at_s, shifted, mid, place, *refs):
-    tables = refs[:count]
-    if ahead:
-        out, part, feat, lhs, fw, fu, aw, au = refs[count:]
-        level, ids = ahead
-        row = place[2 * level * SUBS : (2 * level + 1) * SUBS, :]
-        lane = place[(2 * level + 1) * SUBS : (2 * level + 2) * SUBS, :]
-        store_rows(part, picked_tables(row, lane, [tables[k] for k in ids]), SUBS)
-    else:
-        out, feat, lhs, fw, fu, aw, au = refs[count:]
+def placed(place, level):
+    row = place[2 * level * SUBS : (2 * level + 1) * SUBS, :]
+    return row, place[(2 * level + 1) * SUBS : (2 * level + 2) * SUBS, :]
+
+
+def window_kernel(spans, ahead, dense, inside, count, bodies, at_q, at_s, shifted, mid, place, *refs):
+    tables, sides = list(refs[:count]), refs[count : count + bodies]
+    refs = list(refs[count + bodies :])
+    out = refs.pop(0)
+    for level, ids in ahead:
+        row, lane = placed(place, level)
+        store_rows(refs.pop(0), picked_tables(row, lane, [tables[k] for k in ids]), SUBS)
+    if dense is not None:
+        to = refs.pop(0)
+        packed_table(tables[dense], to, to.shape[0] // 10)
+    au, aw = refs.pop(), refs.pop()
+    room = refs.pop() if inside is not None else None
+    feat, lhs, fw, fu = refs[:4]
+    blhs, bfw = refs[4:6] if bodies else (None, None)
+    near = 0
+    for side in sides:
+        mass, center, blocks = read_bodies(side, mid)
+        body_features(mass, center, blocks, feat, blhs, bfw, near)
+        near += blocks * LANES
+    if inside is not None:
+        packed_table(tables[inside], room, room.shape[0] // 10)
+        tables[inside] = room
     base = span_features([(tables[k], first, many) for k, first, many in spans], mid, feat, lhs, fw, fu)
-    pair_sums(base, 0, at_q, at_s, lhs, fw, fu, None, None, aw, au)
+    pair_sums(base, near, at_q, at_s, lhs, fw, fu, blhs, bfw, aw, au)
     store_sums(out, shifted, aw, au)
 
 
 def pick_kernel(level, base, live, faces, place, part, table, *refs):
-    pick = refs[-1]
-    row = place[2 * level * SUBS : (2 * level + 1) * SUBS, :]
-    lane = place[(2 * level + 1) * SUBS : (2 * level + 2) * SUBS, :]
+    row, lane = placed(place, level)
     rows, line = table_lines(table)
     out = [part[f * SUBS : (f + 1) * SUBS, :] for f in range(10)]
-    store_rows(pick, picked(row, lane, line, base, rows, out), live)
+    store_rows(refs[-1], picked(row, lane, line, base, rows, out), live)
     if faces:
-        pick[10 * live :, :] = refs[0][...]
+        refs[-1][10 * live :, :] = refs[0][...]
 
 
 def last_kernel(merged, faces, parts, live, *refs):
@@ -416,7 +443,7 @@
         out_specs=[vmem] * len(out_shape) if many else vmem,
         scratch_shapes=list(scratch),
         compiler_params=pltpu.CompilerParams(vmem_limit_bytes=32 * 2**20),
-        cost_estimate=pl.CostEstimate(flops=flops, bytes_accessed=2**18, transcendentals=0),
+        cost_estimate=pl.CostEstimate(flops=flops * 64, bytes_accessed=2**18, transcendentals=0),
     )(*args)
 
 
@@ -454,7 +481,7 @@
     pick = call(open_kernel, shaped(10 * wide, LANES), given[:5])
     arrived = swapped(pick, bits - 1)
 
-    some = rows // 4
+    some = rows // 8
     own, place, part, at_q, at_s, shifted, mid, face, near = call(
         functools.partial(start_kernel, merged, some),
         [
@@ -475,28 +502,32 @@
     )
     common = [at_q, at_s, shifted, mid]
 
-    def window(spans, ahead):
+    def window(spans, ahead=(), dense=None, inside=None, bodies=(), cost=1):
         tables = []
-        for table, first, many in spans:
-            if not any(table is known for known in tables):
+        for table in [span[0] for span in spans] + [t for item in ahead for t in item[1]] + [dense]:
+            if table is not None and not any(table is known for known in tables):
                 tables.append(table)
-        if ahead:
-            tables += [t for t in ahead[1] if not any(t is known for known in tables)]
-
-        def place_of(table):
-            return [table is known for known in tables].index(True)
+
+        def at(table):
+            return None if table is None else [table is known for known in tables].index(True)
 
         count = sum(many for table, first, many in spans) * LANES
         kernel = functools.partial(
             window_kernel,
-            [(place_of(table), first, many) for table, first, many in spans],
-            (ahead[0], [place_of(t) for t in ahead[1]]) if ahead else None,
+            [(at(table), first, many) for table, first, many in spans],
+            [(level, [at(t) for t in some_tables]) for level, some_tables in ahead],
+            at(dense),
+            at(inside),
             len(tables),
+            len(bodies),
         )
-        outs = [shaped(3, targets)] + ([shaped(10 * wide, LANES)] if ahead else [])
-        scratch = sum_scratch(targets, count, 0)
-        got = call(kernel, outs, common + [place] + tables, scratch, flops=targets * count * 50)
-        return got
+        outs = [shaped(3, targets)] + [shaped(10 * wide, LANES)] * len(ahead)
+        outs += [shaped(10 * live, LANES)] if dense is not None else []
+        scratch = sum_scratch(targets, count, targets * len(bodies))
+        if inside is not None:
+            scratch.insert(-2, pltpu.VMEM((10 * live, LANES), f32))
+        flops = int(cost * targets * (count * 50 + len(bodies) * targets * 20))
+        return call(kernel, outs, common + [place] + tables + list(bodies), scratch, flops=flops)
 
     sides = []
     if not merged:
@@ -505,32 +536,41 @@
             lax.ppermute(upper, "gz", [(k, k + 1) for k in range(near_by - 1)]),
             lax.ppermute(lower, "gz", [(k + 1, k) for k in range(near_by - 1)]),
         ]
+
+    def cut(start, stop):
+        return (own, start * rows // 8, (stop - start) * rows // 8)
+
     tables = [own]
+    dense = []
     sums = []
     tied = [near, part]
     for level in range(1, levels):
-        arrived, total, part = lax.optimization_barrier((arrived, *tied))
-        sums.append(total)
+        tied = list(lax.optimization_barrier((arrived, *tied)))
+        arrived = tied.pop(0)
+        sums.append(tied.pop(0))
+        part = tied.pop(0)
+        dense += tied
         last = level == levels - 1
         extra = [face] if merged and last else []
         many = live if last else wide
-        base = rows + (level - 1) * wide
         pick = call(
-            functools.partial(pick_kernel, level, base, many, len(extra)),
+            functools.partial(pick_kernel, level, rows + (level - 1) * wide, many, len(extra)),
             shaped(10 * many + len(extra) * 4 * blocks, LANES),
             [place, part, arrived] + extra,
         )
         tables.append(arrived)
+        newest = arrived
         arrived = swapped(pick, bits - 1 - level)
         if level == 1:
-            spans = [(own, some, some)]
+            spans = [cut(1, 3)]
         elif level == 2:
-            spans = [(own, 2 * some, rows - 2 * some)]
+            spans = [cut(3, 8)]
         elif level == 3:
-            spans = [(tables[1], 0, wide), (tables[2], 0, wide)]
+            spans = [(dense[0], 0, live), (dense[1], 0, live)]
         else:
-            spans = [(t, 0, wide) for t in tables[3:]]
-        tied = window(spans, None if last else (level + 1, list(tables)))
+            spans = [(dense[2], 0, live), (newest, 0, wide)]
+        ahead = [] if last else [(level + 1, list(tables))]
+        tied = window(spans, ahead, None if last else newest)
     sums += tied
     return call(
         functools.partial(last_kernel, merged, len(sides), len(sums), live),

time: 25.2 us -> 24.2 us (0.960)
  Pallas kernels: 13.4 us -> 12.6 us
  waiting for transfers between devices: 0.55 us -> 0.19 us
    pallas_call x11, Pallas kernels: 13.4 us -> 12.6 us  [call(): pl.pallas_call(kernel, out_shape=out_shape, in_specs=specs, out_specs=[vm...]
    ppermute x5, waiting for transfers between devices: 0.55 us -> 0.19 us  [swapped(): lax.ppermute(value, AXES, [(k, k ^ mask) for k in range(lax.axis_size(AXE...]
  transfers between devices with their start and end apart: 5 -> 5, of which waited for: 2 -> 1; matrix products, arithmetic and copies ran while one was open for 0% -> 0% of each run, Pallas kernels for 41% -> 39%
where the time goes in v5:
time: 24.2 us; the launch traced here: 24 us
  Pallas kernels  12.6 us (52%)
  starting transfers between devices  9.62 us (40%)
  local copies, waits for them, and re-layouts  1.52 us (6%)
    pallas_call x11, Pallas kernels, call(): pl.pallas_call(kernel, out_shape=out_shape, in_specs=specs, out_specs=[vm...  12.6 us
    ppermute x5, starting transfers between devices, swapped(): lax.ppermute(value, AXES, [(k, k ^ mask) for k in range(lax.axis_size(AXE...  9.62 us
    unnamed x15, local copies, waits for them, and re-layouts  1.52 us
  transfers between devices with their start and end apart: 5, of which 1 were waited for; matrix products, arithmetic and copies ran while one was open for 0% of the time, Pallas kernels for 39%

profile of v5, /device:TPU:0, one launch (start us, length us, event | category | flops | bytes accessed | tf_op | source)
XLA Modules:
  0.0 24.0 jit_solution(15701208410217655783)
XLA Ops:
  0.0 0.0 copy-start
  0.0 0.0 copy-start.1
  0.0 0.8 %copy_bitcast_fusion = (s32[5,1024]{1,0:T(8,128)S(1)}, s32[5,1024]{1,0:T(8,128)S(1)}) fusion(s32[1,5,1024]{2,0,1:T(1,128)} %param.15, s32[1,5,1024]{2,0,1:T(1,128)} %param.14), kind=kLoop, calls=%fused_computation | loop fusion | bytes 81920
  0.8 0.0 copy-done
  0.8 0.0 copy-done.1
  0.8 0.0 copy-done.2
  0.8 0.2 %shard_map.92 = f32[80,128]{1,0:T(8,128)S(1)} custom-call(f32[16,128]{1,0:T(8,128)S(1)} %bitcast.7, f32[3,2048]{1,0:T(4,128)S(1)} %copy-done.1, f32[6,2048]{1,0:T(8,128)S(1)} %copy-done, s32[5,1024]{1,0:T(8,128)S(1)} %get-tuple-element.72.lists, s32[5,1024]{1,0:T(8,128)S(1)} %get-tuple-element.71.masks), custom_call_target="tpu_custom_call" | custom-call | bytes 262144 | tf_op jit(solution)/shard_map/pallas_call | solution.py:439
  1.1 0.0 copy-start.4
  1.1 3.0 %collective-permute-start = (f32[80,128]{1,0:T(8,128)S(1)}, f32[80,128]{1,0:T(8,128)S(1)}, u32[]{:S(2)}, u32[]{:S(2)}) collective-permute-start(f32[80,128]{1,0:T(8,128)S(1)} %shard_map.92), channel_id=1, source_target_pairs={{0,16},{1,17},{2,18},{3,19},{4,20},{5,21},{6,22},{7,23},{8,24},{9,... | collective-permute-start | bytes 122888 | tf_op jit(solution)/shard_map/ppermute | solution.py:465
  4.1 0.0 copy-done.3
  4.1 0.0 copy-done.4
  4.1 0.7 %copy-done.5 = s32[1,2,4]{2,1,0:T(2,128)S(1)} copy-done((s32[1,2,4]{2,1,0:T(2,128)S(1)}, s32[1,2,4]{2,1,0:T(2,128)}, u32[]{:S(2)}) %copy-start.5) | copy-done | bytes 56
  4.8 0.0 copy-done.6
  4.8 1.3 %shard_map.91 = (f32[160,128]{1,0:T(8,128)S(1)}, s32[80,128]{1,0:T(8,128)S(1)}, f32[80,128]{1,0:T(8,128)S(1)}, bf16[64,512]{1,0:T(8,128)(2,1)S(1)}, bf16[96,512]...) custom-call(f32[16,128]{1,0:T(8,128)S(1)} %bitcast.8, ...), custom_call_target="tpu_custom_call" | custom-call | flops 754974720 | bytes 262144 | tf_op jit(solution)/shard_map/pallas_call | solution.py:439
  6.1 0.0 collective-permute-done.table.refs_1_.refs_3_
  6.1 0.1 shard_map.93
  6.2 0.1 collective-permute-start.1
  6.3 1.2 %shard_map.94 = (f32[3,512]{1,0:T(4,128)S(1)}, f32[80,128]{1,0:T(8,128)S(1)}, f32[60,128]{1,0:T(8,128)S(1)}) custom-call(bf16[64,512]{1,0:T(8,128)(2,1)S(1)} %get-tuple-element.38.at_q.refs_0_, bf16[96,512]{1,0:T(8,128)(2,1)S(1)} %get-tuple-element.39.at_s.refs_1_, f32[8,512]{1,0:T(8,128)S(1)} %get-tuple-element.40.shifted.refs_2_, ...), custom_call_target="tpu_custom_call" | custom-call | flops 838860800 | bytes 262144 | tf_op jit(solution)/shard_map/pallas_call | solution.py:439
  7.5 0.0 collective-permute-done.1.table.refs_2_.refs_4_
  7.5 0.1 shard_map.95
  7.7 3.2 %collective-permute-start.2 = (f32[80,128]{1,0:T(8,128)S(1)}, f32[80,128]{1,0:T(8,128)S(1)}, u32[]{:S(2)}, u32[]{:S(2)}) collective-permute-start(f32[80,128]{1,0:T(8,128)S(1)} %shard_map.95), channel_id=1, source_target_pairs={{0,4},{1,5},{2,6},{3,7},{4,0},{5,1},{6,2},{7,3},{8,12},{9,13},{10,... | collective-permute-start | bytes 122888 | tf_op jit(solution)/shard_map/ppermute | solution.py:465
  10.9 2.1 %shard_map.96 = (f32[3,512]{1,0:T(4,128)S(1)}, f32[80,128]{1,0:T(8,128)S(1)}, f32[60,128]{1,0:T(8,128)S(1)}) custom-call(bf16[64,512]{1,0:T(8,128)(2,1)S(1)} %get-tuple-element.38.at_q.refs_0_, bf16[96,512]{1,0:T(8,128)(2,1)S(1)} %get-tuple-element.39.at_s.refs_1_, f32[8,512]{1,0:T(8,128)S(1)} %get-tuple-element.40.shifted.refs_2_, ...), custom_call_target="tpu_custom_call" | custom-call | flops 2097152000 | bytes 262144 | tf_op jit(solution)/shard_map/pallas_call | solution.py:439
  12.9 0.1 collective-permute-done.2.table.refs_5_
  13.1 0.1 shard_map.97
  13.2 1.7 %collective-permute-start.3 = (f32[80,128]{1,0:T(8,128)S(1)}, f32[80,128]{1,0:T(8,128)S(1)}, u32[]{:S(2)}, u32[]{:S(2)}) collective-permute-start(f32[80,128]{1,0:T(8,128)S(1)} %shard_map.97), channel_id=1, source_target_pairs={{0,2},{1,3},{2,0},{3,1},{4,6},{5,7},{6,4},{7,5},{8,10},{9,11},{10,... | collective-permute-start | bytes 122888 | tf_op jit(solution)/shard_map/ppermute | solution.py:465
  15.0 2.4 %shard_map.98 = (f32[3,512]{1,0:T(4,128)S(1)}, f32[80,128]{1,0:T(8,128)S(1)}, f32[60,128]{1,0:T(8,128)S(1)}) custom-call(bf16[64,512]{1,0:T(8,128)(2,1)S(1)} %get-tuple-element.38.at_q.refs_0_, bf16[96,512]{1,0:T(8,128)(2,1)S(1)} %get-tuple-element.39.at_s.refs_1_, f32[8,512]{1,0:T(8,128)S(1)} %get-tuple-element.40.shifted.refs_2_, ...), custom_call_target="tpu_custom_call" | custom-call | flops 2516582400 | bytes 262144 | tf_op jit(solution)/shard_map/pallas_call | solution.py:439
  17.4 0.0 collective-permute-done.3.table.refs_1_
  17.4 0.1 shard_map.99
  17.5 1.6 %collective-permute-start.4 = (f32[76,128]{1,0:T(8,128)S(1)}, f32[76,128]{1,0:T(8,128)S(1)}, u32[]{:S(2)}, u32[]{:S(2)}) collective-permute-start(f32[76,128]{1,0:T(8,128)S(1)} %shard_map.99), channel_id=1, source_target_pairs={{0,1},{1,0},{2,3},{3,2},{4,5},{5,4},{6,7},{7,6},{8,9},{9,8},{10,11... | collective-permute-start | bytes 116744 | tf_op jit(solution)/shard_map/ppermute | solution.py:465
  19.2 2.6 %shard_map.100.refs_9_ = f32[3,512]{1,0:T(4,128)S(1)} custom-call(bf16[64,512]{1,0:T(8,128)(2,1)S(1)} %get-tuple-element.38.at_q.refs_0_, bf16[96,512]{1,0:T(8,128)(2,1)S(1)} %get-tuple-element.39.at_s.refs_1_, f32[8,512]{1,0:T(8,128)S(1)} %get-tuple-element.40.shifted.refs_2_, f32[8,128]{1,0:T(8,128)S(1)} %get-tuple-element.41.mid.refs_3_, ...), custom_call_target="tpu_custom_call" | custom-call | flops 2936012800 | bytes 262144 | tf_op jit(solution)/shard_map/pallas_call | solution.py:439
  21.7 0.0 collective-permute-done.4.refs_4_
  21.7 2.3 %shard_map.101 = f32[3,512]{1,0:T(4,128)} custom-call(bf16[64,512]{1,0:T(8,128)(2,1)S(1)} %get-tuple-element.38.at_q.refs_0_, bf16[96,512]{1,0:T(8,128)(2,1)S(1)} %get-tuple-element.39.at_s.refs_1_, f32[8,512]{1,0:T(8,128)S(1)} %get-tuple-element.40.shifted.refs_2_, f32[8,128]{1,0:T(8,128)S(1)} %get-tuple-element.41.mid.refs_3_, ...), custom_call_target="tpu_custom_call" | custom-call | flops 1258291200 | bytes 262144 | tf_op jit(solution)/shard_map/pallas_call | solution.py:439
  (4 shorter events, 0.0 us)
Async XLA Ops:
  0.0 0.8 %copy-start = (f32[6,2048]{1,0:T(8,128)S(1)}, f32[6,2048]{1,0:T(8,128)}, u32[]{:S(2)}) copy-start(f32[6,2048]{1,0:T(8,128)} %quad.3) | copy-start | bytes 147460
  0.0 0.8 %copy-start.1 = (f32[3,2048]{1,0:T(4,128)S(1)}, f32[3,2048]{1,0:T(4,128)}, u32[]{:S(2)}) copy-start(f32[3,2048]{1,0:T(4,128)} %center.3) | copy-start | bytes 73732
  0.0 0.8 %copy-start.2 = (f32[2048]{0:T(1024)S(1)}, f32[2048]{0:T(1024)}, u32[]{:S(2)}) copy-start(f32[2048]{0:T(1024)} %param.11) | copy-start | bytes 24580
  0.8 3.3 %copy-start.3 = (f32[3,512]{1,0:T(4,128)S(1)}, f32[3,512]{1,0:T(4,128)}, u32[]{:S(2)}) copy-start(f32[3,512]{1,0:T(4,128)} %pos.1) | copy-start | bytes 18436
  1.1 3.0 %copy-start.4 = (f32[512]{0:T(512)S(1)}, f32[512]{0:T(512)}, u32[]{:S(2)}) copy-start(f32[512]{0:T(512)} %param.10) | copy-start | bytes 6148
  1.1 5.0 %collective-permute-start = (f32[80,128]{1,0:T(8,128)S(1)}, f32[80,128]{1,0:T(8,128)S(1)}, u32[]{:S(2)}, u32[]{:S(2)}) collective-permute-start(f32[80,128]{1,0:T(8,128)S(1)} %shard_map.92), channel_id=1, source_target_pairs={{0,16},{1,17},{2,18},{3,19},{4,20},{5,21},{6,22},{7,23},{8,24},{9,... | collective-permute-start | bytes 122888 | tf_op jit(solution)/shard_map/ppermute | solution.py:465
  4.1 0.7 %copy-start.5 = (s32[1,2,4]{2,1,0:T(2,128)S(1)}, s32[1,2,4]{2,1,0:T(2,128)}, u32[]{:S(2)}) copy-start(s32[1,2,4]{2,1,0:T(2,128)} %param.16) | copy-start | bytes 100
  4.1 0.7 %copy-start.6 = (s32[1,2]{1,0:T(1,128)S(1)}, s32[1,2]{1,0:T(1,128)}, u32[]{:S(2)}) copy-start(s32[1,2]{1,0:T(1,128)} %counts.1) | copy-start | bytes 28
  6.2 1.3 %collective-permute-start.1 = (f32[80,128]{1,0:T(8,128)S(1)}, f32[80,128]{1,0:T(8,128)S(1)}, u32[]{:S(2)}, u32[]{:S(2)}) collective-permute-start(f32[80,128]{1,0:T(8,128)S(1)} %shard_map.93), channel_id=1, source_target_pairs={{0,8},{1,9},{2,10},{3,11},{4,12},{5,13},{6,14},{7,15},{8,0},{9,1},... | collective-permute-start | bytes 122888 | tf_op jit(solution)/shard_map/ppermute | solution.py:465
  7.7 5.4 %collective-permute-start.2 = (f32[80,128]{1,0:T(8,128)S(1)}, f32[80,128]{1,0:T(8,128)S(1)}, u32[]{:S(2)}, u32[]{:S(2)}) collective-permute-start(f32[80,128]{1,0:T(8,128)S(1)} %shard_map.95), channel_id=1, source_target_pairs={{0,4},{1,5},{2,6},{3,7},{4,0},{5,1},{6,2},{7,3},{8,12},{9,13},{10,... | collective-permute-start | bytes 122888 | tf_op jit(solution)/shard_map/ppermute | solution.py:465
  13.2 4.1 %collective-permute-start.3 = (f32[80,128]{1,0:T(8,128)S(1)}, f32[80,128]{1,0:T(8,128)S(1)}, u32[]{:S(2)}, u32[]{:S(2)}) collective-permute-start(f32[80,128]{1,0:T(8,128)S(1)} %shard_map.97), channel_id=1, source_target_pairs={{0,2},{1,3},{2,0},{3,1},{4,6},{5,7},{6,4},{7,5},{8,10},{9,11},{10,... | collective-permute-start | bytes 122888 | tf_op jit(solution)/shard_map/ppermute | solution.py:465
  17.5 4.2 %collective-permute-start.4 = (f32[76,128]{1,0:T(8,128)S(1)}, f32[76,128]{1,0:T(8,128)S(1)}, u32[]{:S(2)}, u32[]{:S(2)}) collective-permute-start(f32[76,128]{1,0:T(8,128)S(1)} %shard_map.99), channel_id=1, source_target_pairs={{0,1},{1,0},{2,3},{3,2},{4,5},{5,4},{6,7},{7,6},{8,9},{9,8},{10,11... | collective-permute-start | bytes 116744 | tf_op jit(solution)/shard_map/ppermute | solution.py:465

commit v6 on v5

--- a/solution.py
+++ b/solution.py
@@ -175,13 +175,9 @@
 
 
 def slot_place(lists, masks, level):
-    rows, lanes = [], []
-    for r in range(lists.shape[1] // LANES):
-        at = slice(r * LANES, (r + 1) * LANES)
-        index = lists[level : level + 1, at]
-        rows.append(jnp.where(masks[level : level + 1, at] > 0, index >> 7, -1))
-        lanes.append(index & (LANES - 1))
-    return jnp.concatenate(rows, 0), jnp.concatenate(lanes, 0)
+    at = slice(level * SUBS, (level + 1) * SUBS)
+    index = lists[at, :]
+    return jnp.where(masks[at, :] > 0, index >> 7, -1), index & (LANES - 1)
 
 
 def picked(row, lane, lines, base, count, out):
@@ -219,7 +215,14 @@
         to[f * count : (f + 1) * count, :] = value[0:count, :]
 
 
-def open_kernel(mass, center, quad, lists, masks, pick):
+def open_kernel(count, *refs):
+    sources, pick, here, sems = refs[:count], refs[count], refs[count + 1 : -1], refs[-1]
+    moves = [pltpu.make_async_copy(a, b, sems.at[k]) for k, (a, b) in enumerate(zip(sources, here))]
+    for move in moves:
+        move.start()
+    mass, center, quad, lists, masks = here[:5]
+    for move in moves[:5]:
+        move.wait()
     row, lane = slot_place(lists, masks, 0)
 
     def line(f, k):
@@ -230,6 +233,8 @@
 
     zeros = [jnp.zeros(row.shape, f32)] * 10
     store_rows(pick, picked(row, lane, line, 0, mass.shape[0], zeros), row.shape[0])
+    for move in moves[5:]:
+        move.wait()
 
 
 def packed(live, value, bits):
@@ -317,7 +322,7 @@
     tab, bod, feat, lhs, fw, fu, blhs, bfw, aw, au,
 ):
     slots = SUBS
-    levels = lists.shape[0]
+    levels = lists.shape[0] // slots
     for level in range(levels):
         row, lane = slot_place(lists, masks, level)
         if level == levels - 1:
@@ -476,12 +481,18 @@
     near_by = lax.axis_size("gz")
     merged = near_by == 2 and bits == levels
     given = [cell_mass.reshape(rows, LANES), cell_center, cell_quad]
-    given += [cell_lists[0], slot_masks[0]]
+    given += [cell_lists.reshape(levels * wide, LANES), slot_masks.reshape(levels * wide, LANES)]
     given += [body_pos, body_mass.reshape(blocks, LANES), face_lists[0], face_counts]
-    pick = call(open_kernel, shaped(10 * wide, LANES), given[:5])
+    pick, *given = call(
+        functools.partial(open_kernel, len(given)),
+        [shaped(10 * wide, LANES)] + [shaped(*g.shape, dtype=g.dtype) for g in given],
+        [pltpu.with_memory_space_constraint(g, pltpu.HBM) for g in given],
+        [pltpu.SemaphoreType.DMA((len(given),))],
+        [pl.BlockSpec(memory_space=pltpu.HBM)] * len(given),
+    )
     arrived = swapped(pick, bits - 1)
 
-    some = rows // 8
+    some = 3 * rows // 8
     own, place, part, at_q, at_s, shifted, mid, face, near = call(
         functools.partial(start_kernel, merged, some),
         [
@@ -562,15 +573,15 @@
         newest = arrived
         arrived = swapped(pick, bits - 1 - level)
         if level == 1:
-            spans = [cut(1, 3)]
+            spans = [cut(3, 5)]
         elif level == 2:
-            spans = [cut(3, 8)]
+            spans = [cut(5, 7), (dense[0], 0, live)]
         elif level == 3:
-            spans = [(dense[0], 0, live), (dense[1], 0, live)]
+            spans = [cut(7, 8), (dense[1], 0, live)]
         else:
-            spans = [(dense[2], 0, live), (newest, 0, wide)]
+            spans = [(dense[2], 0, live), (newest, 0, live)]
         ahead = [] if last else [(level + 1, list(tables))]
-        tied = window(spans, ahead, None if last else newest)
+        tied = window(spans, ahead, None if last else newest, newest if last else None)
     sums += tied
     return call(
         functools.partial(last_kernel, merged, len(sides), len(sums), live),

time: 24.2 us -> 24.2 us (level)
  local copies, waits for them, and re-layouts: 1.52 us -> 0 us
  Pallas kernels: 12.6 us -> 13.3 us
  waiting for transfers between devices: 0.19 us -> 0.88 us
    unnamed x15 -> x0, local copies, waits for them, and re-layouts: 1.52 us -> none
    pallas_call x11, Pallas kernels: 12.6 us -> 13.3 us  [call(): pl.pallas_call(kernel, out_shape=out_shape, in_specs=specs, out_specs=[vm...]
    ppermute x5, waiting for transfers between devices: 0.19 us -> 0.88 us  [swapped(): lax.ppermute(value, AXES, [(k, k ^ mask) for k in range(lax.axis_size(AXE...]
  transfers between devices with their start and end apart: 5 -> 5, of which waited for: 1 -> 3; matrix products, arithmetic and copies ran while one was open for 0% -> 0% of each run, Pallas kernels for 39% -> 38%
where the time goes in v6:
time: 24.2 us; the launch traced here: 24 us
  Pallas kernels  13.3 us (55%)
  starting transfers between devices  9.66 us (40%)
  waiting for transfers between devices  0.88 us (4%)
    pallas_call x11, Pallas kernels, call(): pl.pallas_call(kernel, out_shape=out_shape, in_specs=specs, out_specs=[vm...  13.3 us
    ppermute x5, starting transfers between devices, swapped(): lax.ppermute(value, AXES, [(k, k ^ mask) for k in range(lax.axis_size(AXE...  9.66 us
    ppermute x5, waiting for transfers between devices, swapped(): lax.ppermute(value, AXES, [(k, k ^ mask) for k in range(lax.axis_size(AXE...  0.88 us
  transfers between devices with their start and end apart: 5, of which 3 were waited for; matrix products, arithmetic and copies ran while one was open for 0% of the time, Pallas kernels for 38%

profile of v6, /device:TPU:0, one launch (start us, length us, event | category | flops | bytes accessed | tf_op | source)
XLA Modules:
  0.0 24.0 jit_solution(2533503128323014830)
XLA Ops:
  0.0 1.2 %shard_map.91 = (f32[80,128]{1,0:T(8,128)S(1)}, f32[16,128]{1,0:T(8,128)S(1)}, f32[3,2048]{1,0:T(4,128)S(1)}, f32[6,2048]{1,0:T(8,128)S(1)}, s32[40,128]{1,0:T(8...) custom-call(f32[16,128]{1,0:T(8,128)} %bitcast.7, ...), custom_call_target="tpu_custom_call" | custom-call | bytes 262144 | tf_op jit(solution)/shard_map/pallas_call | solution.py:444
  1.2 3.0 %collective-permute-start = (f32[80,128]{1,0:T(8,128)S(1)}, f32[80,128]{1,0:T(8,128)S(1)}, u32[]{:S(2)}, u32[]{:S(2)}) collective-permute-start(f32[80,128]{1,0:T(8,128)S(1)} %get-tuple-element.62), channel_id=1, source_target_pairs={{0,16},{1,17},{2,18},{3,19},{4,20},{5,21},{6,22},{7,23},{8,24},{9,... | collective-permute-start | bytes 122888 | tf_op jit(solution)/shard_map/ppermute | solution.py:470
  4.2 1.9 %shard_map.92 = (f32[160,128]{1,0:T(8,128)S(1)}, s32[80,128]{1,0:T(8,128)S(1)}, f32[80,128]{1,0:T(8,128)S(1)}, bf16[64,512]{1,0:T(8,128)(2,1)S(1)}, bf16[96,512]...) custom-call(f32[16,128]{1,0:T(8,128)S(1)} %get-tuple-element.48.mass, ...), custom_call_target="tpu_custom_call" | custom-call | flops 1593835520 | bytes 262144 | tf_op jit(solution)/shard_map/pallas_call | solution.py:444
  6.1 0.1 collective-permute-done.table.refs_1_.refs_2_
  6.2 0.1 shard_map.93
  6.4 0.1 collective-permute-start.1
  6.4 1.2 %shard_map.94 = (f32[3,512]{1,0:T(4,128)S(1)}, f32[80,128]{1,0:T(8,128)S(1)}, f32[60,128]{1,0:T(8,128)S(1)}) custom-call(bf16[64,512]{1,0:T(8,128)(2,1)S(1)} %get-tuple-element.57.at_q.refs_0_, bf16[96,512]{1,0:T(8,128)(2,1)S(1)} %get-tuple-element.58.at_s.refs_1_, f32[8,512]{1,0:T(8,128)S(1)} %get-tuple-element.59.shifted.refs_2_, ...), custom_call_target="tpu_custom_call" | custom-call | flops 838860800 | bytes 262144 | tf_op jit(solution)/shard_map/pallas_call | solution.py:444
  7.6 0.0 collective-permute-done.1.table.refs_3_
  7.6 0.1 shard_map.95
  7.8 3.2 %collective-permute-start.2 = (f32[80,128]{1,0:T(8,128)S(1)}, f32[80,128]{1,0:T(8,128)S(1)}, u32[]{:S(2)}, u32[]{:S(2)}) collective-permute-start(f32[80,128]{1,0:T(8,128)S(1)} %shard_map.95), channel_id=1, source_target_pairs={{0,4},{1,5},{2,6},{3,7},{4,0},{5,1},{6,2},{7,3},{8,12},{9,13},{10,... | collective-permute-start | bytes 122888 | tf_op jit(solution)/shard_map/ppermute | solution.py:470
  11.0 2.0 %shard_map.96 = (f32[3,512]{1,0:T(4,128)S(1)}, f32[80,128]{1,0:T(8,128)S(1)}, f32[60,128]{1,0:T(8,128)S(1)}) custom-call(bf16[64,512]{1,0:T(8,128)(2,1)S(1)} %get-tuple-element.57.at_q.refs_0_, bf16[96,512]{1,0:T(8,128)(2,1)S(1)} %get-tuple-element.58.at_s.refs_1_, f32[8,512]{1,0:T(8,128)S(1)} %get-tuple-element.59.shifted.refs_2_, ...), custom_call_target="tpu_custom_call" | custom-call | flops 2097152000 | bytes 262144 | tf_op jit(solution)/shard_map/pallas_call | solution.py:444
  13.0 0.2 collective-permute-done.2.table.refs_4_
  13.2 0.1 shard_map.97
  13.4 1.7 %collective-permute-start.3 = (f32[80,128]{1,0:T(8,128)S(1)}, f32[80,128]{1,0:T(8,128)S(1)}, u32[]{:S(2)}, u32[]{:S(2)}) collective-permute-start(f32[80,128]{1,0:T(8,128)S(1)} %shard_map.97), channel_id=1, source_target_pairs={{0,2},{1,3},{2,0},{3,1},{4,6},{5,7},{6,4},{7,5},{8,10},{9,11},{10,... | collective-permute-start | bytes 122888 | tf_op jit(solution)/shard_map/ppermute | solution.py:470
  15.1 1.8 %shard_map.98 = (f32[3,512]{1,0:T(4,128)S(1)}, f32[80,128]{1,0:T(8,128)S(1)}, f32[60,128]{1,0:T(8,128)S(1)}) custom-call(bf16[64,512]{1,0:T(8,128)(2,1)S(1)} %get-tuple-element.57.at_q.refs_0_, bf16[96,512]{1,0:T(8,128)(2,1)S(1)} %get-tuple-element.58.at_s.refs_1_, f32[8,512]{1,0:T(8,128)S(1)} %get-tuple-element.59.shifted.refs_2_, ...), custom_call_target="tpu_custom_call" | custom-call | flops 1677721600 | bytes 262144 | tf_op jit(solution)/shard_map/pallas_call | solution.py:444
  16.8 0.6 %collective-permute-done.3.table.refs_1_ = f32[80,128]{1,0:T(8,128)S(1)} collective-permute-done((f32[80,128]{1,0:T(8,128)S(1)}, f32[80,128]{1,0:T(8,128)S(1)}, u32[]{:S(2)}, u32[]{:S(2)}) %collective-permute-start.3) | collective-permute-done | bytes 40992 | tf_op jit(solution)/shard_map/ppermute | solution.py:470
  17.4 0.1 shard_map.99
  17.6 1.7 %collective-permute-start.4 = (f32[76,128]{1,0:T(8,128)S(1)}, f32[76,128]{1,0:T(8,128)S(1)}, u32[]{:S(2)}, u32[]{:S(2)}) collective-permute-start(f32[76,128]{1,0:T(8,128)S(1)} %shard_map.99), channel_id=1, source_target_pairs={{0,1},{1,0},{2,3},{3,2},{4,5},{5,4},{6,7},{7,6},{8,9},{9,8},{10,11... | collective-permute-start | bytes 116744 | tf_op jit(solution)/shard_map/ppermute | solution.py:470
  19.3 2.4 %shard_map.100.refs_9_ = f32[3,512]{1,0:T(4,128)S(1)} custom-call(bf16[64,512]{1,0:T(8,128)(2,1)S(1)} %get-tuple-element.57.at_q.refs_0_, bf16[96,512]{1,0:T(8,128)(2,1)S(1)} %get-tuple-element.58.at_s.refs_1_, f32[8,512]{1,0:T(8,128)S(1)} %get-tuple-element.59.shifted.refs_2_, f32[8,128]{1,0:T(8,128)S(1)} %get-tuple-element.60.mid.refs_3_, ...), custom_call_target="tpu_custom_call" | custom-call | flops 2516582400 | bytes 262144 | tf_op jit(solution)/shard_map/pallas_call | solution.py:444
  21.6 0.0 collective-permute-done.4.refs_4_
  21.6 2.3 %shard_map.101 = f32[3,512]{1,0:T(4,128)} custom-call(bf16[64,512]{1,0:T(8,128)(2,1)S(1)} %get-tuple-element.57.at_q.refs_0_, bf16[96,512]{1,0:T(8,128)(2,1)S(1)} %get-tuple-element.58.at_s.refs_1_, f32[8,512]{1,0:T(8,128)S(1)} %get-tuple-element.59.shifted.refs_2_, f32[8,128]{1,0:T(8,128)S(1)} %get-tuple-element.60.mid.refs_3_, ...), custom_call_target="tpu_custom_call" | custom-call | flops 1258291200 | bytes 262144 | tf_op jit(solution)/shard_map/pallas_call | solution.py:444
Async XLA Ops:
  1.2 5.0 %collective-permute-start = (f32[80,128]{1,0:T(8,128)S(1)}, f32[80,128]{1,0:T(8,128)S(1)}, u32[]{:S(2)}, u32[]{:S(2)}) collective-permute-start(f32[80,128]{1,0:T(8,128)S(1)} %get-tuple-element.62), channel_id=1, source_target_pairs={{0,16},{1,17},{2,18},{3,19},{4,20},{5,21},{6,22},{7,23},{8,24},{9,... | collective-permute-start | bytes 122888 | tf_op jit(solution)/shard_map/ppermute | solution.py:470
  6.4 1.3 %collective-permute-start.1 = (f32[80,128]{1,0:T(8,128)S(1)}, f32[80,128]{1,0:T(8,128)S(1)}, u32[]{:S(2)}, u32[]{:S(2)}) collective-permute-start(f32[80,128]{1,0:T(8,128)S(1)} %shard_map.93), channel_id=1, source_target_pairs={{0,8},{1,9},{2,10},{3,11},{4,12},{5,13},{6,14},{7,15},{8,0},{9,1},... | collective-permute-start | bytes 122888 | tf_op jit(solution)/shard_map/ppermute | solution.py:470
  7.8 5.4 %collective-permute-start.2 = (f32[80,128]{1,0:T(8,128)S(1)}, f32[80,128]{1,0:T(8,128)S(1)}, u32[]{:S(2)}, u32[]{:S(2)}) collective-permute-start(f32[80,128]{1,0:T(8,128)S(1)} %shard_map.95), channel_id=1, source_target_pairs={{0,4},{1,5},{2,6},{3,7},{4,0},{5,1},{6,2},{7,3},{8,12},{9,13},{10,... | collective-permute-start | bytes 122888 | tf_op jit(solution)/shard_map/ppermute | solution.py:470
  13.4 4.1 %collective-permute-start.3 = (f32[80,128]{1,0:T(8,128)S(1)}, f32[80,128]{1,0:T(8,128)S(1)}, u32[]{:S(2)}, u32[]{:S(2)}) collective-permute-start(f32[80,128]{1,0:T(8,128)S(1)} %shard_map.97), channel_id=1, source_target_pairs={{0,2},{1,3},{2,0},{3,1},{4,6},{5,7},{6,4},{7,5},{8,10},{9,11},{10,... | collective-permute-start | bytes 122888 | tf_op jit(solution)/shard_map/ppermute | solution.py:470
  17.6 4.1 %collective-permute-start.4 = (f32[76,128]{1,0:T(8,128)S(1)}, f32[76,128]{1,0:T(8,128)S(1)}, u32[]{:S(2)}, u32[]{:S(2)}) collective-permute-start(f32[76,128]{1,0:T(8,128)S(1)} %shard_map.99), channel_id=1, source_target_pairs={{0,1},{1,0},{2,3},{3,2},{4,5},{5,4},{6,7},{7,6},{8,9},{9,8},{10,11... | collective-permute-start | bytes 116744 | tf_op jit(solution)/shard_map/ppermute | solution.py:470

commit v7 on v6

--- a/solution.py
+++ b/solution.py
@@ -127,7 +127,7 @@
     targets = at_q.shape[1]
     wide = math.gcd(targets, UNIT)
     units = []
-    for count, is_cell in ((cells, True), (bodies, False)):
+    for count, is_cell in ((bodies, False), (cells, True)):
         deep = math.gcd(count, UNIT) if count else 1
         for b in range(count // deep):
             for t in range(targets // wide):
@@ -383,9 +383,9 @@
     return row, place[(2 * level + 1) * SUBS : (2 * level + 2) * SUBS, :]
 
 
-def window_kernel(spans, ahead, dense, inside, count, bodies, at_q, at_s, shifted, mid, place, *refs):
-    tables, sides = list(refs[:count]), refs[count : count + bodies]
-    refs = list(refs[count + bodies :])
+def window_kernel(spans, ahead, dense, inside, count, parts, at_q, at_s, shifted, mid, place, *refs):
+    tables, sums = list(refs[:count]), refs[count : count + parts]
+    refs = list(refs[count + parts :])
     out = refs.pop(0)
     for level, ids in ahead:
         row, lane = placed(place, level)
@@ -395,19 +395,13 @@
         packed_table(tables[dense], to, to.shape[0] // 10)
     au, aw = refs.pop(), refs.pop()
     room = refs.pop() if inside is not None else None
-    feat, lhs, fw, fu = refs[:4]
-    blhs, bfw = refs[4:6] if bodies else (None, None)
-    near = 0
-    for side in sides:
-        mass, center, blocks = read_bodies(side, mid)
-        body_features(mass, center, blocks, feat, blhs, bfw, near)
-        near += blocks * LANES
+    feat, lhs, fw, fu = refs
     if inside is not None:
         packed_table(tables[inside], room, room.shape[0] // 10)
         tables[inside] = room
     base = span_features([(tables[k], first, many) for k, first, many in spans], mid, feat, lhs, fw, fu)
-    pair_sums(base, near, at_q, at_s, lhs, fw, fu, blhs, bfw, aw, au)
-    store_sums(out, shifted, aw, au)
+    pair_sums(base, 0, at_q, at_s, lhs, fw, fu, None, None, aw, au)
+    store_sums(out, shifted, aw, au, sums)
 
 
 def pick_kernel(level, base, live, faces, place, part, table, *refs):
@@ -513,7 +507,7 @@
     )
     common = [at_q, at_s, shifted, mid]
 
-    def window(spans, ahead=(), dense=None, inside=None, bodies=(), cost=1):
+    def window(spans, ahead=(), dense=None, inside=None, parts=()):
         tables = []
         for table in [span[0] for span in spans] + [t for item in ahead for t in item[1]] + [dense]:
             if table is not None and not any(table is known for known in tables):
@@ -530,15 +524,15 @@
             at(dense),
             at(inside),
             len(tables),
-            len(bodies),
+            len(parts),
         )
         outs = [shaped(3, targets)] + [shaped(10 * wide, LANES)] * len(ahead)
         outs += [shaped(10 * live, LANES)] if dense is not None else []
-        scratch = sum_scratch(targets, count, targets * len(bodies))
+        scratch = sum_scratch(targets, count, 0)
         if inside is not None:
             scratch.insert(-2, pltpu.VMEM((10 * live, LANES), f32))
-        flops = int(cost * targets * (count * 50 + len(bodies) * targets * 20))
-        return call(kernel, outs, common + [place] + tables + list(bodies), scratch, flops=flops)
+        args = common + [place] + tables + list(parts)
+        return call(kernel, outs, args, scratch, flops=targets * count * 50)
 
     sides = []
     if not merged:
@@ -581,8 +575,9 @@
         else:
             spans = [(dense[2], 0, live), (newest, 0, live)]
         ahead = [] if last else [(level + 1, list(tables))]
-        tied = window(spans, ahead, None if last else newest, newest if last else None)
-    sums += tied
+        tied = window(spans, ahead, None if last else newest, newest if last else None, sums if last else ())
+
+    sums = list(tied)
     return call(
         functools.partial(last_kernel, merged, len(sides), len(sums), live),
         shaped(3, targets),

time: 24.2 us -> 24.1 us (level)
  no operation moved by 1% of the time
where the time goes in v7:
time: 24.1 us; the launch traced here: 24 us
  Pallas kernels  13.3 us (55%)
  starting transfers between devices  9.66 us (40%)
  waiting for transfers between devices  0.91 us (4%)
    pallas_call x11, Pallas kernels, call(): pl.pallas_call(kernel, out_shape=out_shape, in_specs=specs, out_specs=[vm...  13.3 us
    ppermute x5, starting transfers between devices, swapped(): lax.ppermute(value, AXES, [(k, k ^ mask) for k in range(lax.axis_size(AXE...  9.66 us
    ppermute x5, waiting for transfers between devices, swapped(): lax.ppermute(value, AXES, [(k, k ^ mask) for k in range(lax.axis_size(AXE...  0.91 us
  transfers between devices with their start and end apart: 5, of which 3 were waited for; matrix products, arithmetic and copies ran while one was open for 0% of the time, Pallas kernels for 38%

profile of v7, /device:TPU:0, one launch (start us, length us, event | category | flops | bytes accessed | tf_op | source)
XLA Modules:
  0.0 24.0 jit_solution(6495119179072671874)
XLA Ops:
  0.0 1.2 %shard_map.91 = (f32[80,128]{1,0:T(8,128)S(1)}, f32[16,128]{1,0:T(8,128)S(1)}, f32[3,2048]{1,0:T(4,128)S(1)}, f32[6,2048]{1,0:T(8,128)S(1)}, s32[40,128]{1,0:T(8...) custom-call(f32[16,128]{1,0:T(8,128)} %bitcast.7, ...), custom_call_target="tpu_custom_call" | custom-call | bytes 262144 | tf_op jit(solution)/shard_map/pallas_call | solution.py:438
  1.2 3.0 %collective-permute-start = (f32[80,128]{1,0:T(8,128)S(1)}, f32[80,128]{1,0:T(8,128)S(1)}, u32[]{:S(2)}, u32[]{:S(2)}) collective-permute-start(f32[80,128]{1,0:T(8,128)S(1)} %get-tuple-element.62), channel_id=1, source_target_pairs={{0,16},{1,17},{2,18},{3,19},{4,20},{5,21},{6,22},{7,23},{8,24},{9,... | collective-permute-start | bytes 122888 | tf_op jit(solution)/shard_map/ppermute | solution.py:464
  4.2 1.9 %shard_map.92 = (f32[160,128]{1,0:T(8,128)S(1)}, s32[80,128]{1,0:T(8,128)S(1)}, f32[80,128]{1,0:T(8,128)S(1)}, bf16[64,512]{1,0:T(8,128)(2,1)S(1)}, bf16[96,512]...) custom-call(f32[16,128]{1,0:T(8,128)S(1)} %get-tuple-element.48.mass, ...), custom_call_target="tpu_custom_call" | custom-call | flops 1593835520 | bytes 262144 | tf_op jit(solution)/shard_map/pallas_call | solution.py:438
  6.1 0.1 collective-permute-done.table.refs_1_.refs_2_
  6.2 0.1 shard_map.93
  6.4 0.1 collective-permute-start.1
  6.4 1.2 %shard_map.94 = (f32[3,512]{1,0:T(4,128)S(1)}, f32[80,128]{1,0:T(8,128)S(1)}, f32[60,128]{1,0:T(8,128)S(1)}) custom-call(bf16[64,512]{1,0:T(8,128)(2,1)S(1)} %get-tuple-element.57.at_q.refs_0_, bf16[96,512]{1,0:T(8,128)(2,1)S(1)} %get-tuple-element.58.at_s.refs_1_, f32[8,512]{1,0:T(8,128)S(1)} %get-tuple-element.59.shifted.refs_2_, ...), custom_call_target="tpu_custom_call" | custom-call | flops 838860800 | bytes 262144 | tf_op jit(solution)/shard_map/pallas_call | solution.py:438
  7.6 0.0 collective-permute-done.1.table.refs_3_
  7.6 0.1 shard_map.95
  7.8 3.2 %collective-permute-start.2 = (f32[80,128]{1,0:T(8,128)S(1)}, f32[80,128]{1,0:T(8,128)S(1)}, u32[]{:S(2)}, u32[]{:S(2)}) collective-permute-start(f32[80,128]{1,0:T(8,128)S(1)} %shard_map.95), channel_id=1, source_target_pairs={{0,4},{1,5},{2,6},{3,7},{4,0},{5,1},{6,2},{7,3},{8,12},{9,13},{10,... | collective-permute-start | bytes 122888 | tf_op jit(solution)/shard_map/ppermute | solution.py:464
  11.0 2.0 %shard_map.96 = (f32[3,512]{1,0:T(4,128)S(1)}, f32[80,128]{1,0:T(8,128)S(1)}, f32[60,128]{1,0:T(8,128)S(1)}) custom-call(bf16[64,512]{1,0:T(8,128)(2,1)S(1)} %get-tuple-element.57.at_q.refs_0_, bf16[96,512]{1,0:T(8,128)(2,1)S(1)} %get-tuple-element.58.at_s.refs_1_, f32[8,512]{1,0:T(8,128)S(1)} %get-tuple-element.59.shifted.refs_2_, ...), custom_call_target="tpu_custom_call" | custom-call | flops 2097152000 | bytes 262144 | tf_op jit(solution)/shard_map/pallas_call | solution.py:438
  13.0 0.2 collective-permute-done.2.table.refs_4_
  13.2 0.1 shard_map.97
  13.4 1.7 %collective-permute-start.3 = (f32[80,128]{1,0:T(8,128)S(1)}, f32[80,128]{1,0:T(8,128)S(1)}, u32[]{:S(2)}, u32[]{:S(2)}) collective-permute-start(f32[80,128]{1,0:T(8,128)S(1)} %shard_map.97), channel_id=1, source_target_pairs={{0,2},{1,3},{2,0},{3,1},{4,6},{5,7},{6,4},{7,5},{8,10},{9,11},{10,... | collective-permute-start | bytes 122888 | tf_op jit(solution)/shard_map/ppermute | solution.py:464
  15.1 1.8 %shard_map.98 = (f32[3,512]{1,0:T(4,128)S(1)}, f32[80,128]{1,0:T(8,128)S(1)}, f32[60,128]{1,0:T(8,128)S(1)}) custom-call(bf16[64,512]{1,0:T(8,128)(2,1)S(1)} %get-tuple-element.57.at_q.refs_0_, bf16[96,512]{1,0:T(8,128)(2,1)S(1)} %get-tuple-element.58.at_s.refs_1_, f32[8,512]{1,0:T(8,128)S(1)} %get-tuple-element.59.shifted.refs_2_, ...), custom_call_target="tpu_custom_call" | custom-call | flops 1677721600 | bytes 262144 | tf_op jit(solution)/shard_map/pallas_call | solution.py:438
  16.8 0.6 %collective-permute-done.3.table.refs_1_ = f32[80,128]{1,0:T(8,128)S(1)} collective-permute-done((f32[80,128]{1,0:T(8,128)S(1)}, f32[80,128]{1,0:T(8,128)S(1)}, u32[]{:S(2)}, u32[]{:S(2)}) %collective-permute-start.3) | collective-permute-done | bytes 40992 | tf_op jit(solution)/shard_map/ppermute | solution.py:464
  17.4 0.1 shard_map.99
  17.6 1.7 %collective-permute-start.4 = (f32[76,128]{1,0:T(8,128)S(1)}, f32[76,128]{1,0:T(8,128)S(1)}, u32[]{:S(2)}, u32[]{:S(2)}) collective-permute-start(f32[76,128]{1,0:T(8,128)S(1)} %shard_map.99), channel_id=1, source_target_pairs={{0,1},{1,0},{2,3},{3,2},{4,5},{5,4},{6,7},{7,6},{8,9},{9,8},{10,11... | collective-permute-start | bytes 116744 | tf_op jit(solution)/shard_map/ppermute | solution.py:464
  19.3 2.4 %shard_map.100.refs_5_ = f32[3,512]{1,0:T(4,128)S(1)} custom-call(bf16[64,512]{1,0:T(8,128)(2,1)S(1)} %get-tuple-element.57.at_q.refs_0_, bf16[96,512]{1,0:T(8,128)(2,1)S(1)} %get-tuple-element.58.at_s.refs_1_, f32[8,512]{1,0:T(8,128)S(1)} %get-tuple-element.59.shifted.refs_2_, f32[8,128]{1,0:T(8,128)S(1)} %get-tuple-element.60.mid.refs_3_, ...), custom_call_target="tpu_custom_call" | custom-call | flops 2516582400 | bytes 262144 | tf_op jit(solution)/shard_map/pallas_call | solution.py:438
  21.6 0.0 collective-permute-done.4.refs_4_
  21.6 2.3 %shard_map.101 = f32[3,512]{1,0:T(4,128)} custom-call(bf16[64,512]{1,0:T(8,128)(2,1)S(1)} %get-tuple-element.57.at_q.refs_0_, bf16[96,512]{1,0:T(8,128)(2,1)S(1)} %get-tuple-element.58.at_s.refs_1_, f32[8,512]{1,0:T(8,128)S(1)} %get-tuple-element.59.shifted.refs_2_, f32[8,128]{1,0:T(8,128)S(1)} %get-tuple-element.60.mid.refs_3_, ...), custom_call_target="tpu_custom_call" | custom-call | flops 1258291200 | bytes 262144 | tf_op jit(solution)/shard_map/pallas_call | solution.py:438
Async XLA Ops:
  1.2 5.0 %collective-permute-start = (f32[80,128]{1,0:T(8,128)S(1)}, f32[80,128]{1,0:T(8,128)S(1)}, u32[]{:S(2)}, u32[]{:S(2)}) collective-permute-start(f32[80,128]{1,0:T(8,128)S(1)} %get-tuple-element.62), channel_id=1, source_target_pairs={{0,16},{1,17},{2,18},{3,19},{4,20},{5,21},{6,22},{7,23},{8,24},{9,... | collective-permute-start | bytes 122888 | tf_op jit(solution)/shard_map/ppermute | solution.py:464
  6.4 1.3 %collective-permute-start.1 = (f32[80,128]{1,0:T(8,128)S(1)}, f32[80,128]{1,0:T(8,128)S(1)}, u32[]{:S(2)}, u32[]{:S(2)}) collective-permute-start(f32[80,128]{1,0:T(8,128)S(1)} %shard_map.93), channel_id=1, source_target_pairs={{0,8},{1,9},{2,10},{3,11},{4,12},{5,13},{6,14},{7,15},{8,0},{9,1},... | collective-permute-start | bytes 122888 | tf_op jit(solution)/shard_map/ppermute | solution.py:464
  7.8 5.4 %collective-permute-start.2 = (f32[80,128]{1,0:T(8,128)S(1)}, f32[80,128]{1,0:T(8,128)S(1)}, u32[]{:S(2)}, u32[]{:S(2)}) collective-permute-start(f32[80,128]{1,0:T(8,128)S(1)} %shard_map.95), channel_id=1, source_target_pairs={{0,4},{1,5},{2,6},{3,7},{4,0},{5,1},{6,2},{7,3},{8,12},{9,13},{10,... | collective-permute-start | bytes 122888 | tf_op jit(solution)/shard_map/ppermute | solution.py:464
  13.4 4.1 %collective-permute-start.3 = (f32[80,128]{1,0:T(8,128)S(1)}, f32[80,128]{1,0:T(8,128)S(1)}, u32[]{:S(2)}, u32[]{:S(2)}) collective-permute-start(f32[80,128]{1,0:T(8,128)S(1)} %shard_map.97), channel_id=1, source_target_pairs={{0,2},{1,3},{2,0},{3,1},{4,6},{5,7},{6,4},{7,5},{8,10},{9,11},{10,... | collective-permute-start | bytes 122888 | tf_op jit(solution)/shard_map/ppermute | solution.py:464
  17.6 4.1 %collective-permute-start.4 = (f32[76,128]{1,0:T(8,128)S(1)}, f32[76,128]{1,0:T(8,128)S(1)}, u32[]{:S(2)}, u32[]{:S(2)}) collective-permute-start(f32[76,128]{1,0:T(8,128)S(1)} %shard_map.99), channel_id=1, source_target_pairs={{0,1},{1,0},{2,3},{3,2},{4,5},{5,4},{6,7},{7,6},{8,9},{9,8},{10,11... | collective-permute-start | bytes 116744 | tf_op jit(solution)/shard_map/ppermute | solution.py:464

commit v8 on v7

--- a/solution.py
+++ b/solution.py
@@ -175,9 +175,13 @@
 
 
 def slot_place(lists, masks, level):
-    at = slice(level * SUBS, (level + 1) * SUBS)
-    index = lists[at, :]
-    return jnp.where(masks[at, :] > 0, index >> 7, -1), index & (LANES - 1)
+    rows, lanes = [], []
+    for r in range(lists.shape[1] // LANES):
+        at = slice(r * LANES, (r + 1) * LANES)
+        index = lists[level : level + 1, at]
+        rows.append(jnp.where(masks[level : level + 1, at] > 0, index >> 7, -1))
+        lanes.append(index & (LANES - 1))
+    return jnp.concatenate(rows, 0), jnp.concatenate(lanes, 0)
 
 
 def picked(row, lane, lines, base, count, out):
@@ -215,14 +219,7 @@
         to[f * count : (f + 1) * count, :] = value[0:count, :]
 
 
-def open_kernel(count, *refs):
-    sources, pick, here, sems = refs[:count], refs[count], refs[count + 1 : -1], refs[-1]
-    moves = [pltpu.make_async_copy(a, b, sems.at[k]) for k, (a, b) in enumerate(zip(sources, here))]
-    for move in moves:
-        move.start()
-    mass, center, quad, lists, masks = here[:5]
-    for move in moves[:5]:
-        move.wait()
+def open_kernel(mass, center, quad, lists, masks, pick):
     row, lane = slot_place(lists, masks, 0)
 
     def line(f, k):
@@ -233,8 +230,6 @@
 
     zeros = [jnp.zeros(row.shape, f32)] * 10
     store_rows(pick, picked(row, lane, line, 0, mass.shape[0], zeros), row.shape[0])
-    for move in moves[5:]:
-        move.wait()
 
 
 def packed(live, value, bits):
@@ -316,13 +311,27 @@
         out[k : k + 1, :] = total[k]
 
 
+def face_blocks(one_side, bod, faces, counts, face):
+    blocks = bod.shape[0] // 4
+    lower = lax.axis_index("gz") > 0
+    for k in range(1 if one_side else 2):
+        order = jnp.where(lower, faces[0:1, :], faces[1:2, :]) if one_side else faces[k : k + 1, :]
+        many = jnp.where(lower, counts[:, 0:1], counts[:, 1:2]) if one_side else counts[:, k : k + 1]
+        for j in range(blocks):
+            take = jnp.where(j < many, order[:, j : j + 1], -1)
+            got = jnp.zeros((4, LANES), f32)
+            for b in range(blocks):
+                got = jnp.where(take == b, bod[pl.ds(b, 4, stride=blocks), :], got)
+            face[pl.ds(k * 4 * blocks + j, 4, stride=blocks), :] = got
+
+
 def start_kernel(
-    one_side, some, mass, center, quad, lists, masks, pos, weight, faces, counts,
-    own, place, part, at_q, at_s, shifted, mid, face, out,
-    tab, bod, feat, lhs, fw, fu, blhs, bfw, aw, au,
+    some, mass, center, quad, lists, masks, pos, weight,
+    own, place, part, at_q, at_s, shifted, mid, bod, out,
+    tab, feat, lhs, fw, fu, blhs, bfw, aw, au,
 ):
     slots = SUBS
-    levels = lists.shape[0] // slots
+    levels = lists.shape[0]
     for level in range(levels):
         row, lane = slot_place(lists, masks, level)
         if level == levels - 1:
@@ -362,16 +371,6 @@
     body_features(own_mass, own_center, blocks, feat, blhs, bfw, 0)
     span_features([(own, 0, some)], mid, feat, lhs, fw, fu)
 
-    lower = lax.axis_index("gz") > 0
-    for k in range(1 if one_side else 2):
-        order = jnp.where(lower, faces[0:1, :], faces[1:2, :]) if one_side else faces[k : k + 1, :]
-        many = jnp.where(lower, counts[:, 0:1], counts[:, 1:2]) if one_side else counts[:, k : k + 1]
-        for j in range(blocks):
-            take = jnp.where(j < many, order[:, j : j + 1], -1)
-            got = jnp.zeros((4, LANES), f32)
-            for b in range(blocks):
-                got = jnp.where(take == b, bod[pl.ds(b, 4, stride=blocks), :], got)
-            face[pl.ds(k * 4 * blocks + j, 4, stride=blocks), :] = got
     row, lane = place[2 * slots : 3 * slots, :], place[3 * slots : 4 * slots, :]
     store_rows(part, picked_tables(row, lane, [own]), slots)
     pair_sums(some * LANES, targets, at_q, at_s, lhs, fw, fu, blhs, bfw, aw, au)
@@ -383,7 +382,15 @@
     return row, place[(2 * level + 1) * SUBS : (2 * level + 2) * SUBS, :]
 
 
-def window_kernel(spans, ahead, dense, inside, count, parts, at_q, at_s, shifted, mid, place, *refs):
+def window_kernel(spans, ahead, dense, inside, count, parts, sided, at_q, at_s, shifted, mid, place, *refs):
+    if sided:
+        bod, far, near, sems = refs[0], refs[1:3], refs[-3:-1], refs[-1]
+        spot = 4 + count + parts + len(ahead) + (dense is not None)
+        face = refs[spot]
+        moves = [pltpu.make_async_copy(a, b, sems.at[k]) for k, (a, b) in enumerate(zip(far, near))]
+        for move in moves:
+            move.start()
+        refs = refs[3:spot] + refs[spot + 1 : -3]
     tables, sums = list(refs[:count]), refs[count : count + parts]
     refs = list(refs[count + parts :])
     out = refs.pop(0)
@@ -402,6 +409,10 @@
     base = span_features([(tables[k], first, many) for k, first, many in spans], mid, feat, lhs, fw, fu)
     pair_sums(base, 0, at_q, at_s, lhs, fw, fu, None, None, aw, au)
     store_sums(out, shifted, aw, au, sums)
+    if sided:
+        for move in moves:
+            move.wait()
+        face_blocks(sided == 1, bod, *near, face)
 
 
 def pick_kernel(level, base, live, faces, place, part, table, *refs):
@@ -475,20 +486,15 @@
     near_by = lax.axis_size("gz")
     merged = near_by == 2 and bits == levels
     given = [cell_mass.reshape(rows, LANES), cell_center, cell_quad]
-    given += [cell_lists.reshape(levels * wide, LANES), slot_masks.reshape(levels * wide, LANES)]
-    given += [body_pos, body_mass.reshape(blocks, LANES), face_lists[0], face_counts]
-    pick, *given = call(
-        functools.partial(open_kernel, len(given)),
-        [shaped(10 * wide, LANES)] + [shaped(*g.shape, dtype=g.dtype) for g in given],
-        [pltpu.with_memory_space_constraint(g, pltpu.HBM) for g in given],
-        [pltpu.SemaphoreType.DMA((len(given),))],
-        [pl.BlockSpec(memory_space=pltpu.HBM)] * len(given),
-    )
+    given += [cell_lists[0], slot_masks[0]]
+    pick = call(open_kernel, shaped(10 * wide, LANES), given)
+    given += [body_pos, body_mass.reshape(blocks, LANES)]
+    notes = [face_lists[0], face_counts]
     arrived = swapped(pick, bits - 1)
 
     some = 3 * rows // 8
-    own, place, part, at_q, at_s, shifted, mid, face, near = call(
-        functools.partial(start_kernel, merged, some),
+    own, place, part, at_q, at_s, shifted, mid, bod, near = call(
+        functools.partial(start_kernel, some),
         [
             shaped(10 * rows, LANES),
             shaped(2 * levels * wide, LANES, dtype=jnp.int32),
@@ -497,17 +503,17 @@
             shaped(QROWS + SROWS, targets, dtype=bf16),
             shaped(SUBS, targets),
             shaped(SUBS, LANES),
-            shaped((1 if merged else 2) * 4 * blocks, LANES),
+            shaped(4 * blocks, LANES),
             shaped(3, targets),
         ],
         given,
-        [pltpu.VMEM((16 * rows, LANES), f32), pltpu.VMEM((4 * blocks, LANES), f32)]
+        [pltpu.VMEM((16 * rows, LANES), f32)]
         + sum_scratch(targets, some * LANES, targets),
         flops=targets * (some * LANES * 50 + targets * 20),
     )
     common = [at_q, at_s, shifted, mid]
 
-    def window(spans, ahead=(), dense=None, inside=None, parts=()):
+    def window(spans, ahead=(), dense=None, inside=None, parts=(), sided=()):
         tables = []
         for table in [span[0] for span in spans] + [t for item in ahead for t in item[1]] + [dense]:
             if table is not None and not any(table is known for known in tables):
@@ -525,22 +531,22 @@
             at(inside),
             len(tables),
             len(parts),
+            (1 if merged else 2) if sided else 0,
         )
         outs = [shaped(3, targets)] + [shaped(10 * wide, LANES)] * len(ahead)
         outs += [shaped(10 * live, LANES)] if dense is not None else []
         scratch = sum_scratch(targets, count, 0)
         if inside is not None:
             scratch.insert(-2, pltpu.VMEM((10 * live, LANES), f32))
-        args = common + [place] + tables + list(parts)
-        return call(kernel, outs, args, scratch, flops=targets * count * 50)
-
-    sides = []
-    if not merged:
-        lower, upper = face[: 4 * blocks], face[4 * blocks :]
-        sides = [
-            lax.ppermute(upper, "gz", [(k, k + 1) for k in range(near_by - 1)]),
-            lax.ppermute(lower, "gz", [(k + 1, k) for k in range(near_by - 1)]),
-        ]
+        args = common + [place] + list(sided) + tables + list(parts)
+        specs = [pl.BlockSpec(memory_space=pltpu.VMEM)] * len(args)
+        if sided:
+            for k in range(len(common) + 2, len(common) + 4):
+                args[k] = pltpu.with_memory_space_constraint(args[k], pltpu.HBM)
+                specs[k] = pl.BlockSpec(memory_space=pltpu.HBM)
+            outs += [shaped((1 if merged else 2) * 4 * blocks, LANES)]
+            scratch += [pltpu.VMEM(n.shape, n.dtype) for n in notes] + [pltpu.SemaphoreType.DMA((2,))]
+        return call(kernel, outs, args, scratch, specs, flops=targets * count * 50)
 
     def cut(start, stop):
         return (own, start * rows // 8, (stop - start) * rows // 8)
@@ -554,8 +560,10 @@
         arrived = tied.pop(0)
         sums.append(tied.pop(0))
         part = tied.pop(0)
+        last = level == levels - 1
+        if last:
+            face = tied.pop()
         dense += tied
-        last = level == levels - 1
         extra = [face] if merged and last else []
         many = live if last else wide
         pick = call(
@@ -574,8 +582,17 @@
             spans = [cut(7, 8), (dense[1], 0, live)]
         else:
             spans = [(dense[2], 0, live), (newest, 0, live)]
+        sided = [bod, *notes] if level == levels - 2 else ()
         ahead = [] if last else [(level + 1, list(tables))]
-        tied = window(spans, ahead, None if last else newest, newest if last else None, sums if last else ())
+        tied = window(spans, ahead, None if last else newest, newest if last else None, sums if last else (), sided)
+
+    sides = []
+    if not merged:
+        lower, upper = face[: 4 * blocks], face[4 * blocks :]
+        sides = [
+            lax.ppermute(upper, "gz", [(k, k + 1) for k in range(near_by - 1)]),
+            lax.ppermute(lower, "gz", [(k + 1, k) for k in range(near_by - 1)]),
+        ]
 
     sums = list(tied)
     return call(

time: 24.1 us -> 24 us (level)
  local copies, waits for them, and re-layouts: 0 us -> 0.85 us
  waiting for transfers between devices: 0.91 us -> 0.4 us
  Pallas kernels: 13.3 us -> 12.8 us
    unnamed x0 -> x11, local copies, waits for them, and re-layouts: none -> 0.85 us
    ppermute x5, waiting for transfers between devices: 0.91 us -> 0.4 us  [swapped(): lax.ppermute(value, AXES, [(k, k ^ mask) for k in range(lax.axis_size(AXE...]
    pallas_call x11, Pallas kernels: 13.3 us -> 12.8 us  [call(): pl.pallas_call(kernel, out_shape=out_shape, in_specs=specs, out_specs=[vm...]
  transfers between devices with their start and end apart: 5 -> 5, of which waited for: 3 -> 3; matrix products, arithmetic and copies ran while one was open for 0% -> 0% of each run, Pallas kernels for 38% -> 41%
where the time goes in v8:
time: 24 us; the launch traced here: 23.9 us
  Pallas kernels  12.8 us (53%)
  starting transfers between devices  9.67 us (40%)
  local copies, waits for them, and re-layouts  0.85 us (4%)
  waiting for transfers between devices  0.4 us (2%)
    pallas_call x11, Pallas kernels, call(): pl.pallas_call(kernel, out_shape=out_shape, in_specs=specs, out_specs=[vm...  12.8 us
    ppermute x5, starting transfers between devices, swapped(): lax.ppermute(value, AXES, [(k, k ^ mask) for k in range(lax.axis_size(AXE...  9.67 us
    unnamed x11, local copies, waits for them, and re-layouts  0.85 us
  transfers between devices with their start and end apart: 5, of which 3 were waited for; matrix products, arithmetic and copies ran while one was open for 0% of the time, Pallas kernels for 41%

profile of v8, /device:TPU:0, one launch (start us, length us, event | category | flops | bytes accessed | tf_op | source)
XLA Modules:
  0.0 23.9 jit_solution(12035932352242865076)
XLA Ops:
  0.0 0.0 copy-start
  0.0 0.0 copy-start.1
  0.0 0.0 copy-start.2
  0.0 0.8 %copy_bitcast_fusion = (s32[5,1024]{1,0:T(8,128)S(1)}, s32[5,1024]{1,0:T(8,128)S(1)}) fusion(s32[1,5,1024]{2,0,1:T(1,128)} %param.15, s32[1,5,1024]{2,0,1:T(1,128)} %param.14), kind=kLoop, calls=%fused_computation | loop fusion | bytes 81920
  0.8 0.0 copy-done
  0.8 0.0 copy-done.1
  0.8 0.0 copy-done.2
  0.8 0.0 copy-start.3
  0.8 0.0 copy-start.4
  0.9 0.2 %shard_map.92 = f32[80,128]{1,0:T(8,128)S(1)} custom-call(f32[16,128]{1,0:T(8,128)S(1)} %bitcast.7, f32[3,2048]{1,0:T(4,128)S(1)} %copy-done.1, f32[6,2048]{1,0:T(8,128)S(1)} %copy-done, s32[5,1024]{1,0:T(8,128)S(1)} %get-tuple-element.76.lists, s32[5,1024]{1,0:T(8,128)S(1)} %get-tuple-element.75.masks), custom_call_target="tpu_custom_call" | custom-call | bytes 262144 | tf_op jit(solution)/shard_map/pallas_call | solution.py:449
  1.1 3.0 %collective-permute-start = (f32[80,128]{1,0:T(8,128)S(1)}, f32[80,128]{1,0:T(8,128)S(1)}, u32[]{:S(2)}, u32[]{:S(2)}) collective-permute-start(f32[80,128]{1,0:T(8,128)S(1)} %shard_map.92), channel_id=1, source_target_pairs={{0,16},{1,17},{2,18},{3,19},{4,20},{5,21},{6,22},{7,23},{8,24},{9,... | collective-permute-start | bytes 122888 | tf_op jit(solution)/shard_map/ppermute | solution.py:475
  4.1 0.0 copy-done.3
  4.1 0.0 copy-done.4
  4.1 1.8 %shard_map.91 = (f32[160,128]{1,0:T(8,128)S(1)}, s32[80,128]{1,0:T(8,128)S(1)}, f32[80,128]{1,0:T(8,128)S(1)}, bf16[64,512]{1,0:T(8,128)(2,1)S(1)}, bf16[96,512]...) custom-call(f32[16,128]{1,0:T(8,128)S(1)} %bitcast.8, ...), custom_call_target="tpu_custom_call" | custom-call | flops 1593835520 | bytes 262144 | tf_op jit(solution)/shard_map/pallas_call | solution.py:449
  6.0 0.1 collective-permute-done.table.refs_1_.refs_2_.refs_5_
  6.1 0.1 shard_map.93
  6.2 0.1 collective-permute-start.1
  6.3 1.2 %shard_map.94 = (f32[3,512]{1,0:T(4,128)S(1)}, f32[80,128]{1,0:T(8,128)S(1)}, f32[60,128]{1,0:T(8,128)S(1)}) custom-call(bf16[64,512]{1,0:T(8,128)(2,1)S(1)} %get-tuple-element.40.at_q.refs_0_, bf16[96,512]{1,0:T(8,128)(2,1)S(1)} %get-tuple-element.41.at_s.refs_1_, f32[8,512]{1,0:T(8,128)S(1)} %get-tuple-element.42.shifted.refs_2_, ...), custom_call_target="tpu_custom_call" | custom-call | flops 838860800 | bytes 262144 | tf_op jit(solution)/shard_map/pallas_call | solution.py:449
  7.5 0.0 collective-permute-done.1.table.refs_3_.refs_6_
  7.5 0.1 shard_map.95
  7.7 3.2 %collective-permute-start.2 = (f32[80,128]{1,0:T(8,128)S(1)}, f32[80,128]{1,0:T(8,128)S(1)}, u32[]{:S(2)}, u32[]{:S(2)}) collective-permute-start(f32[80,128]{1,0:T(8,128)S(1)} %shard_map.95), channel_id=1, source_target_pairs={{0,4},{1,5},{2,6},{3,7},{4,0},{5,1},{6,2},{7,3},{8,12},{9,13},{10,... | collective-permute-start | bytes 122888 | tf_op jit(solution)/shard_map/ppermute | solution.py:475
  10.9 2.0 %shard_map.96 = (f32[3,512]{1,0:T(4,128)S(1)}, f32[80,128]{1,0:T(8,128)S(1)}, f32[60,128]{1,0:T(8,128)S(1)}) custom-call(bf16[64,512]{1,0:T(8,128)(2,1)S(1)} %get-tuple-element.40.at_q.refs_0_, bf16[96,512]{1,0:T(8,128)(2,1)S(1)} %get-tuple-element.41.at_s.refs_1_, f32[8,512]{1,0:T(8,128)S(1)} %get-tuple-element.42.shifted.refs_2_, ...), custom_call_target="tpu_custom_call" | custom-call | flops 2097152000 | bytes 262144 | tf_op jit(solution)/shard_map/pallas_call | solution.py:449
  12.9 0.2 collective-permute-done.2.table.refs_7_
  13.1 0.1 shard_map.97
  13.2 1.7 %collective-permute-start.3 = (f32[80,128]{1,0:T(8,128)S(1)}, f32[80,128]{1,0:T(8,128)S(1)}, u32[]{:S(2)}, u32[]{:S(2)}) collective-permute-start(f32[80,128]{1,0:T(8,128)S(1)} %shard_map.97), channel_id=1, source_target_pairs={{0,2},{1,3},{2,0},{3,1},{4,6},{5,7},{6,4},{7,5},{8,10},{9,11},{10,... | collective-permute-start | bytes 122888 | tf_op jit(solution)/shard_map/ppermute | solution.py:475
  15.0 2.2 %shard_map.98 = (f32[3,512]{1,0:T(4,128)S(1)}, f32[80,128]{1,0:T(8,128)S(1)}, f32[60,128]{1,0:T(8,128)S(1)}, f32[16,128]{1,0:T(8,128)S(1)}) custom-call(bf16[64,512]{1,0:T(8,128)(2,1)S(1)} %get-tuple-element.40.at_q.refs_0_, bf16[96,512]{1,0:T(8,128)(2,1)S(1)} %get-tuple-element.41.at_s.refs_1_, f32[8,512]{1,0:T(8,128)S(1)} %get-tuple-element.42.shifted.refs_2_, ...), custom_call_target="tpu_custom_call" | custom-call | flops 1677721600 | bytes 262144 | tf_op jit(solution)/shard_map/pallas_call | solution.py:449
  17.2 0.1 collective-permute-done.3.table.refs_1_
  17.3 0.1 shard_map.99
  17.5 1.7 %collective-permute-start.4 = (f32[76,128]{1,0:T(8,128)S(1)}, f32[76,128]{1,0:T(8,128)S(1)}, u32[]{:S(2)}, u32[]{:S(2)}) collective-permute-start(f32[76,128]{1,0:T(8,128)S(1)} %shard_map.99), channel_id=1, source_target_pairs={{0,1},{1,0},{2,3},{3,2},{4,5},{5,4},{6,7},{7,6},{8,9},{9,8},{10,11... | collective-permute-start | bytes 116744 | tf_op jit(solution)/shard_map/ppermute | solution.py:475
  19.1 2.4 %shard_map.100.refs_5_ = f32[3,512]{1,0:T(4,128)S(1)} custom-call(bf16[64,512]{1,0:T(8,128)(2,1)S(1)} %get-tuple-element.40.at_q.refs_0_, bf16[96,512]{1,0:T(8,128)(2,1)S(1)} %get-tuple-element.41.at_s.refs_1_, f32[8,512]{1,0:T(8,128)S(1)} %get-tuple-element.42.shifted.refs_2_, f32[8,128]{1,0:T(8,128)S(1)} %get-tuple-element.43.mid.refs_3_, ...), custom_call_target="tpu_custom_call" | custom-call | flops 2516582400 | bytes 262144 | tf_op jit(solution)/shard_map/pallas_call | solution.py:449
  21.5 0.0 collective-permute-done.4.refs_4_
  21.5 2.3 %shard_map.101 = f32[3,512]{1,0:T(4,128)} custom-call(bf16[64,512]{1,0:T(8,128)(2,1)S(1)} %get-tuple-element.40.at_q.refs_0_, bf16[96,512]{1,0:T(8,128)(2,1)S(1)} %get-tuple-element.41.at_s.refs_1_, f32[8,512]{1,0:T(8,128)S(1)} %get-tuple-element.42.shifted.refs_2_, f32[8,128]{1,0:T(8,128)S(1)} %get-tuple-element.43.mid.refs_3_, ...), custom_call_target="tpu_custom_call" | custom-call | flops 1258291200 | bytes 262144 | tf_op jit(solution)/shard_map/pallas_call | solution.py:449
Async XLA Ops:
  0.0 0.8 %copy-start = (f32[6,2048]{1,0:T(8,128)S(1)}, f32[6,2048]{1,0:T(8,128)}, u32[]{:S(2)}) copy-start(f32[6,2048]{1,0:T(8,128)} %quad.3) | copy-start | bytes 147460
  0.0 0.8 %copy-start.1 = (f32[3,2048]{1,0:T(4,128)S(1)}, f32[3,2048]{1,0:T(4,128)}, u32[]{:S(2)}) copy-start(f32[3,2048]{1,0:T(4,128)} %center.3) | copy-start | bytes 73732
  0.0 0.8 %copy-start.2 = (f32[2048]{0:T(1024)S(1)}, f32[2048]{0:T(1024)}, u32[]{:S(2)}) copy-start(f32[2048]{0:T(1024)} %param.11) | copy-start | bytes 24580
  0.8 3.3 %copy-start.3 = (f32[3,512]{1,0:T(4,128)S(1)}, f32[3,512]{1,0:T(4,128)}, u32[]{:S(2)}) copy-start(f32[3,512]{1,0:T(4,128)} %pos.1) | copy-start | bytes 18436
  0.8 3.3 %copy-start.4 = (f32[512]{0:T(512)S(1)}, f32[512]{0:T(512)}, u32[]{:S(2)}) copy-start(f32[512]{0:T(512)} %param.10) | copy-start | bytes 6148
  1.1 5.0 %collective-permute-start = (f32[80,128]{1,0:T(8,128)S(1)}, f32[80,128]{1,0:T(8,128)S(1)}, u32[]{:S(2)}, u32[]{:S(2)}) collective-permute-start(f32[80,128]{1,0:T(8,128)S(1)} %shard_map.92), channel_id=1, source_target_pairs={{0,16},{1,17},{2,18},{3,19},{4,20},{5,21},{6,22},{7,23},{8,24},{9,... | collective-permute-start | bytes 122888 | tf_op jit(solution)/shard_map/ppermute | solution.py:475
  6.2 1.3 %collective-permute-start.1 = (f32[80,128]{1,0:T(8,128)S(1)}, f32[80,128]{1,0:T(8,128)S(1)}, u32[]{:S(2)}, u32[]{:S(2)}) collective-permute-start(f32[80,128]{1,0:T(8,128)S(1)} %shard_map.93), channel_id=1, source_target_pairs={{0,8},{1,9},{2,10},{3,11},{4,12},{5,13},{6,14},{7,15},{8,0},{9,1},... | collective-permute-start | bytes 122888 | tf_op jit(solution)/shard_map/ppermute | solution.py:475
  7.7 5.4 %collective-permute-start.2 = (f32[80,128]{1,0:T(8,128)S(1)}, f32[80,128]{1,0:T(8,128)S(1)}, u32[]{:S(2)}, u32[]{:S(2)}) collective-permute-start(f32[80,128]{1,0:T(8,128)S(1)} %shard_map.95), channel_id=1, source_target_pairs={{0,4},{1,5},{2,6},{3,7},{4,0},{5,1},{6,2},{7,3},{8,12},{9,13},{10,... | collective-permute-start | bytes 122888 | tf_op jit(solution)/shard_map/ppermute | solution.py:475
  13.2 4.1 %collective-permute-start.3 = (f32[80,128]{1,0:T(8,128)S(1)}, f32[80,128]{1,0:T(8,128)S(1)}, u32[]{:S(2)}, u32[]{:S(2)}) collective-permute-start(f32[80,128]{1,0:T(8,128)S(1)} %shard_map.97), channel_id=1, source_target_pairs={{0,2},{1,3},{2,0},{3,1},{4,6},{5,7},{6,4},{7,5},{8,10},{9,11},{10,... | collective-permute-start | bytes 122888 | tf_op jit(solution)/shard_map/ppermute | solution.py:475
  17.5 4.1 %collective-permute-start.4 = (f32[76,128]{1,0:T(8,128)S(1)}, f32[76,128]{1,0:T(8,128)S(1)}, u32[]{:S(2)}, u32[]{:S(2)}) collective-permute-start(f32[76,128]{1,0:T(8,128)S(1)} %shard_map.99), channel_id=1, source_target_pairs={{0,1},{1,0},{2,3},{3,2},{4,5},{5,4},{6,7},{7,6},{8,9},{9,8},{10,11... | collective-permute-start | bytes 116744 | tf_op jit(solution)/shard_map/ppermute | solution.py:475

commit v9 on v8

--- a/solution.py
+++ b/solution.py
@@ -492,7 +492,7 @@
     notes = [face_lists[0], face_counts]
     arrived = swapped(pick, bits - 1)
 
-    some = 3 * rows // 8
+    some = rows // 2
     own, place, part, at_q, at_s, shifted, mid, bod, near = call(
         functools.partial(start_kernel, some),
         [
@@ -575,11 +575,11 @@
         newest = arrived
         arrived = swapped(pick, bits - 1 - level)
         if level == 1:
-            spans = [cut(3, 5)]
+            spans = [cut(4, 6)]
         elif level == 2:
-            spans = [cut(5, 7), (dense[0], 0, live)]
+            spans = [cut(6, 8), (dense[0], 0, live)]
         elif level == 3:
-            spans = [cut(7, 8), (dense[1], 0, live)]
+            spans = [(dense[1], 0, live)]
         else:
             spans = [(dense[2], 0, live), (newest, 0, live)]
         sided = [bod, *notes] if level == levels - 2 else ()

time: 24 us -> 24 us (level)
  Pallas kernels: 12.8 us -> 13.1 us
    pallas_call x11, Pallas kernels: 12.8 us -> 13.1 us  [call(): pl.pallas_call(kernel, out_shape=out_shape, in_specs=specs, out_specs=[vm...]
  transfers between devices with their start and end apart: 5 -> 5, of which waited for: 3 -> 2; matrix products, arithmetic and copies ran while one was open for 0% -> 0% of each run, Pallas kernels for 41% -> 42%
where the time goes in v9:
time: 24 us; the launch traced here: 23.9 us
  Pallas kernels  13.1 us (55%)
  starting transfers between devices  9.53 us (40%)
  local copies, waits for them, and re-layouts  0.85 us (4%)
  waiting for transfers between devices  0.27 us (1%)
    pallas_call x11, Pallas kernels, call(): pl.pallas_call(kernel, out_shape=out_shape, in_specs=specs, out_specs=[vm...  13.1 us
    ppermute x5, starting transfers between devices, swapped(): lax.ppermute(value, AXES, [(k, k ^ mask) for k in range(lax.axis_size(AXE...  9.53 us
    unnamed x11, local copies, waits for them, and re-layouts  0.85 us
  transfers between devices with their start and end apart: 5, of which 2 were waited for; matrix products, arithmetic and copies ran while one was open for 0% of the time, Pallas kernels for 42%

profile of v9, /device:TPU:0, one launch (start us, length us, event | category | flops | bytes accessed | tf_op | source)
XLA Modules:
  0.0 23.9 jit_solution(12393884852554623542)
XLA Ops:
  0.0 0.0 copy-start
  0.0 0.0 copy-start.1
  0.0 0.0 copy-start.2
  0.0 0.8 %copy_bitcast_fusion = (s32[5,1024]{1,0:T(8,128)S(1)}, s32[5,1024]{1,0:T(8,128)S(1)}) fusion(s32[1,5,1024]{2,0,1:T(1,128)} %param.15, s32[1,5,1024]{2,0,1:T(1,128)} %param.14), kind=kLoop, calls=%fused_computation | loop fusion | bytes 81920
  0.8 0.0 copy-done
  0.8 0.0 copy-done.1
  0.8 0.0 copy-done.2
  0.8 0.0 copy-start.3
  0.8 0.0 copy-start.4
  0.9 0.2 %shard_map.92 = f32[80,128]{1,0:T(8,128)S(1)} custom-call(f32[16,128]{1,0:T(8,128)S(1)} %bitcast.7, f32[3,2048]{1,0:T(4,128)S(1)} %copy-done.1, f32[6,2048]{1,0:T(8,128)S(1)} %copy-done, s32[5,1024]{1,0:T(8,128)S(1)} %get-tuple-element.76.lists, s32[5,1024]{1,0:T(8,128)S(1)} %get-tuple-element.75.masks), custom_call_target="tpu_custom_call" | custom-call | bytes 262144 | tf_op jit(solution)/shard_map/pallas_call | solution.py:449
  1.1 3.0 %collective-permute-start = (f32[80,128]{1,0:T(8,128)S(1)}, f32[80,128]{1,0:T(8,128)S(1)}, u32[]{:S(2)}, u32[]{:S(2)}) collective-permute-start(f32[80,128]{1,0:T(8,128)S(1)} %shard_map.92), channel_id=1, source_target_pairs={{0,16},{1,17},{2,18},{3,19},{4,20},{5,21},{6,22},{7,23},{8,24},{9,... | collective-permute-start | bytes 122888 | tf_op jit(solution)/shard_map/ppermute | solution.py:475
  4.1 0.0 copy-done.3
  4.1 0.0 copy-done.4
  4.1 2.1 %shard_map.91 = (f32[160,128]{1,0:T(8,128)S(1)}, s32[80,128]{1,0:T(8,128)S(1)}, f32[80,128]{1,0:T(8,128)S(1)}, bf16[64,512]{1,0:T(8,128)(2,1)S(1)}, bf16[96,512]...) custom-call(f32[16,128]{1,0:T(8,128)S(1)} %bitcast.8, ...), custom_call_target="tpu_custom_call" | custom-call | flops 2013265920 | bytes 262144 | tf_op jit(solution)/shard_map/pallas_call | solution.py:449
  6.2 0.0 collective-permute-done.table.refs_1_.refs_2_.refs_5_
  6.2 0.1 shard_map.93
  6.4 0.1 collective-permute-start.1
  6.5 1.2 %shard_map.94 = (f32[3,512]{1,0:T(4,128)S(1)}, f32[80,128]{1,0:T(8,128)S(1)}, f32[60,128]{1,0:T(8,128)S(1)}) custom-call(bf16[64,512]{1,0:T(8,128)(2,1)S(1)} %get-tuple-element.40.at_q.refs_0_, bf16[96,512]{1,0:T(8,128)(2,1)S(1)} %get-tuple-element.41.at_s.refs_1_, f32[8,512]{1,0:T(8,128)S(1)} %get-tuple-element.42.shifted.refs_2_, ...), custom_call_target="tpu_custom_call" | custom-call | flops 838860800 | bytes 262144 | tf_op jit(solution)/shard_map/pallas_call | solution.py:449
  7.7 0.0 collective-permute-done.1.table.refs_3_.refs_6_
  7.7 0.1 shard_map.95
  7.8 3.0 %collective-permute-start.2 = (f32[80,128]{1,0:T(8,128)S(1)}, f32[80,128]{1,0:T(8,128)S(1)}, u32[]{:S(2)}, u32[]{:S(2)}) collective-permute-start(f32[80,128]{1,0:T(8,128)S(1)} %shard_map.95), channel_id=1, source_target_pairs={{0,4},{1,5},{2,6},{3,7},{4,0},{5,1},{6,2},{7,3},{8,12},{9,13},{10,... | collective-permute-start | bytes 122888 | tf_op jit(solution)/shard_map/ppermute | solution.py:475
  10.9 2.0 %shard_map.96 = (f32[3,512]{1,0:T(4,128)S(1)}, f32[80,128]{1,0:T(8,128)S(1)}, f32[60,128]{1,0:T(8,128)S(1)}) custom-call(bf16[64,512]{1,0:T(8,128)(2,1)S(1)} %get-tuple-element.40.at_q.refs_0_, bf16[96,512]{1,0:T(8,128)(2,1)S(1)} %get-tuple-element.41.at_s.refs_1_, f32[8,512]{1,0:T(8,128)S(1)} %get-tuple-element.42.shifted.refs_2_, ...), custom_call_target="tpu_custom_call" | custom-call | flops 2097152000 | bytes 262144 | tf_op jit(solution)/shard_map/pallas_call | solution.py:449
  12.9 0.2 collective-permute-done.2.table.refs_7_
  13.1 0.1 shard_map.97
  13.2 1.7 %collective-permute-start.3 = (f32[80,128]{1,0:T(8,128)S(1)}, f32[80,128]{1,0:T(8,128)S(1)}, u32[]{:S(2)}, u32[]{:S(2)}) collective-permute-start(f32[80,128]{1,0:T(8,128)S(1)} %shard_map.97), channel_id=1, source_target_pairs={{0,2},{1,3},{2,0},{3,1},{4,6},{5,7},{6,4},{7,5},{8,10},{9,11},{10,... | collective-permute-start | bytes 122888 | tf_op jit(solution)/shard_map/ppermute | solution.py:475
  15.0 2.3 %shard_map.98 = (f32[3,512]{1,0:T(4,128)S(1)}, f32[80,128]{1,0:T(8,128)S(1)}, f32[60,128]{1,0:T(8,128)S(1)}, f32[16,128]{1,0:T(8,128)S(1)}) custom-call(bf16[64,512]{1,0:T(8,128)(2,1)S(1)} %get-tuple-element.40.at_q.refs_0_, bf16[96,512]{1,0:T(8,128)(2,1)S(1)} %get-tuple-element.41.at_s.refs_1_, f32[8,512]{1,0:T(8,128)S(1)} %get-tuple-element.42.shifted.refs_2_, ...), custom_call_target="tpu_custom_call" | custom-call | flops 1258291200 | bytes 262144 | tf_op jit(solution)/shard_map/pallas_call | solution.py:449
  17.3 0.1 collective-permute-done.3.table.refs_1_
  17.3 0.1 shard_map.99
  17.5 1.7 %collective-permute-start.4 = (f32[76,128]{1,0:T(8,128)S(1)}, f32[76,128]{1,0:T(8,128)S(1)}, u32[]{:S(2)}, u32[]{:S(2)}) collective-permute-start(f32[76,128]{1,0:T(8,128)S(1)} %shard_map.99), channel_id=1, source_target_pairs={{0,1},{1,0},{2,3},{3,2},{4,5},{5,4},{6,7},{7,6},{8,9},{9,8},{10,11... | collective-permute-start | bytes 116744 | tf_op jit(solution)/shard_map/ppermute | solution.py:475
  19.1 2.4 %shard_map.100.refs_5_ = f32[3,512]{1,0:T(4,128)S(1)} custom-call(bf16[64,512]{1,0:T(8,128)(2,1)S(1)} %get-tuple-element.40.at_q.refs_0_, bf16[96,512]{1,0:T(8,128)(2,1)S(1)} %get-tuple-element.41.at_s.refs_1_, f32[8,512]{1,0:T(8,128)S(1)} %get-tuple-element.42.shifted.refs_2_, f32[8,128]{1,0:T(8,128)S(1)} %get-tuple-element.43.mid.refs_3_, ...), custom_call_target="tpu_custom_call" | custom-call | flops 2516582400 | bytes 262144 | tf_op jit(solution)/shard_map/pallas_call | solution.py:449
  21.5 0.0 collective-permute-done.4.refs_4_
  21.5 2.3 %shard_map.101 = f32[3,512]{1,0:T(4,128)} custom-call(bf16[64,512]{1,0:T(8,128)(2,1)S(1)} %get-tuple-element.40.at_q.refs_0_, bf16[96,512]{1,0:T(8,128)(2,1)S(1)} %get-tuple-element.41.at_s.refs_1_, f32[8,512]{1,0:T(8,128)S(1)} %get-tuple-element.42.shifted.refs_2_, f32[8,128]{1,0:T(8,128)S(1)} %get-tuple-element.43.mid.refs_3_, ...), custom_call_target="tpu_custom_call" | custom-call | flops 1258291200 | bytes 262144 | tf_op jit(solution)/shard_map/pallas_call | solution.py:449
Async XLA Ops:
  0.0 0.8 %copy-start = (f32[6,2048]{1,0:T(8,128)S(1)}, f32[6,2048]{1,0:T(8,128)}, u32[]{:S(2)}) copy-start(f32[6,2048]{1,0:T(8,128)} %quad.3) | copy-start | bytes 147460
  0.0 0.8 %copy-start.1 = (f32[3,2048]{1,0:T(4,128)S(1)}, f32[3,2048]{1,0:T(4,128)}, u32[]{:S(2)}) copy-start(f32[3,2048]{1,0:T(4,128)} %center.3) | copy-start | bytes 73732
  0.0 0.8 %copy-start.2 = (f32[2048]{0:T(1024)S(1)}, f32[2048]{0:T(1024)}, u32[]{:S(2)}) copy-start(f32[2048]{0:T(1024)} %param.11) | copy-start | bytes 24580
  0.8 3.3 %copy-start.3 = (f32[3,512]{1,0:T(4,128)S(1)}, f32[3,512]{1,0:T(4,128)}, u32[]{:S(2)}) copy-start(f32[3,512]{1,0:T(4,128)} %pos.1) | copy-start | bytes 18436
  0.8 3.3 %copy-start.4 = (f32[512]{0:T(512)S(1)}, f32[512]{0:T(512)}, u32[]{:S(2)}) copy-start(f32[512]{0:T(512)} %param.10) | copy-start | bytes 6148
  1.1 5.1 %collective-permute-start = (f32[80,128]{1,0:T(8,128)S(1)}, f32[80,128]{1,0:T(8,128)S(1)}, u32[]{:S(2)}, u32[]{:S(2)}) collective-permute-start(f32[80,128]{1,0:T(8,128)S(1)} %shard_map.92), channel_id=1, source_target_pairs={{0,16},{1,17},{2,18},{3,19},{4,20},{5,21},{6,22},{7,23},{8,24},{9,... | collective-permute-start | bytes 122888 | tf_op jit(solution)/shard_map/ppermute | solution.py:475
  6.4 1.3 %collective-permute-start.1 = (f32[80,128]{1,0:T(8,128)S(1)}, f32[80,128]{1,0:T(8,128)S(1)}, u32[]{:S(2)}, u32[]{:S(2)}) collective-permute-start(f32[80,128]{1,0:T(8,128)S(1)} %shard_map.93), channel_id=1, source_target_pairs={{0,8},{1,9},{2,10},{3,11},{4,12},{5,13},{6,14},{7,15},{8,0},{9,1},... | collective-permute-start | bytes 122888 | tf_op jit(solution)/shard_map/ppermute | solution.py:475
  7.8 5.3 %collective-permute-start.2 = (f32[80,128]{1,0:T(8,128)S(1)}, f32[80,128]{1,0:T(8,128)S(1)}, u32[]{:S(2)}, u32[]{:S(2)}) collective-permute-start(f32[80,128]{1,0:T(8,128)S(1)} %shard_map.95), channel_id=1, source_target_pairs={{0,4},{1,5},{2,6},{3,7},{4,0},{5,1},{6,2},{7,3},{8,12},{9,13},{10,... | collective-permute-start | bytes 122888 | tf_op jit(solution)/shard_map/ppermute | solution.py:475
  13.2 4.1 %collective-permute-start.3 = (f32[80,128]{1,0:T(8,128)S(1)}, f32[80,128]{1,0:T(8,128)S(1)}, u32[]{:S(2)}, u32[]{:S(2)}) collective-permute-start(f32[80,128]{1,0:T(8,128)S(1)} %shard_map.97), channel_id=1, source_target_pairs={{0,2},{1,3},{2,0},{3,1},{4,6},{5,7},{6,4},{7,5},{8,10},{9,11},{10,... | collective-permute-start | bytes 122888 | tf_op jit(solution)/shard_map/ppermute | solution.py:475
  17.5 4.1 %collective-permute-start.4 = (f32[76,128]{1,0:T(8,128)S(1)}, f32[76,128]{1,0:T(8,128)S(1)}, u32[]{:S(2)}, u32[]{:S(2)}) collective-permute-start(f32[76,128]{1,0:T(8,128)S(1)} %shard_map.99), channel_id=1, source_target_pairs={{0,1},{1,0},{2,3},{3,2},{4,5},{5,4},{6,7},{7,6},{8,9},{9,8},{10,11... | collective-permute-start | bytes 116744 | tf_op jit(solution)/shard_map/ppermute | solution.py:475
